TPU v7x, 128 devices: a whole 4x4x4 slice. The times are simulated.
128 devices in a mesh: shot: 4 (over y_lo, core), dom: 32 (over y_hi, x, z).
Axes of the slice: x: 4, y: 4 (y_hi: 2, y_lo: 2; y = y_hi * 2 + y_lo), z: 4, core: 2. Of those that a mesh axis runs over, the one named last changes fastest.
Arguments:
- wave_prev: float32 [4, 32, 48, 64, 256], P('shot', 'dom'), may hold values from -6 to 6
- wave_now: float32 [4, 32, 48, 64, 256], P('shot', 'dom'), may hold values from -6 to 6
- stiffness: float32 [32, 48, 64, 256], P('dom'), may hold values from 0.04 to 0.12
- buoyancy: float32 [32, 48, 64, 256], P('dom'), may hold values from 0.6 to 1.4
- snapshots: bfloat16 [4, 4, 32, 48, 64, 256], P('shot', None, 'dom'), may hold values from -4 to 4
- traces: float32 [4, 4, 1024], P('shot'), may hold values from -6 to 6
- aperture: int32 [4, 32], P('shot', 'dom'), may hold values from 0 to 1, as said below
- receivers: int32 [4, 1024, 3], P('shot'), may hold values from 0 to 383, as said below
- sources: int32 [4, 3], P('shot'), may hold values from 0 to 383, as said below
Outputs:
- gradient: float32 [32, 48, 64, 256], P('dom')
- wave_last: float32 [4, 32, 48, 64, 256], P('shot', 'dom')
Inputs may be any that keep to these rules, and one draw needn't show every extreme that they name: Each shot's aperture is the tiles whose x position lies in 5 consecutive positions and whose y position lies in 3 consecutive positions. Receiver x indices lie in 0 to 383, y in 0 to 255, z in 0 to 7; receivers may share cells. `sources`: each source lies in the grid, inside its shot's aperture, at a depth under 8.
All inputs are finite; a program needn't handle non-finite values.
Results may differ from a plain program's by a relative error of at most 0.0003.
Values sent between devices are 32-bit elements; how exact they have to be, the bound alone decides.
No kernel may reach another device: no remote copies, remote signals or barrier semaphores. Data moves between devices by JAX's collectives and lax.ppermute only.
A program may use at most 320 MiB of HBM per device.

v0:
```python
import jax
import jax.numpy as jnp
from jax import lax
from jax.sharding import PartitionSpec as P

STEPS = 4
MUTE = 6


second_coef = (-205.0 / 72.0, 8.0 / 5.0, -1.0 / 5.0, 8.0 / 315.0, -1.0 / 560.0)
first_coef = (4.0 / 5.0, -1.0 / 5.0, 4.0 / 105.0, -1.0 / 280.0)


def passed_along(block, axis, distance):
    devices = range(lax.axis_size(axis))
    route = [(i - distance, i) for i in devices if i - distance in devices]
    return lax.ppermute(block, axis, route)


def second_part(extended, axis, length):
    total = jnp.zeros_like(lax.slice_in_dim(extended, 4, 4 + length, axis=axis))
    for step in range(1, 5):
        upper = lax.slice_in_dim(extended, 4 + step, 4 + step + length, axis=axis)
        lower = lax.slice_in_dim(extended, 4 - step, 4 - step + length, axis=axis)
        total = total + second_coef[step] * (upper + lower)
    return total


def first_part(extended, axis, length):
    total = jnp.zeros_like(lax.slice_in_dim(extended, 4, 4 + length, axis=axis))
    for step in range(1, 5):
        upper = lax.slice_in_dim(extended, 4 + step, 4 + step + length, axis=axis)
        lower = lax.slice_in_dim(extended, 4 - step, 4 - step + length, axis=axis)
        total = total + first_coef[step - 1] * (upper - lower)
    return total


def operator(field, x_ext, y_ext, z_ext, buoy, slopes):
    lap = 3.0 * second_coef[0] * field
    lap = (
        lap
        + second_part(x_ext, 0, field.shape[0])
        + second_part(y_ext, 1, field.shape[1])
        + second_part(z_ext, 2, field.shape[2])
    )
    flux = (
        slopes[0] * first_part(x_ext, 0, field.shape[0])
        + slopes[1] * first_part(y_ext, 1, field.shape[1])
        + slopes[2] * first_part(z_ext, 2, field.shape[2])
    )
    return buoy * lap + flux


def extend(field, tile_y):
    lower_x = passed_along(field[-4:], "dom", 4)
    upper_x = passed_along(field[:4], "dom", -4)
    lower_y = passed_along(field[:, -4:], "dom", 1)
    upper_y = passed_along(field[:, :4], "dom", -1)
    lower_y = jnp.where(tile_y == 0, jnp.zeros_like(lower_y), lower_y)
    upper_y = jnp.where(tile_y == 3, jnp.zeros_like(upper_y), upper_y)
    x_ext = jnp.concatenate([lower_x, field, upper_x], axis=0)
    y_ext = jnp.concatenate([lower_y, field, upper_y], axis=1)
    z_ext = jnp.pad(field, ((0, 0), (0, 0), (4, 4)))
    return (x_ext, y_ext, z_ext)


def muted(image, source, grid_x, grid_y, grid_z):
    distance = (grid_x - source[0]) ** 2 + (grid_y - source[1]) ** 2 + (grid_z - source[2]) ** 2
    return jnp.where(distance < MUTE * MUTE, 0.0, 1.0).astype(jnp.float32) * image


def on_device(
    wave_prev, wave_now, stiffness, buoyancy, snapshots, traces, aperture, receivers, sources
):
    index = lax.axis_index("dom")
    tile_x = index // 4
    tile_y = index % 4
    stiff = stiffness[0]
    buoy = buoyancy[0]
    size_x, size_y, size_z = buoy.shape
    grid_x = (tile_x * size_x + jnp.arange(size_x, dtype=jnp.int32))[:, None, None]
    grid_y = (tile_y * size_y + jnp.arange(size_y, dtype=jnp.int32))[None, :, None]
    grid_z = jnp.arange(size_z, dtype=jnp.int32)[None, None, :]
    bx_ext, by_ext, bz_ext = extend(buoy, tile_y)
    slopes = (
        first_part(bx_ext, 0, size_x),
        first_part(by_ext, 1, size_y),
        first_part(bz_ext, 2, size_z),
    )
    previous = wave_prev[0, 0]
    current = wave_now[0, 0]
    open_tile = aperture[0, 0] > 0
    rec = receivers[0]
    local_x = rec[:, 0] - tile_x * size_x
    local_y = rec[:, 1] - tile_y * size_y
    inside = (local_x >= 0) & (local_x < size_x) & (local_y >= 0) & (local_y < size_y)
    clip_x = jnp.clip(local_x, 0, size_x - 1)
    clip_y = jnp.clip(local_y, 0, size_y - 1)
    image = jnp.zeros((size_x, size_y, size_z), jnp.float32)
    for step in range(STEPS):
        x_ext, y_ext, z_ext = extend(current, tile_y)
        amounts = jnp.where(inside, traces[0, step], 0.0)
        inject = (
            jnp.zeros((size_x, size_y, size_z), jnp.float32)
            .at[clip_x, clip_y, rec[:, 2]]
            .add(amounts)
        )

        def advance(operands):
            x_part, y_part, z_part, now_field, old_field, source_term = operands
            change = operator(now_field, x_part, y_part, z_part, buoy, slopes)
            return 2.0 * now_field - old_field + stiff * change + source_term

        def closed(operands):
            return jnp.zeros_like(operands[3])

        following = lax.cond(
            open_tile, advance, closed, (x_ext, y_ext, z_ext, current, previous, inject)
        )
        image = image + snapshots[0, step, 0].astype(jnp.float32) * following
        previous, current = (current, following)
    total = muted(image, sources[0], grid_x, grid_y, grid_z)
    waves = [current]
    gradient = lax.psum(total, "shot")
    return (gradient[None], jnp.stack(waves)[:, None])


def solution(mesh):
    return jax.shard_map(
        on_device,
        mesh=mesh,
        in_specs=(
            P("shot", "dom", None, None, None),
            P("shot", "dom", None, None, None),
            P("dom", None, None, None),
            P("dom", None, None, None),
            P("shot", None, "dom", None, None, None),
            P("shot", None, None),
            P("shot", "dom"),
            P("shot", None, None),
            P("shot", None),
        ),
        out_specs=(P("dom", None, None, None), P("shot", "dom", None, None, None)),
        check_vma=False,
    )
```

profile of v0, /device:TPU:57, one launch (start us, length us, event | category | flops | bytes accessed | tf_op | source)
XLA Modules:
  0.0 484.0 jit_solution(15524628178703952386)
XLA Ops:
  7.2 1.2 fusion.66
  8.4 3.5 collective-permute-start.7
  12.0 1.9 collective-permute-start.6
  13.9 1.9 slice_bitcast_fusion.1
  15.8 5.0 %collective-permute-start.4 = (f32[4,64,256]{2,1,0:T(8,128)}, f32[4,64,256]{2,1,0:T(8,128)}, u32[]{:S(2)}, u32[]{:S(2)}) collective-permute-start(f32[4,64,256]{2,1,0:T(8,128)} %get-tuple-element.170), channel_id=1, source_target_pairs={{4,0},{5,1},{6,2},{7,3},{8,4},{9,5},{10,6},{11,7},{12,8},{13,9},{1... | collective-permute-start | bytes 786440 | tf_op jit(solution)/shard_map/ppermute | solution.py:17
  20.8 1.9 collective-permute-start.5
  22.8 1.2 fusion.67
  24.0 5.6 %collective-permute-start.3 = (f32[48,4,256]{2,1,0:T(4,128)S(1)}, f32[48,4,256]{2,1,0:T(4,128)S(1)}, u32[]{:S(2)}, u32[]{:S(2)}) collective-permute-start(f32[48,4,256]{2,1,0:T(4,128)S(1)} %get-tuple-element.173), channel_id=1, source_target_pairs={{1,0},{2,1},{3,2},{4,3},{5,4},{6,5},{7,6},{8,7},{9,8},{10,9},{11,1... | collective-permute-start | bytes 589832 | tf_op jit(solution)/shard_map/ppermute | solution.py:17
  29.6 0.7 copy.14
  30.4 1.8 slice_bitcast_fusion.3
  33.1 7.7 %scatter_custom_fusion = f32[786432]{0:T(1024)} fusion(s32[1024]{0:T(1024)S(1)} %broadcast_select_fusion.10, f32[1024]{0:T(1024)S(1)} %get-tuple-element.186, f32[]{:T(128)} %constant.138.clone.1), kind=kCustom, calls=%fused_computation.147 | custom fusion | flops 1024 | bytes 3145732
  40.8 7.8 %scatter_custom_fusion.1 = f32[786432]{0:T(1024)} fusion(s32[1024]{0:T(1024)S(1)} %broadcast_select_fusion.10, f32[1024]{0:T(1024)S(1)} %get-tuple-element.185, f32[]{:T(128)} %constant.138.clone.1), kind=kCustom, calls=%fused_computation.145 | custom fusion | flops 1024 | bytes 3145732
  48.7 7.8 %scatter_custom_fusion.2 = f32[786432]{0:T(1024)} fusion(s32[1024]{0:T(1024)S(1)} %broadcast_select_fusion.10, f32[1024]{0:T(1024)S(1)} %get-tuple-element.184, f32[]{:T(128)} %constant.138.clone.1), kind=kCustom, calls=%fused_computation.143 | custom fusion | flops 1024 | bytes 3145732
  56.4 7.7 %scatter_custom_fusion.3 = f32[786432]{0:T(1024)} fusion(s32[1024]{0:T(1024)S(1)} %broadcast_select_fusion.10, f32[1024]{0:T(1024)S(1)} %get-tuple-element.183, f32[]{:T(128)} %constant.138.clone.1), kind=kCustom, calls=%fused_computation.141 | custom fusion | flops 1024 | bytes 3145732
  67.5 1.9 collective-permute-start.2
  69.4 0.7 broadcast_select_fusion.7
  70.1 1.9 collective-permute-start
  72.1 7.2 %collective-permute-start.1 = (f32[4,64,256]{2,1,0:T(8,128)}, f32[4,64,256]{2,1,0:T(8,128)S(1)}, u32[]{:S(2)}, u32[]{:S(2)}) collective-permute-start(f32[4,64,256]{2,1,0:T(8,128)} %get-tuple-element.175), channel_id=1, source_target_pairs={{4,0},{5,1},{6,2},{7,3},{8,4},{9,5},{10,6},{11,7},{12,8},{13,9},{1... | collective-permute-start | bytes 786440 | tf_op jit(solution)/shard_map/ppermute | solution.py:17
  79.2 0.7 broadcast_select_fusion.6
  80.0 2.4 pad_maximum_fusion.4
  82.9 2.0 pad_maximum_fusion
  84.9 48.6 %fusion.36 = (f32[48,64,256]{2,1,0:T(8,128)}, f32[48,64,256]{2,1,0:T(8,128)}, f32[48,64,256]{2,1,0:T(8,128)}) fusion(f32[48,64,256]{2,1,0:T(8,128)} %bitcast.44, f32[48,4,256]{2,1,0:T(4,128)} %broadcast_select_fusion.6, f32[48,4,256]{2,1,0:T(4,128)} %broadcast_select_fusion.7, f32[4,64,256]{2,1,0:T(8,128)} %collective-permute-done.5, ...), kind=kLoop, calls=%fused_computation.116 | loop fusion | flops 38535168 | bytes 13500416 | tf_op jit(solution)/shard_map/add | solution.py:34
  133.5 38.3 %conditional.4 = (f32[48,64,256]{2,1,0:T(8,128)}) conditional(s32[]{:T(128)} %bitcast.5, () %tuple.32, (f32[48,64,256]{2,1,0:T(8,128)}, f32[1,1,48,64,256]{4,3,2,1,0:T(8,128)}, f32[56,64,256]{2,1,0:T(8,128)}, f32[48,72,256]{2,1,0:T(8,128)S(1)}, f32[48,64,256]{2,1,0:T(8,128)}, /*index=5*/f32[48,64,256]{2,1,0:T(8,128)}, f32[48,64,256]{2,1,0:T(8,128)}, ...), branch_computations={%region_1.2_spmd, %region_2.3_spmd} | conditional | flops 64487424 | bytes 84934664 | solution.py:117
  133.5 4.8 %reshape.141 = f32[48,64,256]{2,1,0:T(8,128)} reshape(f32[786432]{0:T(1024)} %get-tuple-element.149) | data formatting | bytes 6291456 | tf_op jit(solution)/shard_map/scatter-add | solution.py:106
  138.4 33.4 %fusion.1 = f32[48,64,256]{2,1,0:T(8,128)} fusion(f32[48,64,256]{2,1,0:T(8,128)} %reshape.141, f32[1,1,48,64,256]{4,3,2,1,0:T(8,128)} %get-tuple-element.148, f32[48,64,256]{2,1,0:T(8,128)} %get-tuple-element.107, f32[48,64,256]{2,1,0:T(8,128)} %get-tuple-element.113, f32[48,64,256]{2,1,0:T(8,128)} %get-tuple-element.112, ...), kind=kLoop, calls=%fused_computation.14 | loop fusion | flops 64487424 | bytes 78643200 | tf_op jit(solution)/shard_map/cond/branch_1_fun/add | solution.py:112
  171.8 1.2 fusion.64
  173.0 1.9 collective-permute-start.11
  174.9 3.4 collective-permute-start.10
  178.3 1.1 fusion.65
  179.4 1.9 collective-permute-start.8
  181.3 7.2 %collective-permute-start.9 = (f32[4,64,256]{2,1,0:T(8,128)S(1)}, f32[4,64,256]{2,1,0:T(8,128)S(1)}, u32[]{:S(2)}, u32[]{:S(2)}) collective-permute-start(f32[4,64,256]{2,1,0:T(8,128)S(1)} %get-tuple-element.164), channel_id=1, source_target_pairs={{4,0},{5,1},{6,2},{7,3},{8,4},{9,5},{10,6},{11,7},{12,8},{13,9},{1... | collective-permute-start | bytes 786440 | tf_op jit(solution)/shard_map/ppermute | solution.py:17
  188.5 4.8 collective-permute-done.10
  193.4 2.2 pad_maximum_fusion.5
  195.6 4.1 pad_maximum_fusion.1
  199.7 39.0 %conditional.5 = (f32[48,64,256]{2,1,0:T(8,128)}) conditional(s32[]{:T(128)} %bitcast.5, () %tuple.34, (f32[48,64,256]{2,1,0:T(8,128)}, f32[48,64,256]{2,1,0:T(8,128)}, f32[56,64,256]{2,1,0:T(8,128)}, f32[48,72,256]{2,1,0:T(8,128)S(1)}, f32[48,64,256]{2,1,0:T(8,128)}, /*index=5*/f32[48,64,256]{2,1,0:T(8,128)}, f32[48,64,256]{2,1,0:T(8,128)}, ...), branch_computations={%region_4.5_spmd, %region_5.6_spmd} | conditional | flops 64487424 | bytes 84934664 | solution.py:117
  199.7 4.8 reshape.142
  204.5 34.2 %add_add_fusion = f32[48,64,256]{2,1,0:T(8,128)} fusion(f32[48,64,256]{2,1,0:T(8,128)} %reshape.142, f32[48,64,256]{2,1,0:T(8,128)} %get-tuple-element.117, f32[48,64,256]{2,1,0:T(8,128)} %get-tuple-element.123, f32[48,64,256]{2,1,0:T(8,128)} %get-tuple-element.122, f32[48,64,256]{2,1,0:T(8,128)} %get-tuple-element.121, ...), kind=kLoop, calls=%fused_computation.23 | loop fusion | flops 64487424 | bytes 78643200 | tf_op jit(solution)/shard_map/cond/branch_1_fun/add | solution.py:112
  238.7 1.2 fusion.62
  239.9 1.9 collective-permute-start.15
  241.8 5.1 %collective-permute-start.14 = (f32[48,4,256]{2,1,0:T(4,128)S(1)}, f32[48,4,256]{2,1,0:T(4,128)S(1)}, u32[]{:S(2)}, u32[]{:S(2)}) collective-permute-start(f32[48,4,256]{2,1,0:T(4,128)S(1)} %get-tuple-element.157), channel_id=1, source_target_pairs={{0,1},{1,2},{2,3},{3,4},{4,5},{5,6},{6,7},{7,8},{8,9},{9,10},{10,1... | collective-permute-start | bytes 589832 | tf_op jit(solution)/shard_map/ppermute | solution.py:17
  246.9 1.1 fusion.63
  248.0 1.9 collective-permute-start.12
  249.9 7.4 %collective-permute-start.13 = (f32[4,64,256]{2,1,0:T(8,128)S(1)}, f32[4,64,256]{2,1,0:T(8,128)S(1)}, u32[]{:S(2)}, u32[]{:S(2)}) collective-permute-start(f32[4,64,256]{2,1,0:T(8,128)S(1)} %get-tuple-element.160), channel_id=1, source_target_pairs={{4,0},{5,1},{6,2},{7,3},{8,4},{9,5},{10,6},{11,7},{12,8},{13,9},{1... | collective-permute-start | bytes 786440 | tf_op jit(solution)/shard_map/ppermute | solution.py:17
  257.4 4.5 collective-permute-done.14
  262.0 2.2 pad_maximum_fusion.6
  264.2 4.1 pad_maximum_fusion.2
  268.3 38.5 %conditional.6 = (f32[48,64,256]{2,1,0:T(8,128)}) conditional(s32[]{:T(128)} %bitcast.5, () %tuple.36, (f32[48,64,256]{2,1,0:T(8,128)}, f32[48,64,256]{2,1,0:T(8,128)}, f32[56,64,256]{2,1,0:T(8,128)}, f32[48,72,256]{2,1,0:T(8,128)S(1)}, f32[48,64,256]{2,1,0:T(8,128)}, /*index=5*/f32[48,64,256]{2,1,0:T(8,128)}, f32[48,64,256]{2,1,0:T(8,128)}, ...), branch_computations={%region_7.8_spmd, %region_8.9_spmd} | conditional | flops 64487424 | bytes 84934664 | solution.py:117
  268.3 4.8 reshape.143
  273.1 33.7 %add_add_fusion.1 = f32[48,64,256]{2,1,0:T(8,128)} fusion(f32[48,64,256]{2,1,0:T(8,128)} %reshape.143, f32[48,64,256]{2,1,0:T(8,128)} %get-tuple-element.127, f32[48,64,256]{2,1,0:T(8,128)} %get-tuple-element.133, f32[48,64,256]{2,1,0:T(8,128)} %get-tuple-element.132, f32[48,64,256]{2,1,0:T(8,128)} %get-tuple-element.131, ...), kind=kLoop, calls=%fused_computation.32 | loop fusion | flops 64487424 | bytes 78643200 | tf_op jit(solution)/shard_map/cond/branch_1_fun/add | solution.py:112
  306.8 1.2 fusion.60
  308.0 1.9 collective-permute-start.19
  309.9 5.5 %collective-permute-start.18 = (f32[48,4,256]{2,1,0:T(4,128)S(1)}, f32[48,4,256]{2,1,0:T(4,128)S(1)}, u32[]{:S(2)}, u32[]{:S(2)}) collective-permute-start(f32[48,4,256]{2,1,0:T(4,128)S(1)} %get-tuple-element.153), channel_id=1, source_target_pairs={{0,1},{1,2},{2,3},{3,4},{4,5},{5,6},{6,7},{7,8},{8,9},{9,10},{10,1... | collective-permute-start | bytes 589832 | tf_op jit(solution)/shard_map/ppermute | solution.py:17
  315.5 1.1 fusion.61
  316.6 1.9 collective-permute-start.16
  318.5 7.4 %collective-permute-start.17 = (f32[4,64,256]{2,1,0:T(8,128)S(1)}, f32[4,64,256]{2,1,0:T(8,128)S(1)}, u32[]{:S(2)}, u32[]{:S(2)}) collective-permute-start(f32[4,64,256]{2,1,0:T(8,128)S(1)} %get-tuple-element.156), channel_id=1, source_target_pairs={{4,0},{5,1},{6,2},{7,3},{8,4},{9,5},{10,6},{11,7},{12,8},{13,9},{1... | collective-permute-start | bytes 786440 | tf_op jit(solution)/shard_map/ppermute | solution.py:17
  326.0 4.5 collective-permute-done.18
  330.5 2.2 pad_maximum_fusion.7
  332.8 4.1 pad_maximum_fusion.3
  336.9 38.4 %conditional.7 = (f32[48,64,256]{2,1,0:T(8,128)}) conditional(s32[]{:T(128)} %bitcast.5, () %tuple.38, (f32[48,64,256]{2,1,0:T(8,128)}, f32[48,64,256]{2,1,0:T(8,128)}, f32[56,64,256]{2,1,0:T(8,128)}, f32[48,72,256]{2,1,0:T(8,128)S(1)}, f32[48,64,256]{2,1,0:T(8,128)}, /*index=5*/f32[48,64,256]{2,1,0:T(8,128)}, f32[48,64,256]{2,1,0:T(8,128)}, ...), branch_computations={%region_10.11_spmd, %region_11.12_spmd} | conditional | flops 64487424 | bytes 84934664 | solution.py:117
  336.9 4.8 reshape.144
  341.7 33.6 %add_add_fusion.2 = f32[48,64,256]{2,1,0:T(8,128)} fusion(f32[48,64,256]{2,1,0:T(8,128)} %reshape.144, f32[48,64,256]{2,1,0:T(8,128)} %get-tuple-element.137, f32[48,64,256]{2,1,0:T(8,128)} %get-tuple-element.143, f32[48,64,256]{2,1,0:T(8,128)} %get-tuple-element.142, f32[48,64,256]{2,1,0:T(8,128)} %get-tuple-element.141, ...), kind=kLoop, calls=%fused_computation.41 | loop fusion | flops 64487424 | bytes 78643200 | tf_op jit(solution)/shard_map/cond/branch_1_fun/add | solution.py:112
  375.3 8.9 %fusion.49 = f32[1,48,64,256]{3,2,1,0:T(8,128)} fusion(f32[48,64,256]{2,1,0:T(8,128)} %get-tuple-element.195, f32[48,64,256]{2,1,0:T(8,128)} %get-tuple-element.194, f32[48,64,256]{2,1,0:T(8,128)} %get-tuple-element.193, f32[48,64,256]{2,1,0:T(8,128)} %get-tuple-element.192, bf16[1,4,1,48,64,256]{5,4,3,2,1,0:T(8,128)(2,1)} %param.21, ...), kind=kLoop, calls=%fused_computation.134 | loop fusion | flops 11796480 | bytes 22033408 | tf_op jit(solution)/shard_map/broadcast_in_dim | solution.py:125
  384.2 89.1 %all-reduce.7.cloned.1.call-done = f32[1,48,64,256]{3,2,1,0:T(8,128)} async-done(((f32[1,48,64,256]{3,2,1,0:T(8,128)}), f32[1,48,64,256]{3,2,1,0:T(8,128)}) %all-reduce.7.cloned.1.call-update) | async-done | bytes 3145744 | tf_op jit(solution)/shard_map/psum | solution.py:124
  473.3 3.9 copy.25
  (49 shorter events, 4.4 us)
Async XLA Ops:
  7.2 25.0 %copy-start.4 = (s32[3]{0:T(128)S(1)}, s32[3]{0:T(128)}, u32[]{:S(2)}) copy-start(s32[3]{0:T(128)} %constant.167) | copy-start | bytes 40
  7.2 25.1 %copy-start.3 = (s32[3]{0:T(128)S(1)}, s32[3]{0:T(128)}, u32[]{:S(2)}) copy-start(s32[3]{0:T(128)} %constant.170) | copy-start | bytes 40
  7.2 25.2 %copy-start.1 = (f32[1,4,1024]{2,1,0:T(4,128)S(1)}, f32[1,4,1024]{2,1,0:T(4,128)}, u32[]{:S(2)}) copy-start(f32[1,4,1024]{2,1,0:T(4,128)} %param.22) | copy-start | bytes 49156
  7.2 466.1 %all-reduce.7.cloned.1.call-start = ((), (), s32[]{:S(2)}) async-start(), calls=%async_computation | async-start | bytes 6291456 | tf_op jit(solution)/shard_map/psum | solution.py:124
  8.4 63.6 %collective-permute-start.7 = (f32[48,4,256]{2,1,0:T(4,128)S(1)}, f32[48,4,256]{2,1,0:T(4,128)S(1)}, u32[]{:S(2)}, u32[]{:S(2)}) collective-permute-start(f32[48,4,256]{2,1,0:T(4,128)S(1)} %get-tuple-element.169), channel_id=1, source_target_pairs={{0,1},{1,2},{2,3},{3,4},{4,5},{5,6},{6,7},{7,8},{8,9},{9,10},{10,1... | collective-permute-start | bytes 589832 | tf_op jit(solution)/shard_map/ppermute | solution.py:17
  12.0 55.5 %collective-permute-start.6 = (f32[48,4,256]{2,1,0:T(4,128)S(1)}, f32[48,4,256]{2,1,0:T(4,128)S(1)}, u32[]{:S(2)}, u32[]{:S(2)}) collective-permute-start(f32[48,4,256]{2,1,0:T(4,128)S(1)} %get-tuple-element.168), channel_id=1, source_target_pairs={{1,0},{2,1},{3,2},{4,3},{5,4},{6,5},{7,6},{8,7},{9,8},{10,9},{11,1... | collective-permute-start | bytes 589832 | tf_op jit(solution)/shard_map/ppermute | solution.py:17
  15.8 69.1 %collective-permute-start.4 = (f32[4,64,256]{2,1,0:T(8,128)}, f32[4,64,256]{2,1,0:T(8,128)}, u32[]{:S(2)}, u32[]{:S(2)}) collective-permute-start(f32[4,64,256]{2,1,0:T(8,128)} %get-tuple-element.170), channel_id=1, source_target_pairs={{4,0},{5,1},{6,2},{7,3},{8,4},{9,5},{10,6},{11,7},{12,8},{13,9},{1... | collective-permute-start | bytes 786440 | tf_op jit(solution)/shard_map/ppermute | solution.py:17
  20.8 64.0 %collective-permute-start.5 = (f32[4,64,256]{2,1,0:T(8,128)}, f32[4,64,256]{2,1,0:T(8,128)}, u32[]{:S(2)}, u32[]{:S(2)}) collective-permute-start(f32[4,64,256]{2,1,0:T(8,128)} %get-tuple-element.171), channel_id=1, source_target_pairs={{0,4},{1,5},{2,6},{3,7},{4,8},{5,9},{6,10},{7,11},{8,12},{9,13},{1... | collective-permute-start | bytes 786440 | tf_op jit(solution)/shard_map/ppermute | solution.py:17
  24.0 46.1 %collective-permute-start.3 = (f32[48,4,256]{2,1,0:T(4,128)S(1)}, f32[48,4,256]{2,1,0:T(4,128)S(1)}, u32[]{:S(2)}, u32[]{:S(2)}) collective-permute-start(f32[48,4,256]{2,1,0:T(4,128)S(1)} %get-tuple-element.173), channel_id=1, source_target_pairs={{1,0},{2,1},{3,2},{4,3},{5,4},{6,5},{7,6},{8,7},{9,8},{10,9},{11,1... | collective-permute-start | bytes 589832 | tf_op jit(solution)/shard_map/ppermute | solution.py:17
  48.7 15.5 %copy-start.2 = (s32[1,3]{1,0:T(1,128)S(1)}, s32[1,3]{1,0:T(1,128)}, u32[]{:S(2)}) copy-start(s32[1,3]{1,0:T(1,128)} %param.25) | copy-start | bytes 40
  67.5 12.5 %collective-permute-start.2 = (f32[48,4,256]{2,1,0:T(4,128)S(1)}, f32[48,4,256]{2,1,0:T(4,128)S(1)}, u32[]{:S(2)}, u32[]{:S(2)}) collective-permute-start(f32[48,4,256]{2,1,0:T(4,128)S(1)} %get-tuple-element.172), channel_id=1, source_target_pairs={{0,1},{1,2},{2,3},{3,4},{4,5},{5,6},{6,7},{7,8},{8,9},{9,10},{10,1... | collective-permute-start | bytes 589832 | tf_op jit(solution)/shard_map/ppermute | solution.py:17
  70.1 12.3 %collective-permute-start = (f32[4,64,256]{2,1,0:T(8,128)}, f32[4,64,256]{2,1,0:T(8,128)S(1)}, u32[]{:S(2)}, u32[]{:S(2)}) collective-permute-start(f32[4,64,256]{2,1,0:T(8,128)} %get-tuple-element.174), channel_id=1, source_target_pairs={{0,4},{1,5},{2,6},{3,7},{4,8},{5,9},{6,10},{7,11},{8,12},{9,13},{1... | collective-permute-start | bytes 786440 | tf_op jit(solution)/shard_map/ppermute | solution.py:17
  72.1 10.6 %collective-permute-start.1 = (f32[4,64,256]{2,1,0:T(8,128)}, f32[4,64,256]{2,1,0:T(8,128)S(1)}, u32[]{:S(2)}, u32[]{:S(2)}) collective-permute-start(f32[4,64,256]{2,1,0:T(8,128)} %get-tuple-element.175), channel_id=1, source_target_pairs={{4,0},{5,1},{6,2},{7,3},{8,4},{9,5},{10,6},{11,7},{12,8},{13,9},{1... | collective-permute-start | bytes 786440 | tf_op jit(solution)/shard_map/ppermute | solution.py:17
  80.0 2.8 copy-start
  173.0 15.5 %collective-permute-start.11 = (f32[48,4,256]{2,1,0:T(4,128)S(1)}, f32[48,4,256]{2,1,0:T(4,128)S(1)}, u32[]{:S(2)}, u32[]{:S(2)}) collective-permute-start(f32[48,4,256]{2,1,0:T(4,128)S(1)} %get-tuple-element.162), channel_id=1, source_target_pairs={{1,0},{2,1},{3,2},{4,3},{5,4},{6,5},{7,6},{8,7},{9,8},{10,9},{11,1... | collective-permute-start | bytes 589832 | tf_op jit(solution)/shard_map/ppermute | solution.py:17
  174.9 18.4 %collective-permute-start.10 = (f32[48,4,256]{2,1,0:T(4,128)S(1)}, f32[48,4,256]{2,1,0:T(4,128)S(1)}, u32[]{:S(2)}, u32[]{:S(2)}) collective-permute-start(f32[48,4,256]{2,1,0:T(4,128)S(1)} %get-tuple-element.161), channel_id=1, source_target_pairs={{0,1},{1,2},{2,3},{3,4},{4,5},{5,6},{6,7},{7,8},{8,9},{9,10},{10,1... | collective-permute-start | bytes 589832 | tf_op jit(solution)/shard_map/ppermute | solution.py:17
  179.4 16.3 %collective-permute-start.8 = (f32[4,64,256]{2,1,0:T(8,128)S(1)}, f32[4,64,256]{2,1,0:T(8,128)S(1)}, u32[]{:S(2)}, u32[]{:S(2)}) collective-permute-start(f32[4,64,256]{2,1,0:T(8,128)S(1)} %get-tuple-element.163), channel_id=1, source_target_pairs={{0,4},{1,5},{2,6},{3,7},{4,8},{5,9},{6,10},{7,11},{8,12},{9,13},{1... | collective-permute-start | bytes 786440 | tf_op jit(solution)/shard_map/ppermute | solution.py:17
  181.3 14.3 %collective-permute-start.9 = (f32[4,64,256]{2,1,0:T(8,128)S(1)}, f32[4,64,256]{2,1,0:T(8,128)S(1)}, u32[]{:S(2)}, u32[]{:S(2)}) collective-permute-start(f32[4,64,256]{2,1,0:T(8,128)S(1)} %get-tuple-element.164), channel_id=1, source_target_pairs={{4,0},{5,1},{6,2},{7,3},{8,4},{9,5},{10,6},{11,7},{12,8},{13,9},{1... | collective-permute-start | bytes 786440 | tf_op jit(solution)/shard_map/ppermute | solution.py:17
  239.9 17.5 %collective-permute-start.15 = (f32[48,4,256]{2,1,0:T(4,128)S(1)}, f32[48,4,256]{2,1,0:T(4,128)S(1)}, u32[]{:S(2)}, u32[]{:S(2)}) collective-permute-start(f32[48,4,256]{2,1,0:T(4,128)S(1)} %get-tuple-element.158), channel_id=1, source_target_pairs={{1,0},{2,1},{3,2},{4,3},{5,4},{6,5},{7,6},{8,7},{9,8},{10,9},{11,1... | collective-permute-start | bytes 589832 | tf_op jit(solution)/shard_map/ppermute | solution.py:17
  241.8 20.1 %collective-permute-start.14 = (f32[48,4,256]{2,1,0:T(4,128)S(1)}, f32[48,4,256]{2,1,0:T(4,128)S(1)}, u32[]{:S(2)}, u32[]{:S(2)}) collective-permute-start(f32[48,4,256]{2,1,0:T(4,128)S(1)} %get-tuple-element.157), channel_id=1, source_target_pairs={{0,1},{1,2},{2,3},{3,4},{4,5},{5,6},{6,7},{7,8},{8,9},{9,10},{10,1... | collective-permute-start | bytes 589832 | tf_op jit(solution)/shard_map/ppermute | solution.py:17
  248.0 16.2 %collective-permute-start.12 = (f32[4,64,256]{2,1,0:T(8,128)S(1)}, f32[4,64,256]{2,1,0:T(8,128)S(1)}, u32[]{:S(2)}, u32[]{:S(2)}) collective-permute-start(f32[4,64,256]{2,1,0:T(8,128)S(1)} %get-tuple-element.159), channel_id=1, source_target_pairs={{0,4},{1,5},{2,6},{3,7},{4,8},{5,9},{6,10},{7,11},{8,12},{9,13},{1... | collective-permute-start | bytes 786440 | tf_op jit(solution)/shard_map/ppermute | solution.py:17
  249.9 14.3 %collective-permute-start.13 = (f32[4,64,256]{2,1,0:T(8,128)S(1)}, f32[4,64,256]{2,1,0:T(8,128)S(1)}, u32[]{:S(2)}, u32[]{:S(2)}) collective-permute-start(f32[4,64,256]{2,1,0:T(8,128)S(1)} %get-tuple-element.160), channel_id=1, source_target_pairs={{4,0},{5,1},{6,2},{7,3},{8,4},{9,5},{10,6},{11,7},{12,8},{13,9},{1... | collective-permute-start | bytes 786440 | tf_op jit(solution)/shard_map/ppermute | solution.py:17
  308.0 17.9 %collective-permute-start.19 = (f32[48,4,256]{2,1,0:T(4,128)S(1)}, f32[48,4,256]{2,1,0:T(4,128)S(1)}, u32[]{:S(2)}, u32[]{:S(2)}) collective-permute-start(f32[48,4,256]{2,1,0:T(4,128)S(1)} %get-tuple-element.154), channel_id=1, source_target_pairs={{1,0},{2,1},{3,2},{4,3},{5,4},{6,5},{7,6},{8,7},{9,8},{10,9},{11,1... | collective-permute-start | bytes 589832 | tf_op jit(solution)/shard_map/ppermute | solution.py:17
  309.9 20.5 %collective-permute-start.18 = (f32[48,4,256]{2,1,0:T(4,128)S(1)}, f32[48,4,256]{2,1,0:T(4,128)S(1)}, u32[]{:S(2)}, u32[]{:S(2)}) collective-permute-start(f32[48,4,256]{2,1,0:T(4,128)S(1)} %get-tuple-element.153), channel_id=1, source_target_pairs={{0,1},{1,2},{2,3},{3,4},{4,5},{5,6},{6,7},{7,8},{8,9},{9,10},{10,1... | collective-permute-start | bytes 589832 | tf_op jit(solution)/shard_map/ppermute | solution.py:17
  316.6 16.2 %collective-permute-start.16 = (f32[4,64,256]{2,1,0:T(8,128)S(1)}, f32[4,64,256]{2,1,0:T(8,128)S(1)}, u32[]{:S(2)}, u32[]{:S(2)}) collective-permute-start(f32[4,64,256]{2,1,0:T(8,128)S(1)} %get-tuple-element.155), channel_id=1, source_target_pairs={{0,4},{1,5},{2,6},{3,7},{4,8},{5,9},{6,10},{7,11},{8,12},{9,13},{1... | collective-permute-start | bytes 786440 | tf_op jit(solution)/shard_map/ppermute | solution.py:17
  318.5 14.3 %collective-permute-start.17 = (f32[4,64,256]{2,1,0:T(8,128)S(1)}, f32[4,64,256]{2,1,0:T(8,128)S(1)}, u32[]{:S(2)}, u32[]{:S(2)}) collective-permute-start(f32[4,64,256]{2,1,0:T(8,128)S(1)} %get-tuple-element.156), channel_id=1, source_target_pairs={{4,0},{5,1},{6,2},{7,3},{8,4},{9,5},{10,6},{11,7},{12,8},{13,9},{1... | collective-permute-start | bytes 786440 | tf_op jit(solution)/shard_map/ppermute | solution.py:17
Sparse Core Ops, SparseCore 0:
  384.3 88.8 all-reduce.6
where the time goes:
time: 488 us; the launch traced here: 484 us
  other arithmetic  252 us (52%)
  waiting for transfers between devices  103 us (21%)
  starting transfers between devices  76.5 us (16%)
  local copies, waits for them, and re-layouts  37.6 us (8%)
  between operations  15.2 us (3%)
    add x4, other arithmetic, advance(): return 2.0 * now_field - old_field + stiff * change + source_term  135 us
    psum x1, waiting for transfers between devices, on_device(): gradient = lax.psum(total, 'shot')  89.1 us
    ppermute x20, starting transfers between devices, passed_along(): return lax.ppermute(block, axis, route)  76.5 us
    add x1, other arithmetic, first_part(): total = total + first_coef[step - 1] * (upper - lower)  48.6 us
    unnamed x7, other arithmetic  31.2 us
    scatter-add x4, local copies, waits for them, and re-layouts, on_device(): inject = jnp.zeros((size_x, size_y, size_z), jnp.float32).at[clip_x, clip...  19.3 us
    concatenate x4, other arithmetic, extend(): x_ext = jnp.concatenate([lower_x, field, upper_x], axis=0)  14.3 us
    ppermute x20, waiting for transfers between devices, passed_along(): return lax.ppermute(block, axis, route)  14.1 us
  transfers between devices with their start and end apart: 21, of which 5 were waited for; matrix products, arithmetic and copies ran while one was open for 12% of the time, Pallas kernels for 0%

commit v1 on v0

v1 whole, which is shorter than its diff:
```python
import functools

import jax
import jax.numpy as jnp
import ml_dtypes
import numpy as np
from jax import lax
from jax.experimental import pallas as pl
from jax.experimental.pallas import tpu as pltpu
from jax.sharding import PartitionSpec as P

STEPS = 4
MUTE = 6
G = 8
RADIUS = 4

SECOND = (8064.0, -1008.0, 128.0, -9.0)
SECOND_CENTRE = -14350.0
SECOND_SCALE = 5040.0
FIRST = (672.0, -168.0, 32.0, -3.0)
FIRST_SCALE = 840.0

F32 = jnp.float32
BF16 = jnp.bfloat16


def banded(size, weights, odd):
    matrix = np.zeros((size, size + 2 * RADIUS), np.float32)
    for i in range(size):
        for k, w in enumerate(weights, 1):
            matrix[i, i + RADIUS + k] = w
            matrix[i, i + RADIUS - k] = -w if odd else w
    return matrix


def y_matrices(size):
    both = np.concatenate([banded(size, SECOND, False), banded(size, FIRST, True)])
    own = both[:, RADIUS:-RADIUS]
    result = []
    for parity in range(2):
        halo = np.zeros((2 * size, 16), np.float32)
        halo[:, 4 * parity : 4 * parity + 4] = both[:, :RADIUS]
        halo[:, 8 + 4 * parity : 12 + 4 * parity] = both[:, -RADIUS:]
        result.append(np.concatenate([own, own, halo, halo], axis=1))
    return np.stack(result).astype(ml_dtypes.bfloat16)


def z_matrix(size):
    second = banded(size, SECOND, False)[:, RADIUS:-RADIUS].T
    first = banded(size, FIRST, True)[:, RADIUS:-RADIUS].T
    both = np.concatenate([second, first], axis=1)
    return np.concatenate([both, both], axis=0).astype(ml_dtypes.bfloat16)


def parts(value):
    high = value.astype(BF16)
    low = (value - high.astype(F32)).astype(BF16)
    return high, low


def dot(a, b):
    return jnp.dot(a, b, preferred_element_type=F32)


def x_first(window, g):
    total = None
    for k, w in enumerate(FIRST, 1):
        term = w * (window[g + RADIUS + k] - window[g + RADIUS - k])
        total = term if total is None else total + term
    return total


def x_both(window, g):
    second = first = None
    for k in range(1, RADIUS + 1):
        upper, lower = window[g + RADIUS + k], window[g + RADIUS - k]
        s = SECOND[k - 1] * (upper + lower)
        f = FIRST[k - 1] * (upper - lower)
        second = s if second is None else second + s
        first = f if first is None else first + f
    return second, first


def halo_parts(low_ref, high_ref, pair):
    return parts(jnp.concatenate([low_ref[pair], high_ref[pair]], axis=0))


def pack_strips(field, low_ref, high_ref, offset):
    rows = lax.broadcasted_iota(jnp.int32, (8, field.shape[2]), 0)
    last = field.shape[1] - 8

    def body(i, carry):
        even, odd = field[2 * i, 0:8], field[2 * i + 1, 0:8]
        low_ref[offset + i] = jnp.where(rows < 4, even, pltpu.roll(odd, 4, 0))
        even, odd = field[2 * i, last:], field[2 * i + 1, last:]
        high_ref[offset + i] = jnp.where(rows < 4, pltpu.roll(even, 4, 0), odd)
        return carry

    lax.fori_loop(0, field.shape[0] // 2, body, 0, unroll=4)


def strips_kernel(q, b, xl, xh, yl, yh):
    size = q.shape[0]
    for source, at in ((q, 0), (b, RADIUS)):
        xl[at : at + RADIUS] = source[0:RADIUS]
        xh[at : at + RADIUS] = source[size - RADIUS : size]
    pack_strips(q, yl, yh, 0)
    pack_strips(b, yl, yh, size // 2)


def inject_kernel(places, amounts, openness, out, weights):
    pieces = amounts[...]
    high = pieces.astype(BF16).astype(F32)
    rest = pieces - high
    middle = rest.astype(BF16).astype(F32)
    low = rest - middle
    packed = high + pltpu.roll(middle, 32, 1) + pltpu.roll(low, 64, 1)
    weights[...] = packed.astype(BF16)
    size_x, size_y, lanes = out.shape
    block = 4
    receivers = places.shape[1]
    lane = lax.broadcasted_iota(jnp.int32, (block * size_y, lanes), 1)
    scale = openness[0].astype(F32)

    def body(i, carry):
        cells = lax.broadcasted_iota(jnp.int32, (block * size_y, receivers), 0) + i * (block * size_y)
        hit = jnp.where(cells == places[...], 1.0, 0.0).astype(BF16)
        found = dot(hit, weights[...])
        found = found + pltpu.roll(found, lanes - 32, 1) + pltpu.roll(found, lanes - 64, 1)
        found = jnp.where(lane < 32, found * scale, 0.0)
        for j in range(block):
            out[i * block + j] = found[j * size_y : (j + 1) * size_y]
        return carry

    lax.fori_loop(0, size_x // block, body, 0)


def make_coefficients(base, count, plane, r, yl, yh, ymat, zmat, ys, zs, stiff, buoy, coef, scale):
    size_y = r["size_y"]
    pairs = buoy.shape[0] // 2
    for g in range(count):
        high, low = parts(buoy[base + g])
        if g % 2 == 0:
            hh, hl = halo_parts(yl, yh, pairs + (base + g) // 2)
        ys[g, 0:size_y] = dot(ymat[g % 2, size_y:], jnp.concatenate([high, low, hh, hl], axis=0))
        zs[g, :, 0:256] = dot(jnp.concatenate([high, low], axis=1), zmat[:, 256:])
    for row in range(0, size_y, 16):
        for lane in range(0, 256, 128):
            at = (slice(row, row + 16), slice(lane, lane + 128))
            window = [plane(j, at) for j in range(count + 2 * RADIUS)]
            for g in range(count):
                s = stiff[(base + g,) + at] * scale
                t = s * (1.0 / (FIRST_SCALE * FIRST_SCALE))
                coef[0][(base + g,) + at] = s * (1.0 / SECOND_SCALE) * window[g + RADIUS]
                coef[1][(base + g,) + at] = t * x_first(window, g)
                coef[2][(base + g,) + at] = t * ys[(g,) + at]
                coef[3][(base + g,) + at] = t * zs[(g,) + at]


def advance(base, count, plane, r, step, q, p, out, yl, yh, ymat, zmat, ys, zs, coef, inject, snap, image, scale):
    size_y = r["size_y"]
    for g in range(count):
        high, low = parts(q[base + g])
        if g % 2 == 0:
            hh, hl = halo_parts(yl, yh, (base + g) // 2)
        ys[g] = dot(ymat[g % 2], jnp.concatenate([high, low, hh, hl], axis=0))
        zs[g] = dot(jnp.concatenate([high, low], axis=1), zmat[...])
    for row in range(0, size_y, 16):
        for lane in range(0, 256, 128):
            at = (slice(row, row + 16), slice(lane, lane + 128))
            below = (slice(size_y + row, size_y + row + 16), slice(lane, lane + 128))
            beside = (slice(row, row + 16), slice(256 + lane, 256 + lane + 128))
            window = [plane(j, at) for j in range(count + 2 * RADIUS)]
            for g in range(count):
                here = (base + g,) + at
                centre = window[g + RADIUS]
                second, first = x_both(window, g)
                second = (second + 3.0 * SECOND_CENTRE * centre) + (ys[(g,) + at] + zs[(g,) + at])
                change = coef[0][here] * second + coef[1][here] * first
                change = change + coef[2][here] * ys[(g,) + below] + coef[3][here] * zs[(g,) + beside]
                kept = (centre + centre) - p[here]
                if step < 2:
                    kept = kept * scale
                if lane == 0:
                    added = pltpu.roll(inject[base + g, row : row + 16, :], (128 - 8 * step) % 128, 1)
                    depth = lax.broadcasted_iota(jnp.int32, (16, 128), 1)
                    kept = kept + jnp.where(depth < 8, added, 0.0)
                value = kept + change
                out[here] = value
                shown = snap[here].astype(F32) * value
                image[here] = shown if step == 0 else image[here] + shown


def mute(image, source, corner, ranges):
    size_y = image.shape[1]
    y = lax.broadcasted_iota(jnp.int32, (size_y, 128), 0) + corner[1] - source[1]
    z = lax.broadcasted_iota(jnp.int32, (size_y, 128), 1) - source[2]
    flat = y * y + z * z
    for dx in range(1 - MUTE, MUTE):
        at = source[0] - corner[0] + dx
        inside = functools.reduce(lambda a, b: a | b, [(at >= lo) & (at < hi) for lo, hi in ranges])

        @pl.when(inside)
        def _():
            image[at, :, 0:128] = jnp.where(flat + dx * dx < MUTE * MUTE, 0.0, image[at, :, 0:128])


def inner_kernel(step, *refs):
    names = ["q", "p", "snap", "inject", "yl", "yh", "ymat", "zmat", "openness", "source", "corner"]
    names += ["stiff", "buoy"] if step == 0 else ["c0", "c1", "c2", "c3", "image_in"]
    names += ["out", "image"] + (["c0", "c1", "c2", "c3"] if step == 0 else []) + ["ys", "zs"]
    r = dict(zip(names, refs))
    size_x, size_y, _ = r["q"].shape
    r["size_y"] = size_y
    scale = r["openness"][0].astype(F32)
    coef = [r["c%d" % i] for i in range(4)]

    def body(i, carry):
        base = RADIUS + i * G
        common = (r["yl"], r["yh"], r["ymat"], r["zmat"], r["ys"], r["zs"])
        if step == 0:
            plane = lambda j, at: r["buoy"][(base - RADIUS + j,) + at]
            make_coefficients(base, G, plane, r, *common, r["stiff"], r["buoy"], coef, scale)
        plane = lambda j, at: r["q"][(base - RADIUS + j,) + at]
        advance(base, G, plane, r, step, r["q"], r["p"], r["out"], *common, coef, r["inject"], r["snap"], r["image"], scale)
        return carry

    lax.fori_loop(0, (size_x - 2 * RADIUS) // G, body, 0)
    if step == STEPS - 1:
        mute(r["image"], r["source"], r["corner"], [(RADIUS, size_x - RADIUS)])


def outer_kernel(step, *refs):
    names = ["q", "p", "snap", "inject", "yl", "yh", "ymat", "zmat", "openness", "source", "corner", "xl", "xh"]
    names += (["stiff", "buoy"] if step == 0 else []) + ["c0", "c1", "c2", "c3", "image_in"]
    names += ["out", "image"] + (["c0", "c1", "c2", "c3"] if step == 0 else [])
    names += ["sxl", "sxh", "syl", "syh"] if step < STEPS - 1 else []
    names += ["ys", "zs"]
    r = dict(zip(names, refs))
    size_x, size_y, _ = r["q"].shape
    r["size_y"] = size_y
    scale = r["openness"][0].astype(F32)
    coef = [r["c%d" % i] for i in range(4)]
    for base in (0, size_x - RADIUS):

        def reader(field, offset):
            def plane(j, at):
                where = base - RADIUS + j
                if where < 0:
                    return r["xl"][(offset + where + RADIUS,) + at]
                if where >= size_x:
                    return r["xh"][(offset + where - size_x,) + at]
                return field[(where,) + at]

            return plane

        common = (r["yl"], r["yh"], r["ymat"], r["zmat"], r["ys"], r["zs"])
        if step == 0:
            make_coefficients(
                base, RADIUS, reader(r["buoy"], RADIUS), r, *common, r["stiff"], r["buoy"], coef, scale
            )
        advance(
            base, RADIUS, reader(r["q"], 0), r, step, r["q"], r["p"], r["out"], *common, coef, r["inject"],
            r["snap"], r["image"], scale
        )
    if step == STEPS - 1:
        mute(r["image"], r["source"], r["corner"], [(0, RADIUS), (size_x - RADIUS, size_x)])
    else:
        r["sxl"][...] = r["out"][0:RADIUS]
        r["sxh"][...] = r["out"][size_x - RADIUS :]
        pack_strips(r["out"], r["syl"], r["syh"], 0)


VMEM = pl.BlockSpec(memory_space=pltpu.VMEM)
SMEM = pl.BlockSpec(memory_space=pltpu.SMEM)


def call(kernel, name, args, specs, outs, aliases, scratch, flops):
    results = pl.pallas_call(
        kernel,
        name=name,
        in_specs=specs,
        out_specs=[VMEM] * len(outs),
        out_shape=[pltpu.VMEM(shape, F32) for shape in outs],
        input_output_aliases=aliases,
        scratch_shapes=scratch,
        compiler_params=pltpu.CompilerParams(vmem_limit_bytes=12 << 20),
        cost_estimate=pl.CostEstimate(flops=flops, bytes_accessed=1 << 20, transcendentals=0),
    )(*args)
    return list(results)


def exchange(strips):
    sxl, sxh, syl, syh = strips
    tiles = range(lax.axis_size("dom"))
    along_y = [i for i in tiles if i % 4 < 3]
    along_x = [i for i in tiles if i + 4 in tiles]
    yl = lax.ppermute(syh, "dom", [(i, i + 1) for i in along_y])
    yh = lax.ppermute(syl, "dom", [(i + 1, i) for i in along_y])
    xl = lax.ppermute(sxh, "dom", [(i, i + 4) for i in along_x])
    xh = lax.ppermute(sxl, "dom", [(i + 4, i) for i in along_x])
    return xl, xh, yl, yh


def sum_over_shots(image):
    cores = [(i, i ^ 1) for i in range(4)]
    chips = [(i, i ^ 2) for i in range(4)]
    core = lax.axis_index("shot") % 2
    half = image.shape[0] // 2
    sent = lax.dynamic_slice_in_dim(image, (1 - core) * half, half, 0)
    kept = lax.dynamic_slice_in_dim(image, core * half, half, 0)
    mine = kept + lax.ppermute(sent, "shot", cores)
    mine = mine + lax.ppermute(mine, "shot", chips)
    other = lax.ppermute(mine, "shot", cores)
    low = jnp.where(core == 0, mine, other)
    high = jnp.where(core == 0, other, mine)
    return jnp.concatenate([low, high], axis=0)


def on_device(wave_prev, wave_now, stiffness, buoyancy, snapshots, traces, aperture, receivers, sources):
    index = lax.axis_index("dom")
    stiff, buoy = stiffness[0], buoyancy[0]
    size_x, size_y, size_z = buoy.shape
    grid = buoy.shape
    corner = jnp.stack([index // 4 * size_x, index % 4 * size_y]).astype(jnp.int32)
    openness = jnp.where(aperture[0] > 0, 1, 0).astype(jnp.int32)
    source = sources[0]
    q, p = wave_now[0, 0], wave_prev[0, 0]

    rec = receivers[0]
    local_x, local_y = rec[:, 0] - corner[0], rec[:, 1] - corner[1]
    inside = (local_x >= 0) & (local_x < size_x) & (local_y >= 0) & (local_y < size_y)
    places = jnp.where(inside, local_x * size_y + local_y, -1)[None, :]
    lane = jnp.arange(128, dtype=jnp.int32)
    spread = jnp.repeat(jnp.pad(traces[0].T, ((0, 0), (0, 12))), 8, axis=1)
    amounts = jnp.where((rec[:, 2:3] == lane[None, :] % 8) & (lane[None, :] < 32), spread, 0.0)

    ymat, zmat = jnp.asarray(y_matrices(size_y)), jnp.asarray(z_matrix(size_z))

    strips = call(
        strips_kernel, "strips", (q, buoy), [VMEM, VMEM],
        [(2 * RADIUS, size_y, size_z)] * 2 + [(size_x, 8, size_z)] * 2, {}, [], 1 << 20,
    )
    halos = exchange(strips)
    (inject,) = call(
        inject_kernel, "inject", (places, amounts, openness), [VMEM, VMEM, SMEM],
        [(size_x, size_y, 128)], {}, [pltpu.VMEM(amounts.shape, BF16)], 2 << 30,
    )

    work = [pltpu.VMEM((G, 2 * size_y, size_z), F32), pltpu.VMEM((G, size_y, 2 * size_z), F32)]
    coef = image = None
    for step in range(STEPS):
        xl, xh, yl, yh = halos
        snap = snapshots[0, step, 0]
        shared = [snap, inject, yl, yh, ymat, zmat, openness, source, corner]
        specs = [VMEM] * 8 + [SMEM] * 3
        if step == 0:
            args = [q, p] + shared + [stiff, buoy]
            out, image, *coef = call(
                functools.partial(inner_kernel, step), "inner%d" % step, args,
                specs + [VMEM] * 2, [grid] * 6, {1: 0}, work, 4 << 30,
            )
            args = [q, out] + shared + [xl, xh, stiff, buoy] + coef + [image]
            aliases = {1: 0, 19: 1, 15: 2, 16: 3, 17: 4, 18: 5}
            outs = [grid] * 6
        else:
            args = [q, p] + shared + coef + [image]
            out, image = call(
                functools.partial(inner_kernel, step), "inner%d" % step, args,
                specs + [VMEM] * 5, [grid] * 2, {1: 0, 15: 1}, work, 4 << 30,
            )
            args = [q, out] + shared + [xl, xh] + coef + [image]
            aliases = {1: 0, 17: 1}
            outs = [grid] * 2
        if step < STEPS - 1:
            outs = outs + [(RADIUS, size_y, size_z)] * 2 + [(size_x // 2, 8, size_z)] * 2
        results = call(
            functools.partial(outer_kernel, step), "outer%d" % step, args,
            specs + [VMEM] * (len(args) - 11), outs, aliases, work, 1 << 30,
        )
        q, p = results[0], q
        image = results[1]
        if step == 0:
            coef = results[2:6]
        if step < STEPS - 1:
            halos = exchange(results[-4:])
    return sum_over_shots(image)[None], q[None, None]


def solution(mesh):
    return jax.shard_map(
        on_device,
        mesh=mesh,
        in_specs=(
            P("shot", "dom", None, None, None),
            P("shot", "dom", None, None, None),
            P("dom", None, None, None),
            P("dom", None, None, None),
            P("shot", None, "dom", None, None, None),
            P("shot", None, None),
            P("shot", "dom"),
            P("shot", None, None),
            P("shot", None),
        ),
        out_specs=(P("dom", None, None, None), P("shot", "dom", None, None, None)),
        check_vma=False,
    )
```

time: 488 us -> 207 us (0.42)
  other arithmetic: 252 us -> 9.2 us
  waiting for transfers between devices: 103 us -> 40.3 us
  Pallas kernels: 0 us -> 47.8 us
  between operations: 15.2 us -> 1.95 us
  starting transfers between devices: 76.5 us -> 64.5 us
    add x6 -> x2, other arithmetic: 184 us -> 3.43 us  [the longest x1 2.09 us: sum_over_shots(): mine = kept + lax.ppermute(sent, 'shot', cores)]
    psum x1 -> x0, waiting for transfers between devices: 89.1 us -> none  [on_device(): gradient = lax.psum(total, 'shot')]
    pallas_call x0 -> x10, Pallas kernels: none -> 47.8 us  [call(): pl.pallas_call(kernel, name=name, in_specs=specs, out_specs=[VMEM] * len(...]
    unnamed x7 -> x0, other arithmetic: 31.2 us -> none
    unnamed x12 -> x68, local copies, waits for them, and re-layouts: 4.82 us -> 31.6 us
    ppermute x20 -> x19, waiting for transfers between devices: 14.1 us -> 40.3 us  [the longest x1 35.1 us: sum_over_shots(): mine = mine + lax.ppermute(mine, 'shot', chips)]
    concatenate x8 -> x0, other arithmetic: 23.4 us -> none  [the longest x4 14.3 us: extend(): x_ext = jnp.concatenate([lower_x, field, upper_x], axis=0)]
    scatter-add x4 -> x0, local copies, waits for them, and re-layouts: 19.3 us -> none  [on_device(): inject = jnp.zeros((size_x, size_y, size_z), jnp.float32).at[clip_x, clip...]
  transfers between devices with their start and end apart: 21 -> 19, of which waited for: 5 -> 3; matrix products, arithmetic and copies ran while one was open for 12% -> 6% of each run, Pallas kernels for 0% -> 18%
where the time goes in v1:
time: 207 us; the launch traced here: 206 us
  starting transfers between devices  64.5 us (31%)
  Pallas kernels  47.8 us (23%)
  local copies, waits for them, and re-layouts  41.8 us (20%)
  waiting for transfers between devices  40.3 us (19%)
  other arithmetic  9.2 us (4%)
    pallas_call x10, Pallas kernels, call(): pl.pallas_call(kernel, name=name, in_specs=specs, out_specs=[VMEM] * len(...  47.8 us
    ppermute x1, waiting for transfers between devices, sum_over_shots(): mine = mine + lax.ppermute(mine, 'shot', chips)  35.1 us
    unnamed x68, local copies, waits for them, and re-layouts  31.6 us
    ppermute x4, starting transfers between devices, exchange(): xh = lax.ppermute(sxl, 'dom', [(i + 4, i) for i in along_x])  26.9 us
    ppermute x4, starting transfers between devices, exchange(): yl = lax.ppermute(syh, 'dom', [(i, i + 1) for i in along_y])  13.1 us
    ppermute x4, starting transfers between devices, exchange(): xl = lax.ppermute(sxh, 'dom', [(i, i + 4) for i in along_x])  8.88 us
    ppermute x4, starting transfers between devices, exchange(): yh = lax.ppermute(syl, 'dom', [(i + 1, i) for i in along_y])  8.84 us
    squeeze x1, local copies, waits for them, and re-layouts, on_device(): snap = snapshots[0, step, 0]  6 us
  transfers between devices with their start and end apart: 19, of which 3 were waited for; matrix products, arithmetic and copies ran while one was open for 6% of the time, Pallas kernels for 18%

profile of v1, /device:TPU:57, one launch (start us, length us, event | category | flops | bytes accessed | tf_op | source)
XLA Modules:
  0.0 205.6 jit_solution(4377326283428715541)
XLA Ops:
  0.6 4.1 %copy.60 = f32[1,1,48,64,256]{4,3,2,1,0:T(8,128)} copy(f32[1,1,48,64,256]{4,3,2,1,0:T(8,128)} %param.11) | data formatting | bytes 6291456
  4.7 0.4 copy.57
  5.1 1.5 copy-done.18
  6.6 1.4 strips.1
  8.0 3.5 %collective-permute-start = (f32[48,8,256]{2,1,0:T(8,128)}, f32[48,8,256]{2,1,0:T(8,128)}, u32[]{:S(2)}, u32[]{:S(2)}) collective-permute-start(f32[48,8,256]{2,1,0:T(8,128)} %get-tuple-element.42), channel_id=1, source_target_pairs={{0,1},{1,2},{2,3},{4,5},{5,6},{6,7},{8,9},{9,10},{10,11},{12,13},{... | collective-permute-start | bytes 1179656 | tf_op jit(solution)/shard_map/ppermute | solution.py:298
  11.6 2.5 %collective-permute-start.1 = (f32[48,8,256]{2,1,0:T(8,128)}, f32[48,8,256]{2,1,0:T(8,128)}, u32[]{:S(2)}, u32[]{:S(2)}) collective-permute-start(f32[48,8,256]{2,1,0:T(8,128)} %get-tuple-element.43), channel_id=1, source_target_pairs={{1,0},{2,1},{3,2},{5,4},{6,5},{7,6},{9,8},{10,9},{11,10},{13,12},{... | collective-permute-start | bytes 1179656 | tf_op jit(solution)/shard_map/ppermute | solution.py:299
  14.1 3.1 %collective-permute-start.2 = (f32[8,64,256]{2,1,0:T(8,128)}, f32[8,64,256]{2,1,0:T(8,128)}, u32[]{:S(2)}, u32[]{:S(2)}) collective-permute-start(f32[8,64,256]{2,1,0:T(8,128)} %get-tuple-element.45), channel_id=1, source_target_pairs={{0,4},{1,5},{2,6},{3,7},{4,8},{5,9},{6,10},{7,11},{8,12},{9,13},{1... | collective-permute-start | bytes 1572872 | tf_op jit(solution)/shard_map/ppermute | solution.py:300
  17.2 5.8 %collective-permute-start.3 = (f32[8,64,256]{2,1,0:T(8,128)}, f32[8,64,256]{2,1,0:T(8,128)}, u32[]{:S(2)}, u32[]{:S(2)}) collective-permute-start(f32[8,64,256]{2,1,0:T(8,128)} %get-tuple-element.46), channel_id=1, source_target_pairs={{4,0},{5,1},{6,2},{7,3},{8,4},{9,5},{10,6},{11,7},{12,8},{13,9},{1... | collective-permute-start | bytes 1572872 | tf_op jit(solution)/shard_map/ppermute | solution.py:301
  23.1 0.8 broadcast_bitcast_fusion
  23.9 2.0 copy.33
  26.0 6.0 %slice_bitcast_fusion = (bf16[48,64,256]{2,1,0:T(8,128)(2,1)}, bf16[48,64,256]{2,1,0:T(8,128)(2,1)}, bf16[48,64,256]{2,1,0:T(8,128)(2,1)}, bf16[48,64,256]{2,1,0:T(8,128)(2,1)}) fusion(bf16[1,4,1,48,64,256]{5,4,3,2,1,0:T(8,128)(2,1)} %param.15), kind=kLoop, calls=%fused_computation.2 | loop fusion | bytes 12582912 | tf_op jit(solution)/shard_map/squeeze | solution.py:354
  32.0 1.4 and_select_fusion.amounts
  34.0 0.0 copy-start
  34.0 0.0 copy-start.16
  34.1 0.0 copy-start.25
  34.1 4.7 %inject.1.refs_3_ = f32[48,64,128]{2,1,0:T(8,128)S(1)} custom-call(s32[1,1024]{1,0:T(1,128)S(1)} %get-tuple-element.89.places, f32[1024,128]{1,0:T(8,128)S(1)} %and_select_fusion.amounts, s32[1]{0:T(128)} %bitcast.8.openness.refs_8_), custom_call_target="tpu_custom_call" | custom-call | flops 2147483648 | bytes 1048576 | tf_op jit(solution)/shard_map/inject/pallas_call | solution.py:279
  38.8 0.1 pad_add_fusion.refs_10_
  38.9 2.3 %copy-done.24 = f32[1,48,64,256]{3,2,1,0:T(8,128)S(1)} copy-done((f32[1,48,64,256]{3,2,1,0:T(8,128)S(1)}, f32[1,48,64,256]{3,2,1,0:T(8,128)}, u32[]{:S(2)}) %copy-start.24) | copy-done | bytes 3145752
  41.3 10.4 %inner0.1 = (f32[48,64,256]{2,1,0:T(8,128)S(1)}, f32[48,64,256]{2,1,0:T(8,128)S(1)}, f32[48,64,256]{2,1,0:T(8,128)S(1)}, f32[48,64,256]{2,1,0:T(8,128)S(1)}, f32...) custom-call(f32[48,64,256]{2,1,0:T(8,128)S(1)} %bitcast.31, ...), custom_call_target="tpu_custom_call", output_to_operand_aliasing={{0}: (1, {})} | custom-call | flops 4294967296 | bytes 1048576 | tf_op jit(solution)/shard_map/inner0/pallas_call | solution.py:279
  51.7 3.4 %outer0.1 = (f32[48,64,256]{2,1,0:T(8,128)S(1)}, f32[48,64,256]{2,1,0:T(8,128)S(1)}, f32[48,64,256]{2,1,0:T(8,128)S(1)}, f32[48,64,256]{2,1,0:T(8,128)S(1)}, f32...) custom-call(f32[48,64,256]{2,1,0:T(8,128)S(1)} %bitcast.32, ...), custom_call_target="tpu_custom_call", output_to_operand_aliasing={{0}: (1, {}), {1}: (19, {}), {2}: (15, {}), {3}: (16, {}), ... | custom-call | flops 1073741824 | bytes 1048576 | tf_op jit(solution)/shard_map/outer0/pallas_call | solution.py:279
  55.1 2.8 %collective-permute-start.4 = (f32[24,8,256]{2,1,0:T(8,128)S(1)}, f32[24,8,256]{2,1,0:T(8,128)S(1)}, u32[]{:S(2)}, u32[]{:S(2)}) collective-permute-start(f32[24,8,256]{2,1,0:T(8,128)S(1)} %get-tuple-element.53), channel_id=1, source_target_pairs={{0,1},{1,2},{2,3},{4,5},{5,6},{6,7},{8,9},{9,10},{10,11},{12,13},{... | collective-permute-start | bytes 589832 | tf_op jit(solution)/shard_map/ppermute | solution.py:298
  57.9 2.5 %collective-permute-start.5 = (f32[24,8,256]{2,1,0:T(8,128)S(1)}, f32[24,8,256]{2,1,0:T(8,128)S(1)}, u32[]{:S(2)}, u32[]{:S(2)}) collective-permute-start(f32[24,8,256]{2,1,0:T(8,128)S(1)} %get-tuple-element.54), channel_id=1, source_target_pairs={{1,0},{2,1},{3,2},{5,4},{6,5},{7,6},{9,8},{10,9},{11,10},{13,12},{... | collective-permute-start | bytes 589832 | tf_op jit(solution)/shard_map/ppermute | solution.py:299
  60.4 1.9 collective-permute-start.6
  62.4 7.0 %collective-permute-start.7 = (f32[4,64,256]{2,1,0:T(8,128)S(1)}, f32[4,64,256]{2,1,0:T(8,128)S(1)}, u32[]{:S(2)}, u32[]{:S(2)}) collective-permute-start(f32[4,64,256]{2,1,0:T(8,128)S(1)} %get-tuple-element.62), channel_id=1, source_target_pairs={{4,0},{5,1},{6,2},{7,3},{8,4},{9,5},{10,6},{11,7},{12,8},{13,9},{1... | collective-permute-start | bytes 786440 | tf_op jit(solution)/shard_map/ppermute | solution.py:301
  69.4 7.3 %inner1.1 = (f32[48,64,256]{2,1,0:T(8,128)S(1)}, f32[48,64,256]{2,1,0:T(8,128)S(1)}) custom-call(f32[48,64,256]{2,1,0:T(8,128)S(1)} %get-tuple-element.52.refs_0_.refs_1_, f32[48,64,256]{2,1,0:T(8,128)S(1)} %bitcast.33, bf16[48,64,256]{2,1,0:T(8,128)(2,1)S(1)} %copy-done.22, ...), custom_call_target="tpu_custom_call", output_to_operand_aliasing={{0}: (1, {}), {1}: (15, {})} | custom-call | flops 4294967296 | bytes 1048576 | tf_op jit(solution)/shard_map/inner1/pallas_call | solution.py:279
  76.8 1.7 outer1.1
  78.4 3.5 %collective-permute-start.8 = (f32[24,8,256]{2,1,0:T(8,128)S(1)}, f32[24,8,256]{2,1,0:T(8,128)S(1)}, u32[]{:S(2)}, u32[]{:S(2)}) collective-permute-start(f32[24,8,256]{2,1,0:T(8,128)S(1)} %get-tuple-element.65), channel_id=1, source_target_pairs={{0,1},{1,2},{2,3},{4,5},{5,6},{6,7},{8,9},{9,10},{10,11},{12,13},{... | collective-permute-start | bytes 589832 | tf_op jit(solution)/shard_map/ppermute | solution.py:298
  81.9 1.9 collective-permute-start.9
  83.8 1.9 collective-permute-start.10
  85.8 7.0 %collective-permute-start.11 = (f32[4,64,256]{2,1,0:T(8,128)S(1)}, f32[4,64,256]{2,1,0:T(8,128)S(1)}, u32[]{:S(2)}, u32[]{:S(2)}) collective-permute-start(f32[4,64,256]{2,1,0:T(8,128)S(1)} %get-tuple-element.70), channel_id=1, source_target_pairs={{4,0},{5,1},{6,2},{7,3},{8,4},{9,5},{10,6},{11,7},{12,8},{13,9},{1... | collective-permute-start | bytes 786440 | tf_op jit(solution)/shard_map/ppermute | solution.py:301
  92.8 6.9 %inner2.1 = (f32[48,64,256]{2,1,0:T(8,128)S(1)}, f32[48,64,256]{2,1,0:T(8,128)S(1)}) custom-call(f32[48,64,256]{2,1,0:T(8,128)S(1)} %get-tuple-element.64.refs_0_.refs_1_, f32[48,64,256]{2,1,0:T(8,128)S(1)} %get-tuple-element.52.refs_0_.refs_1_, bf16[48,64,256]{2,1,0:T(8,128)(2,1)S(1)} %copy-done.21, ...), custom_call_target="tpu_custom_call", output_to_operand_aliasing={{0}: (1, {}), {1}: (15, {})} | custom-call | flops 4294967296 | bytes 1048576 | tf_op jit(solution)/shard_map/inner2/pallas_call | solution.py:279
  99.8 2.4 %outer2.1 = (f32[48,64,256]{2,1,0:T(8,128)S(1)}, f32[48,64,256]{2,1,0:T(8,128)S(1)}, f32[4,64,256]{2,1,0:T(8,128)S(1)}, f32[4,64,256]{2,1,0:T(8,128)S(1)}, f32[24,8,256]{2,1,0:T(8,128)}, /*index=5*/f32[24,8,256]{2,1,0:T(8,128)}) custom-call(f32[48,64,256]{2,1,0:T(8,128)S(1)} %get-tuple-element.64.refs_0_.refs_1_, ...), custom_call_target="tpu_custom_call", output_to_operand_aliasing={{0}: (1, {}), {1}: (17, {})} | custom-call | flops 1073741824 | bytes 1048576 | tf_op jit(solution)/shard_map/outer2/pallas_call | solution.py:279
  102.2 1.7 copy-done.1
  103.9 1.7 copy-done.3
  105.6 0.7 copy-done.27
  106.3 0.7 copy-done.28
  107.0 3.3 %collective-permute-start.12 = (f32[24,8,256]{2,1,0:T(8,128)}, f32[24,8,256]{2,1,0:T(8,128)S(1)}, u32[]{:S(2)}, u32[]{:S(2)}) collective-permute-start(f32[24,8,256]{2,1,0:T(8,128)} %get-tuple-element.73), channel_id=1, source_target_pairs={{0,1},{1,2},{2,3},{4,5},{5,6},{6,7},{8,9},{9,10},{10,11},{12,13},{... | collective-permute-start | bytes 589832 | tf_op jit(solution)/shard_map/ppermute | solution.py:298
  110.4 1.9 collective-permute-start.13
  112.3 1.9 collective-permute-start.14
  114.2 7.2 %collective-permute-start.15 = (f32[4,64,256]{2,1,0:T(8,128)}, f32[4,64,256]{2,1,0:T(8,128)S(1)}, u32[]{:S(2)}, u32[]{:S(2)}) collective-permute-start(f32[4,64,256]{2,1,0:T(8,128)} %copy-done.27), channel_id=1, source_target_pairs={{4,0},{5,1},{6,2},{7,3},{8,4},{9,5},{10,6},{11,7},{12,8},{13,9},{1... | collective-permute-start | bytes 786440 | tf_op jit(solution)/shard_map/ppermute | solution.py:301
  121.4 1.9 copy-done.2
  123.3 1.9 copy-done.4
  125.2 1.9 copy-done.7
  127.1 1.9 copy-done.9
  129.0 1.9 copy-done.11
  130.9 1.9 copy-done.13
  132.8 1.4 copy-done.15
  134.2 1.0 copy-done.17
  135.2 1.4 copy-done.20
  136.6 7.4 %inner3.1 = (f32[48,64,256]{2,1,0:T(8,128)S(1)}, f32[48,64,256]{2,1,0:T(8,128)S(1)}) custom-call(f32[48,64,256]{2,1,0:T(8,128)S(1)} %copy-done.2, f32[48,64,256]{2,1,0:T(8,128)S(1)} %get-tuple-element.64.refs_0_.refs_1_, bf16[48,64,256]{2,1,0:T(8,128)(2,1)S(1)} %copy-done.20, ...), custom_call_target="tpu_custom_call", output_to_operand_aliasing={{0}: (1, {}), {1}: (15, {})} | custom-call | flops 4294967296 | bytes 1048576 | tf_op jit(solution)/shard_map/inner3/pallas_call | solution.py:279
  144.1 2.1 %outer3.1 = (f32[48,64,256]{2,1,0:T(8,128)S(1)}, f32[48,64,256]{2,1,0:T(8,128)S(1)}) custom-call(f32[48,64,256]{2,1,0:T(8,128)S(1)} %copy-done.2, f32[48,64,256]{2,1,0:T(8,128)S(1)} %get-tuple-element.76.refs_1_, bf16[48,64,256]{2,1,0:T(8,128)(2,1)S(1)} %copy-done.20, f32[48,64,128]{2,1,0:T(8,128)S(1)} %copy-done.15, ...), custom_call_target="tpu_custom_call", output_to_operand_aliasing={{0}: (1, {}), {1}: (17, {})} | custom-call | flops 1073741824 | bytes 1048576 | tf_op jit(solution)/shard_map/outer3/pallas_call | solution.py:279
  146.2 1.7 copy-done.5
  147.9 1.3 constant_dynamic-slice_fusion
  149.2 5.1 %collective-permute-start.16 = (f32[24,64,256]{2,1,0:T(8,128)}, f32[24,64,256]{2,1,0:T(8,128)}, u32[]{:S(2)}, u32[]{:S(2)}) collective-permute-start(f32[24,64,256]{2,1,0:T(8,128)} %constant_dynamic-slice_fusion), channel_id=1, source_target_pairs={{0,32},{32,0},{64,96},{96,64},{1,33},{33,1},{65,97},{97,65},{2,34}... | collective-permute-start | bytes 4718600 | tf_op jit(solution)/shard_map/ppermute | solution.py:312
  154.2 3.4 %collective-permute-done.16 = f32[24,64,256]{2,1,0:T(8,128)} collective-permute-done((f32[24,64,256]{2,1,0:T(8,128)}, f32[24,64,256]{2,1,0:T(8,128)}, u32[]{:S(2)}, u32[]{:S(2)}) %collective-permute-start.16) | collective-permute-done | bytes 1572896 | tf_op jit(solution)/shard_map/ppermute | solution.py:312
  157.6 2.1 %dynamic-slice_add_fusion = f32[24,64,256]{2,1,0:T(8,128)S(1)} fusion(f32[24,64,256]{2,1,0:T(8,128)} %collective-permute-done.16, f32[48,64,256]{2,1,0:T(8,128)} %copy-done.5, s32[]{:T(128)S(6)} %select_n.74), kind=kLoop, calls=%fused_computation.1 | loop fusion | flops 393216 | bytes 4718596 | tf_op jit(solution)/shard_map/add | solution.py:312
  159.7 0.5 collective-permute-start.17
  160.2 35.1 %collective-permute-done.17 = f32[24,64,256]{2,1,0:T(8,128)S(1)} collective-permute-done((f32[24,64,256]{2,1,0:T(8,128)S(1)}, f32[24,64,256]{2,1,0:T(8,128)S(1)}, u32[]{:S(2)}, u32[]{:S(2)}) %collective-permute-start.17) | collective-permute-done | bytes 1572896 | tf_op jit(solution)/shard_map/ppermute | solution.py:313
  195.4 1.3 add.54
  196.7 1.2 collective-permute-start.18
  197.9 1.7 copy.58
  199.6 1.7 collective-permute-done.18
  201.3 2.3 %broadcast_select_fusion.1 = (f32[24,64,256]{2,1,0:T(8,128)S(1)}, f32[24,64,256]{2,1,0:T(8,128)S(1)}) fusion(f32[24,64,256]{2,1,0:T(8,128)} %add.54, f32[24,64,256]{2,1,0:T(8,128)} %collective-permute-done.18, pred[]{:T(512)S(6)} %eq.24), kind=kLoop, calls=%fused_computation.7 | loop fusion | flops 786432 | bytes 6291457 | tf_op jit(solution)/shard_map/jit(_where)/select_n | solution.py:315
  203.6 2.0 maximum_bitcast_fusion
  (66 shorter events, 0.2 us)
Async XLA Ops:
  0.6 4.1 %copy-start.29 = (f32[1,1,48,64,256]{4,3,2,1,0:T(8,128)S(1)}, f32[1,1,48,64,256]{4,3,2,1,0:T(8,128)}, u32[]{:S(2)}) copy-start(f32[1,1,48,64,256]{4,3,2,1,0:T(8,128)} %param.12) | copy-start | bytes 9437188
  4.7 1.9 copy-start.18
  6.6 16.5 %copy-start.31 = (s32[1,1024,3]{1,0,2:T(1,128)S(1)}, s32[1,1024,3]{1,0,2:T(1,128)}, u32[]{:S(2)}) copy-start(s32[1,1024,3]{1,0,2:T(1,128)} %param.18) | copy-start | bytes 36868
  6.6 16.5 %copy-start.30 = (f32[1,4,1024]{2,1,0:T(4,128)S(1)}, f32[1,4,1024]{2,1,0:T(4,128)}, u32[]{:S(2)}) copy-start(f32[1,4,1024]{2,1,0:T(4,128)} %param.16) | copy-start | bytes 49156
  8.0 30.8 %collective-permute-start = (f32[48,8,256]{2,1,0:T(8,128)}, f32[48,8,256]{2,1,0:T(8,128)}, u32[]{:S(2)}, u32[]{:S(2)}) collective-permute-start(f32[48,8,256]{2,1,0:T(8,128)} %get-tuple-element.42), channel_id=1, source_target_pairs={{0,1},{1,2},{2,3},{4,5},{5,6},{6,7},{8,9},{9,10},{10,11},{12,13},{... | collective-permute-start | bytes 1179656 | tf_op jit(solution)/shard_map/ppermute | solution.py:298
  11.6 27.3 %collective-permute-start.1 = (f32[48,8,256]{2,1,0:T(8,128)}, f32[48,8,256]{2,1,0:T(8,128)}, u32[]{:S(2)}, u32[]{:S(2)}) collective-permute-start(f32[48,8,256]{2,1,0:T(8,128)} %get-tuple-element.43), channel_id=1, source_target_pairs={{1,0},{2,1},{3,2},{5,4},{6,5},{7,6},{9,8},{10,9},{11,10},{13,12},{... | collective-permute-start | bytes 1179656 | tf_op jit(solution)/shard_map/ppermute | solution.py:299
  14.1 37.6 %collective-permute-start.2 = (f32[8,64,256]{2,1,0:T(8,128)}, f32[8,64,256]{2,1,0:T(8,128)}, u32[]{:S(2)}, u32[]{:S(2)}) collective-permute-start(f32[8,64,256]{2,1,0:T(8,128)} %get-tuple-element.45), channel_id=1, source_target_pairs={{0,4},{1,5},{2,6},{3,7},{4,8},{5,9},{6,10},{7,11},{8,12},{9,13},{1... | collective-permute-start | bytes 1572872 | tf_op jit(solution)/shard_map/ppermute | solution.py:300
  17.2 34.4 %collective-permute-start.3 = (f32[8,64,256]{2,1,0:T(8,128)}, f32[8,64,256]{2,1,0:T(8,128)}, u32[]{:S(2)}, u32[]{:S(2)}) collective-permute-start(f32[8,64,256]{2,1,0:T(8,128)} %get-tuple-element.46), channel_id=1, source_target_pairs={{4,0},{5,1},{6,2},{7,3},{8,4},{9,5},{10,6},{11,7},{12,8},{13,9},{1... | collective-permute-start | bytes 1572872 | tf_op jit(solution)/shard_map/ppermute | solution.py:301
  32.0 6.9 %copy-start.23 = (bf16[48,64,256]{2,1,0:T(8,128)(2,1)S(1)}, bf16[48,64,256]{2,1,0:T(8,128)(2,1)}, u32[]{:S(2)}) copy-start(bf16[48,64,256]{2,1,0:T(8,128)(2,1)} %get-tuple-element.84.refs_2_) | copy-start | bytes 4718596
  34.0 4.9 %copy-start = (f32[1,1,48,64,256]{4,3,2,1,0:T(8,128)S(1)}, f32[1,1,48,64,256]{4,3,2,1,0:T(8,128)}, u32[]{:S(2)}) copy-start(f32[1,1,48,64,256]{4,3,2,1,0:T(8,128)} %copy.60) | copy-start | bytes 9437188
  34.0 4.9 %copy-start.16 = (bf16[512,512]{1,0:T(8,128)(2,1)S(1)}, bf16[512,512]{1,0:T(8,128)(2,1)}, u32[]{:S(2)}) copy-start(bf16[512,512]{1,0:T(8,128)(2,1)} %constant.88.clone.refs_7_) | copy-start | bytes 1572868
  34.1 4.9 %copy-start.19 = (f32[1,48,64,256]{3,2,1,0:T(8,128)S(1)}, f32[1,48,64,256]{3,2,1,0:T(8,128)}, u32[]{:S(2)}) copy-start(f32[1,48,64,256]{3,2,1,0:T(8,128)} %param.14) | copy-start | bytes 9437188
  34.1 4.9 %copy-start.25 = (bf16[2,128,160]{2,1,0:T(8,128)(2,1)S(1)}, bf16[2,128,160]{2,1,0:T(8,128)(2,1)}, u32[]{:S(2)}) copy-start(bf16[2,128,160]{2,1,0:T(8,128)(2,1)} %constant.87.clone.refs_6_) | copy-start | bytes 245764
  34.1 4.9 %copy-start.26 = (s32[1,3]{1,0:T(1,128)S(1)}, s32[1,3]{1,0:T(1,128)}, u32[]{:S(2)}) copy-start(s32[1,3]{1,0:T(1,128)} %param.19) | copy-start | bytes 40
  38.8 61.0 %copy-start.14 = (f32[48,64,128]{2,1,0:T(8,128)}, f32[48,64,128]{2,1,0:T(8,128)S(1)}, u32[]{:S(2)}) copy-start(f32[48,64,128]{2,1,0:T(8,128)S(1)} %inject.1.refs_3_) | copy-start | bytes 4718596
  38.9 2.3 %copy-start.24 = (f32[1,48,64,256]{3,2,1,0:T(8,128)S(1)}, f32[1,48,64,256]{3,2,1,0:T(8,128)}, u32[]{:S(2)}) copy-start(f32[1,48,64,256]{3,2,1,0:T(8,128)} %param.13) | copy-start | bytes 9437188
  51.7 17.7 %copy-start.22 = (bf16[48,64,256]{2,1,0:T(8,128)(2,1)S(1)}, bf16[48,64,256]{2,1,0:T(8,128)(2,1)}, u32[]{:S(2)}) copy-start(bf16[48,64,256]{2,1,0:T(8,128)(2,1)} %get-tuple-element.83.refs_2_) | copy-start | bytes 4718596
  55.1 44.7 %copy-start.6 = (f32[48,64,256]{2,1,0:T(8,128)}, f32[48,64,256]{2,1,0:T(8,128)S(1)}, u32[]{:S(2)}) copy-start(f32[48,64,256]{2,1,0:T(8,128)S(1)} %get-tuple-element.55.refs_11_.refs_13_) | copy-start | bytes 9437188
  55.1 44.7 %copy-start.8 = (f32[48,64,256]{2,1,0:T(8,128)}, f32[48,64,256]{2,1,0:T(8,128)S(1)}, u32[]{:S(2)}) copy-start(f32[48,64,256]{2,1,0:T(8,128)S(1)} %get-tuple-element.56.refs_12_.refs_14_) | copy-start | bytes 9437188
  55.1 44.7 %copy-start.10 = (f32[48,64,256]{2,1,0:T(8,128)}, f32[48,64,256]{2,1,0:T(8,128)S(1)}, u32[]{:S(2)}) copy-start(f32[48,64,256]{2,1,0:T(8,128)S(1)} %get-tuple-element.57.refs_13_.refs_15_) | copy-start | bytes 9437188
  55.1 44.7 %copy-start.12 = (f32[48,64,256]{2,1,0:T(8,128)}, f32[48,64,256]{2,1,0:T(8,128)S(1)}, u32[]{:S(2)}) copy-start(f32[48,64,256]{2,1,0:T(8,128)S(1)} %get-tuple-element.58.refs_14_.refs_16_) | copy-start | bytes 9437188
  55.1 14.2 %collective-permute-start.4 = (f32[24,8,256]{2,1,0:T(8,128)S(1)}, f32[24,8,256]{2,1,0:T(8,128)S(1)}, u32[]{:S(2)}, u32[]{:S(2)}) collective-permute-start(f32[24,8,256]{2,1,0:T(8,128)S(1)} %get-tuple-element.53), channel_id=1, source_target_pairs={{0,1},{1,2},{2,3},{4,5},{5,6},{6,7},{8,9},{9,10},{10,11},{12,13},{... | collective-permute-start | bytes 589832 | tf_op jit(solution)/shard_map/ppermute | solution.py:298
  57.9 11.4 %collective-permute-start.5 = (f32[24,8,256]{2,1,0:T(8,128)S(1)}, f32[24,8,256]{2,1,0:T(8,128)S(1)}, u32[]{:S(2)}, u32[]{:S(2)}) collective-permute-start(f32[24,8,256]{2,1,0:T(8,128)S(1)} %get-tuple-element.54), channel_id=1, source_target_pairs={{1,0},{2,1},{3,2},{5,4},{6,5},{7,6},{9,8},{10,9},{11,10},{13,12},{... | collective-permute-start | bytes 589832 | tf_op jit(solution)/shard_map/ppermute | solution.py:299
  60.4 16.3 %collective-permute-start.6 = (f32[4,64,256]{2,1,0:T(8,128)S(1)}, f32[4,64,256]{2,1,0:T(8,128)S(1)}, u32[]{:S(2)}, u32[]{:S(2)}) collective-permute-start(f32[4,64,256]{2,1,0:T(8,128)S(1)} %get-tuple-element.61), channel_id=1, source_target_pairs={{0,4},{1,5},{2,6},{3,7},{4,8},{5,9},{6,10},{7,11},{8,12},{9,13},{1... | collective-permute-start | bytes 786440 | tf_op jit(solution)/shard_map/ppermute | solution.py:300
  62.4 14.4 %collective-permute-start.7 = (f32[4,64,256]{2,1,0:T(8,128)S(1)}, f32[4,64,256]{2,1,0:T(8,128)S(1)}, u32[]{:S(2)}, u32[]{:S(2)}) collective-permute-start(f32[4,64,256]{2,1,0:T(8,128)S(1)} %get-tuple-element.62), channel_id=1, source_target_pairs={{4,0},{5,1},{6,2},{7,3},{8,4},{9,5},{10,6},{11,7},{12,8},{13,9},{1... | collective-permute-start | bytes 786440 | tf_op jit(solution)/shard_map/ppermute | solution.py:301
  76.7 16.0 %copy-start.21 = (bf16[48,64,256]{2,1,0:T(8,128)(2,1)S(1)}, bf16[48,64,256]{2,1,0:T(8,128)(2,1)}, u32[]{:S(2)}) copy-start(bf16[48,64,256]{2,1,0:T(8,128)(2,1)} %get-tuple-element.85.refs_2_) | copy-start | bytes 4718596
  78.4 14.3 %collective-permute-start.8 = (f32[24,8,256]{2,1,0:T(8,128)S(1)}, f32[24,8,256]{2,1,0:T(8,128)S(1)}, u32[]{:S(2)}, u32[]{:S(2)}) collective-permute-start(f32[24,8,256]{2,1,0:T(8,128)S(1)} %get-tuple-element.65), channel_id=1, source_target_pairs={{0,1},{1,2},{2,3},{4,5},{5,6},{6,7},{8,9},{9,10},{10,11},{12,13},{... | collective-permute-start | bytes 589832 | tf_op jit(solution)/shard_map/ppermute | solution.py:298
  81.9 10.9 %collective-permute-start.9 = (f32[24,8,256]{2,1,0:T(8,128)S(1)}, f32[24,8,256]{2,1,0:T(8,128)S(1)}, u32[]{:S(2)}, u32[]{:S(2)}) collective-permute-start(f32[24,8,256]{2,1,0:T(8,128)S(1)} %get-tuple-element.66), channel_id=1, source_target_pairs={{1,0},{2,1},{3,2},{5,4},{6,5},{7,6},{9,8},{10,9},{11,10},{13,12},{... | collective-permute-start | bytes 589832 | tf_op jit(solution)/shard_map/ppermute | solution.py:299
  83.8 15.9 %collective-permute-start.10 = (f32[4,64,256]{2,1,0:T(8,128)S(1)}, f32[4,64,256]{2,1,0:T(8,128)S(1)}, u32[]{:S(2)}, u32[]{:S(2)}) collective-permute-start(f32[4,64,256]{2,1,0:T(8,128)S(1)} %get-tuple-element.69), channel_id=1, source_target_pairs={{0,4},{1,5},{2,6},{3,7},{4,8},{5,9},{6,10},{7,11},{8,12},{9,13},{1... | collective-permute-start | bytes 786440 | tf_op jit(solution)/shard_map/ppermute | solution.py:300
  85.8 14.0 %collective-permute-start.11 = (f32[4,64,256]{2,1,0:T(8,128)S(1)}, f32[4,64,256]{2,1,0:T(8,128)S(1)}, u32[]{:S(2)}, u32[]{:S(2)}) collective-permute-start(f32[4,64,256]{2,1,0:T(8,128)S(1)} %get-tuple-element.70), channel_id=1, source_target_pairs={{4,0},{5,1},{6,2},{7,3},{8,4},{9,5},{10,6},{11,7},{12,8},{13,9},{1... | collective-permute-start | bytes 786440 | tf_op jit(solution)/shard_map/ppermute | solution.py:301
  102.2 1.7 copy-start.1
  103.9 1.7 copy-start.3
  105.6 0.7 copy-start.27
  106.3 0.7 copy-start.28
  107.0 14.4 %collective-permute-start.12 = (f32[24,8,256]{2,1,0:T(8,128)}, f32[24,8,256]{2,1,0:T(8,128)S(1)}, u32[]{:S(2)}, u32[]{:S(2)}) collective-permute-start(f32[24,8,256]{2,1,0:T(8,128)} %get-tuple-element.73), channel_id=1, source_target_pairs={{0,1},{1,2},{2,3},{4,5},{5,6},{6,7},{8,9},{9,10},{10,11},{12,13},{... | collective-permute-start | bytes 589832 | tf_op jit(solution)/shard_map/ppermute | solution.py:298
  110.4 11.1 %collective-permute-start.13 = (f32[24,8,256]{2,1,0:T(8,128)}, f32[24,8,256]{2,1,0:T(8,128)}, u32[]{:S(2)}, u32[]{:S(2)}) collective-permute-start(f32[24,8,256]{2,1,0:T(8,128)} %get-tuple-element.74), channel_id=1, source_target_pairs={{1,0},{2,1},{3,2},{5,4},{6,5},{7,6},{9,8},{10,9},{11,10},{13,12},{... | collective-permute-start | bytes 589832 | tf_op jit(solution)/shard_map/ppermute | solution.py:299
  112.3 31.8 %collective-permute-start.14 = (f32[4,64,256]{2,1,0:T(8,128)}, f32[4,64,256]{2,1,0:T(8,128)S(1)}, u32[]{:S(2)}, u32[]{:S(2)}) collective-permute-start(f32[4,64,256]{2,1,0:T(8,128)} %copy-done.28), channel_id=1, source_target_pairs={{0,4},{1,5},{2,6},{3,7},{4,8},{5,9},{6,10},{7,11},{8,12},{9,13},{1... | collective-permute-start | bytes 786440 | tf_op jit(solution)/shard_map/ppermute | solution.py:300
  114.2 29.8 %collective-permute-start.15 = (f32[4,64,256]{2,1,0:T(8,128)}, f32[4,64,256]{2,1,0:T(8,128)S(1)}, u32[]{:S(2)}, u32[]{:S(2)}) collective-permute-start(f32[4,64,256]{2,1,0:T(8,128)} %copy-done.27), channel_id=1, source_target_pairs={{4,0},{5,1},{6,2},{7,3},{8,4},{9,5},{10,6},{11,7},{12,8},{13,9},{1... | collective-permute-start | bytes 786440 | tf_op jit(solution)/shard_map/ppermute | solution.py:301
  121.4 1.9 copy-start.2
  123.3 1.9 copy-start.4
  125.2 1.9 copy-start.7
  127.1 1.9 copy-start.9
  129.0 1.9 copy-start.11
  130.9 1.9 copy-start.13
  132.8 1.4 copy-start.15
  134.2 1.0 copy-start.17
  135.2 1.4 copy-start.20
  146.2 1.7 copy-start.5
  149.2 8.4 %collective-permute-start.16 = (f32[24,64,256]{2,1,0:T(8,128)}, f32[24,64,256]{2,1,0:T(8,128)}, u32[]{:S(2)}, u32[]{:S(2)}) collective-permute-start(f32[24,64,256]{2,1,0:T(8,128)} %constant_dynamic-slice_fusion), channel_id=1, source_target_pairs={{0,32},{32,0},{64,96},{96,64},{1,33},{33,1},{65,97},{97,65},{2,34}... | collective-permute-start | bytes 4718600 | tf_op jit(solution)/shard_map/ppermute | solution.py:312
  159.7 35.7 %collective-permute-start.17 = (f32[24,64,256]{2,1,0:T(8,128)S(1)}, f32[24,64,256]{2,1,0:T(8,128)S(1)}, u32[]{:S(2)}, u32[]{:S(2)}) collective-permute-start(f32[24,64,256]{2,1,0:T(8,128)S(1)} %dynamic-slice_add_fusion), channel_id=1, source_target_pairs={{0,64},{32,96},{64,0},{96,32},{1,65},{33,97},{65,1},{97,33},{2,66}... | collective-permute-start | bytes 4718600 | tf_op jit(solution)/shard_map/ppermute | solution.py:313
  196.7 4.6 %collective-permute-start.18 = (f32[24,64,256]{2,1,0:T(8,128)}, f32[24,64,256]{2,1,0:T(8,128)}, u32[]{:S(2)}, u32[]{:S(2)}) collective-permute-start(f32[24,64,256]{2,1,0:T(8,128)} %add.54), channel_id=1, source_target_pairs={{0,32},{32,0},{64,96},{96,64},{1,33},{33,1},{65,97},{97,65},{2,34}... | collective-permute-start | bytes 4718600 | tf_op jit(solution)/shard_map/ppermute | solution.py:314

commit v2 on v1

v2 whole, which is shorter than its diff:
```python
import functools

import jax
import jax.numpy as jnp
import ml_dtypes
import numpy as np
from jax import lax
from jax.experimental import pallas as pl
from jax.experimental.pallas import tpu as pltpu
from jax.sharding import PartitionSpec as P

STEPS = 4
MUTE = 6
G = 8
RADIUS = 4

SECOND = (8064.0, -1008.0, 128.0, -9.0)
SECOND_CENTRE = -14350.0
SECOND_SCALE = 5040.0
FIRST = (672.0, -168.0, 32.0, -3.0)
FIRST_SCALE = 840.0

F32 = jnp.float32
BF16 = jnp.bfloat16


def banded(size, weights, odd):
    matrix = np.zeros((size, size + 2 * RADIUS), np.float32)
    for i in range(size):
        for k, w in enumerate(weights, 1):
            matrix[i, i + RADIUS + k] = w
            matrix[i, i + RADIUS - k] = -w if odd else w
    return matrix


def y_matrices(size):
    both = np.concatenate([banded(size, SECOND, False), banded(size, FIRST, True)])
    own = both[:, RADIUS:-RADIUS]
    result = []
    for tile, parity in ((0, 0), (0, 1), (1, 0), (1, 1)):
        below, above = 8 * (1 - tile) + 4 * parity, 8 * tile + 4 * parity
        halo = np.zeros((2 * size, 16), np.float32)
        halo[:, below : below + 4] = both[:, :RADIUS]
        halo[:, above : above + 4] = both[:, -RADIUS:]
        result.append(np.concatenate([own, own, halo, halo], axis=1))
    return np.stack(result).astype(ml_dtypes.bfloat16)


def z_matrix(size):
    second = banded(size, SECOND, False)[:, RADIUS:-RADIUS].T
    first = banded(size, FIRST, True)[:, RADIUS:-RADIUS].T
    both = np.concatenate([second, first], axis=1)
    return np.concatenate([both, both], axis=0).astype(ml_dtypes.bfloat16)


def parts(value):
    high = value.astype(BF16)
    low = (value - high.astype(F32)).astype(BF16)
    return high, low


def dot(a, b):
    return jnp.dot(a, b, preferred_element_type=F32)


def x_first(window, g):
    total = None
    for k, w in enumerate(FIRST, 1):
        term = w * (window[g + RADIUS + k] - window[g + RADIUS - k])
        total = term if total is None else total + term
    return total


def x_both(window, g):
    second = first = None
    for k in range(1, RADIUS + 1):
        upper, lower = window[g + RADIUS + k], window[g + RADIUS - k]
        s = SECOND[k - 1] * (upper + lower)
        f = FIRST[k - 1] * (upper - lower)
        second = s if second is None else second + s
        first = f if first is None else first + f
    return second, first


def halo_parts(first_ref, second_ref, pair):
    return parts(jnp.concatenate([first_ref[pair], second_ref[pair]], axis=0))


def pack_strips(lowest, highest, odd_tile, first_ref, second_ref, offset):
    rows = lax.broadcasted_iota(jnp.int32, lowest.shape[1:], 0)

    def body(i, carry):
        even, odd = lowest[2 * i], lowest[2 * i + 1]
        low = jnp.where(rows < 4, even, pltpu.roll(odd, 4, 0))
        even, odd = highest[2 * i], highest[2 * i + 1]
        high = jnp.where(rows < 4, pltpu.roll(even, 4, 0), odd)
        first_ref[offset + i] = jnp.where(odd_tile, low, high)
        second_ref[offset + i] = jnp.where(odd_tile, high, low)
        return carry

    lax.fori_loop(0, lowest.shape[0] // 2, body, 0, unroll=4)


def strips_kernel(q, b, corner, xa, xb, ya, yb, rows, sems):
    size_x, size_y, _ = q.shape
    top = size_x - RADIUS
    copies = []
    for i, source in enumerate((q, b)):
        at = RADIUS * i
        copies += [
            (source.at[:, 0:8], rows.at[i, 0]),
            (source.at[:, size_y - 8 : size_y], rows.at[i, 1]),
            (source.at[pl.ds(top * corner[3], RADIUS)], xa.at[at : at + RADIUS]),
            (source.at[pl.ds(top * (1 - corner[3]), RADIUS)], xb.at[at : at + RADIUS]),
        ]
    copies = [pltpu.make_async_copy(*pair, sems.at[n]) for n, pair in enumerate(copies)]
    for copy in copies:
        copy.start()
    for i in range(2):
        copies[4 * i].wait()
        copies[4 * i + 1].wait()
        pack_strips(rows.at[i, 0], rows.at[i, 1], corner[4] == 1, ya, yb, i * (size_x // 2))
    for i in range(2):
        copies[4 * i + 2].wait()
        copies[4 * i + 3].wait()


def fetch_kernel(places, amounts, openness, corner, *refs):
    count = (len(refs) - 3) // 2
    sources, targets = refs[:count], refs[count + 1 : 2 * count + 1]
    out, (weights, sems) = refs[count], refs[2 * count + 1 :]
    copies = [pltpu.make_async_copy(a, b, sems.at[n]) for n, (a, b) in enumerate(zip(sources, targets))]
    for copy in copies:
        copy.start()
    size_x, size_y, lanes = out.shape
    receivers = amounts.shape[1]
    sublane = lax.broadcasted_iota(jnp.int32, (8, receivers), 0)
    at_depth = sublane == places[2]
    spread = [jnp.where(at_depth, amounts[t : t + 1], 0.0) for t in range(STEPS)]
    spread = jnp.concatenate(spread, axis=0)
    high = spread.astype(BF16).astype(F32)
    rest = spread - high
    middle = rest.astype(BF16).astype(F32)
    pieces = [high, middle, rest - middle, jnp.zeros_like(high)]
    weights[...] = jnp.concatenate(pieces, axis=0).T.astype(BF16)
    block = 8
    scale = openness[0, 0].astype(F32)
    lane = lax.broadcasted_iota(jnp.int32, (block * size_y, lanes), 1)
    local_x = places[0] - corner[0]
    rows = lax.broadcasted_iota(jnp.int32, (size_y, receivers), 0)
    at_y = jnp.where(rows == places[1] - corner[1], 1.0, 0.0).astype(BF16)

    def body(i, carry):
        hits = []
        for j in range(block):
            at_x = jnp.where(local_x == i * block + j, 1.0, 0.0).astype(BF16)
            hits.append(at_y * at_x)
        found = dot(jnp.concatenate(hits, axis=0), weights[...])
        found = found + pltpu.roll(found, lanes - 32, 1) + pltpu.roll(found, lanes - 64, 1)
        found = jnp.where(lane < 32, found * scale, 0.0)
        for j in range(block):
            out[i * block + j] = found[j * size_y : (j + 1) * size_y]
        return carry

    lax.fori_loop(0, size_x // block, body, 0)
    for copy in copies:
        copy.wait()


def make_coefficients(base, count, plane, r, ya, yb, ymat, zmat, ys, zs, stiff, buoy, coef, scale):
    size_y = r["size_y"]
    pairs = buoy.shape[0] // 2
    for g in range(count):
        high, low = parts(buoy[base + g])
        if g % 2 == 0:
            hh, hl = halo_parts(ya, yb, pairs + (base + g) // 2)
        ys[g, 0:size_y] = dot(ymat[r["variant"] + g % 2, size_y:], jnp.concatenate([high, low, hh, hl], axis=0))
        zs[g, :, 0:256] = dot(jnp.concatenate([high, low], axis=1), zmat[:, 256:])
    for row in range(0, size_y, 16):
        for lane in range(0, 256, 128):
            at = (slice(row, row + 16), slice(lane, lane + 128))
            window = [plane(j, at) for j in range(count + 2 * RADIUS)]
            for g in range(count):
                s = stiff[(base + g,) + at] * scale
                t = s * (1.0 / (FIRST_SCALE * FIRST_SCALE))
                coef[0][(base + g,) + at] = s * (1.0 / SECOND_SCALE) * window[g + RADIUS]
                coef[1][(base + g,) + at] = t * x_first(window, g)
                coef[2][(base + g,) + at] = t * ys[(g,) + at]
                coef[3][(base + g,) + at] = t * zs[(g,) + at]


def advance(base, count, plane, r, step, q, p, out, ya, yb, ymat, zmat, ys, zs, coef, inject, snap, image, scale):
    size_y = r["size_y"]
    for g in range(count):
        high, low = parts(q[base + g])
        if g % 2 == 0:
            hh, hl = halo_parts(ya, yb, (base + g) // 2)
        ys[g] = dot(ymat[r["variant"] + g % 2], jnp.concatenate([high, low, hh, hl], axis=0))
        zs[g] = dot(jnp.concatenate([high, low], axis=1), zmat[...])
    elementwise(base, count, plane, r, step, q, p, out, ys, zs, coef, inject, snap, image, scale)


def elementwise(base, count, plane, r, step, q, p, out, ys, zs, coef, inject, snap, image, scale):
    size_y = r["size_y"]
    for row in range(0, size_y, 16):
        for lane in range(0, 256, 128):
            at = (slice(row, row + 16), slice(lane, lane + 128))
            below = (slice(size_y + row, size_y + row + 16), slice(lane, lane + 128))
            beside = (slice(row, row + 16), slice(256 + lane, 256 + lane + 128))
            window = [plane(j, at) for j in range(count + 2 * RADIUS)]
            for g in range(count):
                here = (base + g,) + at
                centre = window[g + RADIUS]
                second, first = x_both(window, g)
                second = (second + 3.0 * SECOND_CENTRE * centre) + (ys[(g,) + at] + zs[(g,) + at])
                change = coef[0][here] * second + coef[1][here] * first
                change = change + coef[2][here] * ys[(g,) + below] + coef[3][here] * zs[(g,) + beside]
                kept = (centre + centre) - p[here]
                if step < 2:
                    kept = kept * scale
                if lane == 0:
                    added = pltpu.roll(inject[base + g, row : row + 16, :], (128 - 8 * step) % 128, 1)
                    depth = lax.broadcasted_iota(jnp.int32, (16, 128), 1)
                    kept = kept + jnp.where(depth < 8, added, 0.0)
                value = kept + change
                out[here] = value
                shown = snap[here].astype(F32) * value
                image[here] = shown if step == 0 else image[here] + shown


def mute(image, source, corner, ranges):
    size_y = image.shape[1]
    y = lax.broadcasted_iota(jnp.int32, (size_y, 128), 0) + corner[1] - source[0, 1]
    z = lax.broadcasted_iota(jnp.int32, (size_y, 128), 1) - source[0, 2]
    flat = y * y + z * z
    for dx in range(1 - MUTE, MUTE):
        at = source[0, 0] - corner[0] + dx
        inside = functools.reduce(lambda a, b: a | b, [(at >= lo) & (at < hi) for lo, hi in ranges])

        @pl.when(inside)
        def _():
            image[at, :, 0:128] = jnp.where(flat + dx * dx < MUTE * MUTE, 0.0, image[at, :, 0:128])


def split_image(image, sent, kept, core, ranges):
    (lower, _), (upper, _) = ranges

    def body(i, carry):
        sent[i] = image[jnp.where(core == 0, upper, lower) + i]
        kept[i] = image[jnp.where(core == 0, lower, upper) + i]
        return carry

    lax.fori_loop(0, sent.shape[0], body, 0)


def step_kernel(step, ranges, edges, splits, names, *refs):
    r = dict(zip(names, refs))
    q, corner = r["q"], r["corner"]
    size_x, size_y, _ = q.shape
    r["size_y"] = size_y
    r["variant"] = 2 * corner[4]
    scale = r["openness"][0, 0].astype(F32)
    coef = [r["c%d" % i] for i in range(4)]
    common = (r["ya"], r["yb"], r["ymat"], r["zmat"], r["ys"], r["zs"])
    if "snap_next" in r:
        copy = pltpu.make_async_copy(r["snaps"].at[step + 1], r["snap_next"], r["sem"])
        copy.start()

    def reader(field, base, offset):
        def plane(j, at):
            where = base - RADIUS + j
            if isinstance(where, int) and where < 0:
                return r["halo"][(0, offset + where + RADIUS) + at]
            if isinstance(where, int) and where >= size_x:
                return r["halo"][(1, offset + where - size_x) + at]
            return field[(where,) + at]

        return plane

    def group(base, count):
        if step == 0:
            make_coefficients(
                base, count, reader(r["buoy"], base, RADIUS), r, *common, r["stiff"], r["buoy"], coef, scale
            )
        advance(
            base, count, reader(q, base, 0), r, step, q, r["p"], r["out"], *common, coef, r["inject"], r["snap"],
            r["image"], scale
        )

    for low, high in ranges:
        count = G if (high - low) % G == 0 else 4

        def body(i, carry):
            group(low + i * count, count)
            return carry

        lax.fori_loop(0, (high - low) // count, body, 0)
    if edges:
        r["halo"][corner[3]] = r["xa"][...]
        r["halo"][1 - corner[3]] = r["xb"][...]
        group(0, RADIUS)
        group(size_x - RADIUS, RADIUS)
        ranges = ranges + [(0, RADIUS), (size_x - RADIUS, size_x)]
    if step == STEPS - 1:
        mute(r["image"], r["source"], corner, ranges)
        for n, halves in enumerate(splits):
            split_image(r["image"], r["sent%d" % n], r["kept%d" % n], corner[2], halves)
    elif edges:
        top = size_x - RADIUS
        r["sxa"][...] = r["out"][pl.ds(top * corner[3], RADIUS)]
        r["sxb"][...] = r["out"][pl.ds(top * (1 - corner[3]), RADIUS)]
        pack_strips(r["out"].at[:, 0:8], r["out"].at[:, size_y - 8 :], corner[4] == 1, r["sya"], r["syb"], 0)
    if "snap_next" in r:
        copy.wait()


def add_kernel(a, b, out):
    out[...] = a[...] + b[...]


def gather_kernel(ranges, corner, mine, other, *refs):
    out, sems = refs[-2:]
    core = corner[2]
    (lower, _), (upper, _) = ranges
    copies = []
    for k, (source, first, second) in enumerate(((mine, lower, upper), (other, upper, lower))):
        at = jnp.where(core == 0, first, second)
        copies.append(pltpu.make_async_copy(source, out.at[pl.ds(at, source.shape[0])], sems.at[k]))
    for copy in copies:
        copy.start()
    for copy in copies:
        copy.wait()


def store_kernel(source, out, sem):
    copy = pltpu.make_async_copy(source, out, sem)
    copy.start()
    copy.wait()


VMEM = pl.BlockSpec(memory_space=pltpu.VMEM)
SMEM = pl.BlockSpec(memory_space=pltpu.SMEM)
HBM = pl.BlockSpec(memory_space=pltpu.HBM)


def placed(args, specs):
    return [a if s is SMEM else pltpu.with_memory_space_constraint(a, s.memory_space) for a, s in zip(args, specs)]


def call(kernel, name, args, specs, outs, aliases={}, scratch=(), weight=1):
    outs = [pltpu.VMEM(o, F32) if isinstance(o, tuple) else o for o in outs]
    results = pl.pallas_call(
        kernel,
        name=name,
        in_specs=specs,
        out_specs=[pl.BlockSpec(memory_space=o.memory_space) for o in outs],
        out_shape=outs,
        input_output_aliases=aliases,
        scratch_shapes=list(scratch),
        compiler_params=pltpu.CompilerParams(vmem_limit_bytes=8 << 20),
        cost_estimate=pl.CostEstimate(flops=weight, bytes_accessed=1, transcendentals=0),
    )(*placed(args, specs))
    return list(results)


def exchange(strips):
    sxa, sxb, sya, syb = strips

    def swap(strip, stride, odd):
        tiles = range(lax.axis_size("dom"))
        position = lambda i: i % 4 if stride == 1 else i // 4
        last = 3 if stride == 1 else len(tiles) // 4 - 1
        pairs = [(i, i + stride) for i in tiles if position(i) % 2 == odd and position(i) < last]
        return lax.ppermute(strip, "dom", pairs + [(b, a) for a, b in pairs])

    ya, yb = swap(sya, 1, 0), swap(syb, 1, 1)
    xa, xb = swap(sxa, 4, 1), swap(sxb, 4, 0)
    return xa, xb, ya, yb


def sum_over_shots(sent, kept):
    cores = [(i, i ^ 1) for i in range(4)]
    chips = [(i, i ^ 2) for i in range(4)]
    shape = sent.shape
    (mine,) = call(add_kernel, "add_cores", (kept, lax.ppermute(sent, "shot", cores)), [VMEM] * 2, [shape])
    (mine,) = call(add_kernel, "add_chips", (mine, lax.ppermute(mine, "shot", chips)), [VMEM] * 2, [shape])
    return mine, lax.ppermute(mine, "shot", cores)


def on_device(wave_prev, wave_now, stiffness, buoyancy, snapshots, traces, aperture, receivers, sources):
    index = lax.axis_index("dom")
    size_x, size_y, size_z = grid = buoyancy.shape[1:]
    corner = [index // 4 * size_x, index % 4 * size_y, lax.axis_index("shot") % 2, index // 4 % 2, index % 2]
    corner = jnp.stack(corner).astype(jnp.int32)
    places = receivers[0].T[:, None, :]
    ymat, zmat = jnp.asarray(y_matrices(size_y)), jnp.asarray(z_matrix(size_z))
    snaps = snapshots[0, :, 0]

    strips = call(
        strips_kernel, "strips", (wave_now[0, 0], buoyancy[0], corner), [HBM, HBM, SMEM],
        [(2 * RADIUS, size_y, size_z)] * 2 + [(size_x, 8, size_z)] * 2,
        scratch=[pltpu.VMEM((2, 2, size_x, 8, size_z), F32), pltpu.SemaphoreType.DMA((8,))],
    )
    halos = exchange(strips)
    fetched = [wave_now[0, 0], wave_prev[0, 0], buoyancy[0], stiffness[0], ymat, zmat]
    args = [places, traces[0], aperture, corner] + fetched
    inject, q, p, buoy, stiff, ymat, zmat = call(
        fetch_kernel, "fetch", args, [VMEM, VMEM, SMEM, SMEM] + [HBM] * len(fetched),
        [(size_x, size_y, 128)] + [pltpu.VMEM(a.shape, a.dtype) for a in fetched],
        scratch=[pltpu.VMEM((traces.shape[2], 128), BF16), pltpu.SemaphoreType.DMA((len(fetched),))],
    )

    held = dict(inject=inject, ymat=ymat, zmat=zmat, openness=aperture, source=sources, corner=corner, snaps=snaps)
    held.update(buoy=buoy, stiff=stiff, snap=snapshots[0, 0, 0])
    places_of = dict(openness=SMEM, source=SMEM, corner=SMEM, snaps=HBM)

    def run(step, ranges, edges, started, extra, splits=(), weight=1):
        ahead = not edges and step < STEPS - 1
        ins = ["q", "p", "snap", "inject", "ya", "yb", "ymat", "zmat", "openness", "source", "corner"]
        ins += (["xa", "xb"] if edges else []) + (["snaps"] if ahead else [])
        ins += ["stiff", "buoy"] if step == 0 else ["c0", "c1", "c2", "c3"]
        results = ["out", "image"] + (["c0", "c1", "c2", "c3"] if step == 0 else [])
        given = [n for n in results if n in started]
        extra = dict(extra)
        scratch = dict(
            ys=pltpu.VMEM((G, 2 * size_y, size_z), F32), zs=pltpu.VMEM((G, size_y, 2 * size_z), F32)
        )
        if ahead:
            extra["snap_next"] = pltpu.VMEM(grid, snaps.dtype)
            scratch["sem"] = pltpu.SemaphoreType.DMA
        if edges:
            scratch["halo"] = pltpu.VMEM((2,) + held["xa"].shape, F32)
        names = ins + [n + "_in" for n in given] + results + list(extra) + list(scratch)
        outs = call(
            functools.partial(step_kernel, step, ranges, edges, splits, names), "step%d" % step,
            [held[n] for n in ins + given], [places_of.get(n, VMEM) for n in ins + given],
            [grid] * len(results) + list(extra.values()),
            {len(ins) + i: results.index(n) for i, n in enumerate(given)}, scratch.values(), weight,
        )
        held.update(zip(results, outs))
        return outs[len(results) :]

    inner = [(RADIUS, size_x - RADIUS)]
    strip_x, strip_y = (RADIUS, size_y, size_z), (size_x // 2, 8, size_z)
    first = ("out", "image", "c0", "c1", "c2", "c3")
    held.update(q=q, p=p)
    for step in range(STEPS - 1):
        held.update(zip(("xa", "xb", "ya", "yb"), halos))
        (snap_next,) = run(step, inner, False, ("image",) if step else (), {}, weight=4 << 30)
        extra = dict(sxa=strip_x, sxb=strip_x, sya=strip_y, syb=strip_y)
        halos = exchange(run(step, [], True, first if step == 0 else ("out", "image"), extra))
        held.update(q=held["out"], p=held["q"], snap=snap_next)

    held.update(zip(("xa", "xb", "ya", "yb"), halos))
    kernels = [
        ([(16, 32)], False, [((16, 24), (24, 32))]),
        ([(4, 16), (32, 44)], True, [((8, 16), (32, 40)), ((0, 8), (40, 48))]),
    ]
    gradient = None
    for n, (ranges, edges, splits) in enumerate(kernels):
        halves = {}
        for i, (lower, _) in enumerate(splits):
            half = (lower[1] - lower[0], size_y, size_z)
            halves.update({"sent%d" % i: half, "kept%d" % i: half})
        halves = run(STEPS - 1, ranges, edges, ("out", "image") if n else ("image",), halves, splits)
        for i, ranges in enumerate(splits):
            mine, other = sum_over_shots(*halves[2 * i : 2 * i + 2])
            started = [] if gradient is None else [gradient]
            (gradient,) = call(
                functools.partial(gather_kernel, ranges), "gather", [corner, mine, other] + started,
                [SMEM, VMEM, VMEM] + [HBM] * len(started), [pltpu.HBM(grid, F32)], {3: 0} if started else {},
                [pltpu.SemaphoreType.DMA((2,))],
            )
    (last,) = call(store_kernel, "store", [held["out"]], [VMEM], [pltpu.HBM(grid, F32)], {}, [pltpu.SemaphoreType.DMA])
    return gradient[None], last[None, None]


def solution(mesh):
    return jax.shard_map(
        on_device,
        mesh=mesh,
        in_specs=(
            P("shot", "dom", None, None, None),
            P("shot", "dom", None, None, None),
            P("dom", None, None, None),
            P("dom", None, None, None),
            P("shot", None, "dom", None, None, None),
            P("shot", None, None),
            P("shot", "dom"),
            P("shot", None, None),
            P("shot", None),
        ),
        out_specs=(P("dom", None, None, None), P("shot", "dom", None, None, None)),
        check_vma=False,
    )
```

time: 207 us -> 135 us (0.65)
  local copies, waits for them, and re-layouts: 41.8 us -> 1.63 us
  starting transfers between devices: 64.5 us -> 41.6 us
  other arithmetic: 9.2 us -> 0 us
  Pallas kernels: 47.8 us -> 50.5 us
  waiting for transfers between devices: 40.3 us -> 37.8 us
    unnamed x68 -> x7, local copies, waits for them, and re-layouts: 31.6 us -> 0.02 us
    ppermute x19 -> x25, starting transfers between devices: 64.5 us -> 41.6 us  [the longest x16 29.9 us: swap(): return lax.ppermute(strip, 'dom', pairs + [(b, a) for a, b in pairs])]
    squeeze x1, local copies, waits for them, and re-layouts: 6 us -> 1.51 us  [on_device(): held.update(buoy=buoy, stiff=stiff, snap=snapshots[0, 0, 0])]
    select_n x3 -> x0, other arithmetic: 3.63 us -> none  [the longest x1 2.27 us: sum_over_shots(): low = jnp.where(core == 0, mine, other)]
    add x2 -> x0, other arithmetic: 3.43 us -> none  [the longest x1 2.09 us: sum_over_shots(): mine = kept + lax.ppermute(sent, 'shot', cores)]
    reshape x2 -> x0, local copies, waits for them, and re-layouts: 2.88 us -> none  [on_device(): spread = jnp.repeat(jnp.pad(traces[0].T, ((0, 0), (0, 12))), 8, axis=1)]
    pallas_call x10 -> x20, Pallas kernels: 47.8 us -> 50.5 us  [call(): pl.pallas_call(kernel, name=name, in_specs=specs, out_specs=[pl.BlockSpec...]
    ppermute x19 -> x25, waiting for transfers between devices: 40.3 us -> 37.8 us  [the longest x3 29.9 us: sum_over_shots(): lax.ppermute(mine, 'shot', chips)]
  transfers between devices with their start and end apart: 19 -> 25, of which waited for: 3 -> 10; matrix products, arithmetic and copies ran while one was open for 6% -> 1% of each run, Pallas kernels for 18% -> 30%
where the time goes in v2:
time: 135 us; the launch traced here: 133 us
  Pallas kernels  50.5 us (37%)
  starting transfers between devices  41.6 us (31%)
  waiting for transfers between devices  37.8 us (28%)
  between operations  1.9 us (1%)
  local copies, waits for them, and re-layouts  1.63 us (1%)
    pallas_call x20, Pallas kernels, call(): pl.pallas_call(kernel, name=name, in_specs=specs, out_specs=[pl.BlockSpec...  50.5 us
    ppermute x3, waiting for transfers between devices, sum_over_shots(): lax.ppermute(mine, 'shot', chips)  29.9 us
    ppermute x16, starting transfers between devices, swap(): return lax.ppermute(strip, 'dom', pairs + [(b, a) for a, b in pairs])  29.9 us
    ppermute x16, waiting for transfers between devices, swap(): return lax.ppermute(strip, 'dom', pairs + [(b, a) for a, b in pairs])  6.89 us
    ppermute x3, starting transfers between devices, sum_over_shots(): lax.ppermute(sent, 'shot', cores)  5.86 us
    ppermute x3, starting transfers between devices, sum_over_shots(): return (mine, lax.ppermute(mine, 'shot', cores))  3.8 us
  transfers between devices with their start and end apart: 25, of which 10 were waited for; matrix products, arithmetic and copies ran while one was open for 1% of the time, Pallas kernels for 30%

profile of v2, /device:TPU:57, one launch (start us, length us, event | category | flops | bytes accessed | tf_op | source)
XLA Modules:
  0.0 133.4 jit_solution(16299726342225876811)
XLA Ops:
  0.7 0.1 stack.23.corner.refs_10_
  0.8 2.3 %strips.1 = (f32[8,64,256]{2,1,0:T(8,128)S(1)}, f32[8,64,256]{2,1,0:T(8,128)S(1)}, f32[48,8,256]{2,1,0:T(8,128)S(1)}, f32[48,8,256]{2,1,0:T(8,128)S(1)}) custom-call(f32[48,64,256]{2,1,0:T(8,128)} %bitcast.25, f32[48,64,256]{2,1,0:T(8,128)} %bitcast.27, s32[5]{0:T(128)S(1)} %stack.23.corner.refs_10_), custom_call_target="tpu_custom_call" | custom-call | flops 1 | bytes 1 | tf_op jit(solution)/shard_map/strips/pallas_call | solution.py:352
  3.1 0.0 copy-start.2
  3.1 0.0 copy-start.1
  3.1 0.1 collective-permute-start
  3.2 4.9 %collective-permute-start.1 = (f32[48,8,256]{2,1,0:T(8,128)S(1)}, f32[48,8,256]{2,1,0:T(8,128)S(1)}, u32[]{:S(2)}, u32[]{:S(2)}) collective-permute-start(f32[48,8,256]{2,1,0:T(8,128)S(1)} %get-tuple-element.61), channel_id=1, source_target_pairs={{1,2},{5,6},{9,10},{13,14},{17,18},{21,22},{25,26},{29,30},{2,1},{... | collective-permute-start | bytes 1179656 | tf_op jit(solution)/shard_map/ppermute | solution.py:374
  8.0 5.1 %collective-permute-start.2 = (f32[8,64,256]{2,1,0:T(8,128)S(1)}, f32[8,64,256]{2,1,0:T(8,128)S(1)}, u32[]{:S(2)}, u32[]{:S(2)}) collective-permute-start(f32[8,64,256]{2,1,0:T(8,128)S(1)} %get-tuple-element.64), channel_id=1, source_target_pairs={{4,8},{5,9},{6,10},{7,11},{12,16},{13,17},{14,18},{15,19},{20,24},... | collective-permute-start | bytes 1572872 | tf_op jit(solution)/shard_map/ppermute | solution.py:374
  13.1 0.1 collective-permute-start.3
  13.2 1.5 %slice_bitcast_fusion.refs_2_ = bf16[48,64,256]{2,1,0:T(8,128)(2,1)S(1)} fusion(bf16[1,4,1,48,64,256]{5,4,3,2,1,0:T(8,128)(2,1)} %param.15), kind=kLoop, calls=%fused_computation | loop fusion | bytes 3145728 | tf_op jit(solution)/shard_map/squeeze | solution.py:414
  15.4 0.0 copy-start
  15.4 5.4 %fetch.1 = (f32[48,64,128]{2,1,0:T(8,128)S(1)}, f32[48,64,256]{2,1,0:T(8,128)S(1)}, f32[48,64,256]{2,1,0:T(8,128)S(1)}, f32[48,64,256]{2,1,0:T(8,128)S(1)}, f32[...) custom-call(s32[3,1,1024]{2,1,0:T(1,128)S(1)} %broadcast_in_dim.9.places, ...), custom_call_target="tpu_custom_call" | custom-call | flops 1 | bytes 1 | tf_op jit(solution)/shard_map/fetch/pallas_call | solution.py:352
  20.8 0.0 collective-permute-done.1.refs_5_
  20.8 9.5 %step0.2 = (f32[48,64,256]{2,1,0:T(8,128)S(1)}, f32[48,64,256]{2,1,0:T(8,128)S(1)}, f32[48,64,256]{2,1,0:T(8,128)S(1)}, f32[48,64,256]{2,1,0:T(8,128)S(1)}, f32[...) custom-call(f32[48,64,256]{2,1,0:T(8,128)S(1)} %get-tuple-element.57.refs_0_.refs_1_, ...), custom_call_target="tpu_custom_call" | custom-call | flops 4294967296 | bytes 1 | tf_op jit(solution)/shard_map/step0/pallas_call | solution.py:352
  30.4 2.6 %step0.3 = (f32[48,64,256]{2,1,0:T(8,128)S(1)}, f32[48,64,256]{2,1,0:T(8,128)S(1)}, f32[48,64,256]{2,1,0:T(8,128)S(1)}, f32[48,64,256]{2,1,0:T(8,128)S(1)}, f32[...) custom-call(f32[48,64,256]{2,1,0:T(8,128)S(1)} %get-tuple-element.57, ...), custom_call_target="tpu_custom_call", output_to_operand_aliasing={{0}: (15, {}), {1}: (16, {}), {2}: (17, {}), {3}: (18, {}),... | custom-call | flops 1 | bytes 1 | tf_op jit(solution)/shard_map/step0/pallas_call | solution.py:352
  32.9 0.1 collective-permute-start.4
  33.0 1.9 %collective-permute-start.5 = (f32[24,8,256]{2,1,0:T(8,128)S(1)}, f32[24,8,256]{2,1,0:T(8,128)S(1)}, u32[]{:S(2)}, u32[]{:S(2)}) collective-permute-start(f32[24,8,256]{2,1,0:T(8,128)S(1)} %get-tuple-element.77), channel_id=1, source_target_pairs={{1,2},{5,6},{9,10},{13,14},{17,18},{21,22},{25,26},{29,30},{2,1},{... | collective-permute-start | bytes 589832 | tf_op jit(solution)/shard_map/ppermute | solution.py:374
  35.0 3.8 %collective-permute-start.6 = (f32[4,64,256]{2,1,0:T(8,128)S(1)}, f32[4,64,256]{2,1,0:T(8,128)S(1)}, u32[]{:S(2)}, u32[]{:S(2)}) collective-permute-start(f32[4,64,256]{2,1,0:T(8,128)S(1)} %get-tuple-element.78), channel_id=1, source_target_pairs={{4,8},{5,9},{6,10},{7,11},{12,16},{13,17},{14,18},{15,19},{20,24},... | collective-permute-start | bytes 786440 | tf_op jit(solution)/shard_map/ppermute | solution.py:374
  38.8 0.1 collective-permute-start.7
  38.9 0.9 collective-permute-done.5.refs_5_
  39.8 5.9 %step1.2 = (f32[48,64,256]{2,1,0:T(8,128)S(1)}, f32[48,64,256]{2,1,0:T(8,128)S(1)}, bf16[48,64,256]{2,1,0:T(8,128)(2,1)S(1)}) custom-call(f32[48,64,256]{2,1,0:T(8,128)S(1)} %get-tuple-element.74.refs_0_.refs_1_, f32[48,64,256]{2,1,0:T(8,128)S(1)} %get-tuple-element.57.refs_0_.refs_1_, ...), custom_call_target="tpu_custom_call", output_to_operand_aliasing={{1}: (16, {})} | custom-call | flops 4294967296 | bytes 1 | tf_op jit(solution)/shard_map/step1/pallas_call | solution.py:352
  45.7 1.1 collective-permute-done.6.refs_11_
  46.7 1.8 %step1.3 = (f32[48,64,256]{2,1,0:T(8,128)S(1)}, f32[48,64,256]{2,1,0:T(8,128)S(1)}, f32[4,64,256]{2,1,0:T(8,128)S(1)}, f32[4,64,256]{2,1,0:T(8,128)S(1)}, f32[24...) custom-call(f32[48,64,256]{2,1,0:T(8,128)S(1)} %get-tuple-element.74.refs_0_.refs_1, ...), custom_call_target="tpu_custom_call", output_to_operand_aliasing={{0}: (17, {}), {1}: (18, {})} | custom-call | flops 1 | bytes 1 | tf_op jit(solution)/shard_map/step1/pallas_call | solution.py:352
  48.5 0.1 collective-permute-start.8
  48.6 3.1 %collective-permute-start.9 = (f32[24,8,256]{2,1,0:T(8,128)S(1)}, f32[24,8,256]{2,1,0:T(8,128)S(1)}, u32[]{:S(2)}, u32[]{:S(2)}) collective-permute-start(f32[24,8,256]{2,1,0:T(8,128)S(1)} %get-tuple-element.90), channel_id=1, source_target_pairs={{1,2},{5,6},{9,10},{13,14},{17,18},{21,22},{25,26},{29,30},{2,1},{... | collective-permute-start | bytes 589832 | tf_op jit(solution)/shard_map/ppermute | solution.py:374
  51.7 3.8 %collective-permute-start.10 = (f32[4,64,256]{2,1,0:T(8,128)S(1)}, f32[4,64,256]{2,1,0:T(8,128)S(1)}, u32[]{:S(2)}, u32[]{:S(2)}) collective-permute-start(f32[4,64,256]{2,1,0:T(8,128)S(1)} %get-tuple-element.91), channel_id=1, source_target_pairs={{4,8},{5,9},{6,10},{7,11},{12,16},{13,17},{14,18},{15,19},{20,24},... | collective-permute-start | bytes 786440 | tf_op jit(solution)/shard_map/ppermute | solution.py:374
  55.5 0.1 collective-permute-start.11
  55.6 0.0 collective-permute-done.8.refs_4_
  55.7 5.9 %step2.2 = (f32[48,64,256]{2,1,0:T(8,128)S(1)}, f32[48,64,256]{2,1,0:T(8,128)S(1)}, bf16[48,64,256]{2,1,0:T(8,128)(2,1)S(1)}) custom-call(f32[48,64,256]{2,1,0:T(8,128)S(1)} %get-tuple-element.87.refs_0_.refs_1_, f32[48,64,256]{2,1,0:T(8,128)S(1)} %get-tuple-element.74.refs_0_.refs_1_, ...), custom_call_target="tpu_custom_call", output_to_operand_aliasing={{1}: (16, {})} | custom-call | flops 4294967296 | bytes 1 | tf_op jit(solution)/shard_map/step2/pallas_call | solution.py:352
  61.6 0.9 collective-permute-done.10.refs_11_
  62.4 1.7 %step2.3 = (f32[48,64,256]{2,1,0:T(8,128)S(1)}, f32[48,64,256]{2,1,0:T(8,128)S(1)}, f32[4,64,256]{2,1,0:T(8,128)S(1)}, f32[4,64,256]{2,1,0:T(8,128)S(1)}, f32[24...) custom-call(f32[48,64,256]{2,1,0:T(8,128)S(1)} %get-tuple-element.87.refs_0_.refs_1, ...), custom_call_target="tpu_custom_call", output_to_operand_aliasing={{0}: (17, {}), {1}: (18, {})} | custom-call | flops 1 | bytes 1 | tf_op jit(solution)/shard_map/step2/pallas_call | solution.py:352
  64.2 4.2 %collective-permute-start.14 = (f32[4,64,256]{2,1,0:T(8,128)S(1)}, f32[4,64,256]{2,1,0:T(8,128)S(1)}, u32[]{:S(2)}, u32[]{:S(2)}) collective-permute-start(f32[4,64,256]{2,1,0:T(8,128)S(1)} %get-tuple-element.100), channel_id=1, source_target_pairs={{4,8},{5,9},{6,10},{7,11},{12,16},{13,17},{14,18},{15,19},{20,24},... | collective-permute-start | bytes 786440 | tf_op jit(solution)/shard_map/ppermute | solution.py:374
  68.4 0.1 collective-permute-start.15
  68.5 0.1 collective-permute-start.12
  68.6 2.4 %collective-permute-start.13 = (f32[24,8,256]{2,1,0:T(8,128)S(1)}, f32[24,8,256]{2,1,0:T(8,128)S(1)}, u32[]{:S(2)}, u32[]{:S(2)}) collective-permute-start(f32[24,8,256]{2,1,0:T(8,128)S(1)} %get-tuple-element.99), channel_id=1, source_target_pairs={{1,2},{5,6},{9,10},{13,14},{17,18},{21,22},{25,26},{29,30},{2,1},{... | collective-permute-start | bytes 589832 | tf_op jit(solution)/shard_map/ppermute | solution.py:374
  71.0 2.1 %collective-permute-done.12.refs_4_ = f32[24,8,256]{2,1,0:T(8,128)S(1)} collective-permute-done((f32[24,8,256]{2,1,0:T(8,128)S(1)}, f32[24,8,256]{2,1,0:T(8,128)S(1)}, u32[]{:S(2)}, u32[]{:S(2)}) %collective-permute-start.12) | collective-permute-done | bytes 196640 | tf_op jit(solution)/shard_map/ppermute | solution.py:374
  73.1 1.9 %collective-permute-done.13.refs_5_ = f32[24,8,256]{2,1,0:T(8,128)S(1)} collective-permute-done((f32[24,8,256]{2,1,0:T(8,128)S(1)}, f32[24,8,256]{2,1,0:T(8,128)S(1)}, u32[]{:S(2)}, u32[]{:S(2)}) %collective-permute-start.13) | collective-permute-done | bytes 196640 | tf_op jit(solution)/shard_map/ppermute | solution.py:374
  75.0 2.9 %step3.2 = (f32[48,64,256]{2,1,0:T(8,128)S(1)}, f32[48,64,256]{2,1,0:T(8,128)S(1)}, f32[8,64,256]{2,1,0:T(8,128)S(1)}, f32[8,64,256]{2,1,0:T(8,128)S(1)}) custom-call(f32[48,64,256]{2,1,0:T(8,128)S(1)} %get-tuple-element.96.refs_0_, f32[48,64,256]{2,1,0:T(8,128)S(1)} %get-tuple-element.87.refs_0_.refs_1_, ...), custom_call_target="tpu_custom_call", output_to_operand_aliasing={{1}: (15, {})} | custom-call | flops 1 | bytes 1 | tf_op jit(solution)/shard_map/step3/pallas_call | solution.py:352
  77.9 5.3 %collective-permute-start.22 = (f32[8,64,256]{2,1,0:T(8,128)S(1)}, f32[8,64,256]{2,1,0:T(8,128)S(1)}, u32[]{:S(2)}, u32[]{:S(2)}) collective-permute-start(f32[8,64,256]{2,1,0:T(8,128)S(1)} %get-tuple-element.110), channel_id=1, source_target_pairs={{0,32},{32,0},{64,96},{96,64},{1,33},{33,1},{65,97},{97,65},{2,34}... | collective-permute-start | bytes 1572872 | tf_op jit(solution)/shard_map/ppermute | solution.py:385
  83.2 0.0 collective-permute-done.14.refs_11_
  83.2 0.0 collective-permute-done.15.refs_12_
  83.2 6.0 %step3.3 = (f32[48,64,256]{2,1,0:T(8,128)S(1)}, f32[48,64,256]{2,1,0:T(8,128)S(1)}, f32[8,64,256]{2,1,0:T(8,128)S(1)}, f32[8,64,256]{2,1,0:T(8,128)S(1)}, f32[8,...) custom-call(f32[48,64,256]{2,1,0:T(8,128)S(1)} %get-tuple-element.96.refs_0_, ...), custom_call_target="tpu_custom_call", output_to_operand_aliasing={{0}: (17, {}), {1}: (18, {})} | custom-call | flops 1 | bytes 1 | tf_op jit(solution)/shard_map/step3/pallas_call | solution.py:352
  89.2 0.1 collective-permute-start.19
  89.3 0.5 collective-permute-start.16
  89.8 0.1 add_cores.5.a
  89.9 0.6 collective-permute-start.23
  90.4 0.8 collective-permute-done.19.b
  91.2 0.1 add_cores.4.a
  91.3 0.5 collective-permute-start.20
  91.8 0.1 collective-permute-done.16.b
  91.9 0.1 add_cores.3.a
  92.0 0.9 collective-permute-start.17
  93.0 10.5 %collective-permute-done.23.b = f32[8,64,256]{2,1,0:T(8,128)S(1)} collective-permute-done((f32[8,64,256]{2,1,0:T(8,128)S(1)}, f32[8,64,256]{2,1,0:T(8,128)S(1)}, u32[]{:S(2)}, u32[]{:S(2)}) %collective-permute-start.23) | collective-permute-done | bytes 524320 | tf_op jit(solution)/shard_map/ppermute | solution.py:386
  103.4 0.1 add_chips.5.mine
  103.5 1.4 %collective-permute-start.24 = (f32[8,64,256]{2,1,0:T(8,128)S(1)}, f32[8,64,256]{2,1,0:T(8,128)S(1)}, u32[]{:S(2)}, u32[]{:S(2)}) collective-permute-start(f32[8,64,256]{2,1,0:T(8,128)S(1)} %add_chips.5.mine), channel_id=1, source_target_pairs={{0,32},{32,0},{64,96},{96,64},{1,33},{33,1},{65,97},{97,65},{2,34}... | collective-permute-start | bytes 1572872 | tf_op jit(solution)/shard_map/ppermute | solution.py:387
  104.9 9.8 %collective-permute-done.20.b = f32[8,64,256]{2,1,0:T(8,128)S(1)} collective-permute-done((f32[8,64,256]{2,1,0:T(8,128)S(1)}, f32[8,64,256]{2,1,0:T(8,128)S(1)}, u32[]{:S(2)}, u32[]{:S(2)}) %collective-permute-start.20) | collective-permute-done | bytes 524320 | tf_op jit(solution)/shard_map/ppermute | solution.py:386
  114.7 0.1 add_chips.4.mine
  114.7 1.4 %collective-permute-start.21 = (f32[8,64,256]{2,1,0:T(8,128)S(1)}, f32[8,64,256]{2,1,0:T(8,128)S(1)}, u32[]{:S(2)}, u32[]{:S(2)}) collective-permute-start(f32[8,64,256]{2,1,0:T(8,128)S(1)} %add_chips.4.mine), channel_id=1, source_target_pairs={{0,32},{32,0},{64,96},{96,64},{1,33},{33,1},{65,97},{97,65},{2,34}... | collective-permute-start | bytes 1572872 | tf_op jit(solution)/shard_map/ppermute | solution.py:387
  116.1 9.7 %collective-permute-done.17.b = f32[8,64,256]{2,1,0:T(8,128)S(1)} collective-permute-done((f32[8,64,256]{2,1,0:T(8,128)S(1)}, f32[8,64,256]{2,1,0:T(8,128)S(1)}, u32[]{:S(2)}, u32[]{:S(2)}) %collective-permute-start.17) | collective-permute-done | bytes 524320 | tf_op jit(solution)/shard_map/ppermute | solution.py:386
  125.9 0.1 add_chips.3.mine
  125.9 1.0 collective-permute-start.18
  126.9 1.7 %store.1 = f32[48,64,256]{2,1,0:T(8,128)} custom-call(f32[48,64,256]{2,1,0:T(8,128)S(1)} %get-tuple-element.111.source), custom_call_target="tpu_custom_call" | custom-call | flops 1 | bytes 1 | tf_op jit(solution)/shard_map/store/pallas_call | solution.py:352
  128.6 1.5 %gather.3.refs_0_ = f32[48,64,256]{2,1,0:T(8,128)} custom-call(s32[5]{0:T(128)S(1)} %stack.23.corner.refs_10_, f32[8,64,256]{2,1,0:T(8,128)S(1)} %add_chips.5.mine, f32[8,64,256]{2,1,0:T(8,128)S(1)} %collective-permute-done.24.other), custom_call_target="tpu_custom_call" | custom-call | flops 1 | bytes 1 | tf_op jit(solution)/shard_map/gather/pallas_call | solution.py:352
  130.1 1.5 %gather.4.refs_0_ = f32[48,64,256]{2,1,0:T(8,128)} custom-call(s32[5]{0:T(128)S(1)} %stack.23.corner.refs_10_, f32[8,64,256]{2,1,0:T(8,128)S(1)} %add_chips.4.mine, f32[8,64,256]{2,1,0:T(8,128)S(1)} %collective-permute-done.21.other, f32[48,64,256]{2,1,0:T(8,128)} %gather.3.refs_0_), custom_call_target="tpu_custom_call", output_to_operand_aliasing={{}: (3, {})} | custom-call | flops 1 | bytes 1 | tf_op jit(solution)/shard_map/gather/pallas_call | solution.py:352
  131.7 1.5 %gather.5 = f32[48,64,256]{2,1,0:T(8,128)} custom-call(s32[5]{0:T(128)S(1)} %stack.23.corner.refs_10_, f32[8,64,256]{2,1,0:T(8,128)S(1)} %add_chips.3.mine, f32[8,64,256]{2,1,0:T(8,128)S(1)} %collective-permute-done.18.other, f32[48,64,256]{2,1,0:T(8,128)} %gather.4.refs_0_), custom_call_target="tpu_custom_call", output_to_operand_aliasing={{}: (3, {})} | custom-call | flops 1 | bytes 1 | tf_op jit(solution)/shard_map/gather/pallas_call | solution.py:352
  (16 shorter events, 0.1 us)
Async XLA Ops:
  3.1 12.3 %copy-start.2 = (s32[1,1024,3]{1,0,2:T(1,128)S(1)}, s32[1,1024,3]{1,0,2:T(1,128)}, u32[]{:S(2)}) copy-start(s32[1,1024,3]{1,0,2:T(1,128)} %param.18) | copy-start | bytes 36868
  3.1 12.3 %copy-start.1 = (f32[1,4,1024]{2,1,0:T(4,128)S(1)}, f32[1,4,1024]{2,1,0:T(4,128)}, u32[]{:S(2)}) copy-start(f32[1,4,1024]{2,1,0:T(4,128)} %param.16) | copy-start | bytes 49156
  3.1 17.7 %collective-permute-start = (f32[48,8,256]{2,1,0:T(8,128)S(1)}, f32[48,8,256]{2,1,0:T(8,128)S(1)}, u32[]{:S(2)}, u32[]{:S(2)}) collective-permute-start(f32[48,8,256]{2,1,0:T(8,128)S(1)} %get-tuple-element.60), channel_id=1, source_target_pairs={{0,1},{2,3},{4,5},{6,7},{8,9},{10,11},{12,13},{14,15},{16,17},{18,... | collective-permute-start | bytes 1179656 | tf_op jit(solution)/shard_map/ppermute | solution.py:374
  3.2 17.7 %collective-permute-start.1 = (f32[48,8,256]{2,1,0:T(8,128)S(1)}, f32[48,8,256]{2,1,0:T(8,128)S(1)}, u32[]{:S(2)}, u32[]{:S(2)}) collective-permute-start(f32[48,8,256]{2,1,0:T(8,128)S(1)} %get-tuple-element.61), channel_id=1, source_target_pairs={{1,2},{5,6},{9,10},{13,14},{17,18},{21,22},{25,26},{29,30},{2,1},{... | collective-permute-start | bytes 1179656 | tf_op jit(solution)/shard_map/ppermute | solution.py:374
  8.0 22.3 %collective-permute-start.2 = (f32[8,64,256]{2,1,0:T(8,128)S(1)}, f32[8,64,256]{2,1,0:T(8,128)S(1)}, u32[]{:S(2)}, u32[]{:S(2)}) collective-permute-start(f32[8,64,256]{2,1,0:T(8,128)S(1)} %get-tuple-element.64), channel_id=1, source_target_pairs={{4,8},{5,9},{6,10},{7,11},{12,16},{13,17},{14,18},{15,19},{20,24},... | collective-permute-start | bytes 1572872 | tf_op jit(solution)/shard_map/ppermute | solution.py:374
  13.1 17.3 %collective-permute-start.3 = (f32[8,64,256]{2,1,0:T(8,128)S(1)}, f32[8,64,256]{2,1,0:T(8,128)S(1)}, u32[]{:S(2)}, u32[]{:S(2)}) collective-permute-start(f32[8,64,256]{2,1,0:T(8,128)S(1)} %get-tuple-element.65), channel_id=1, source_target_pairs={{0,4},{1,5},{2,6},{3,7},{8,12},{9,13},{10,14},{11,15},{16,20},{17,... | collective-permute-start | bytes 1572872 | tf_op jit(solution)/shard_map/ppermute | solution.py:374
  15.4 5.4 %copy-start = (s32[1,3]{1,0:T(1,128)S(1)}, s32[1,3]{1,0:T(1,128)}, u32[]{:S(2)}) copy-start(s32[1,3]{1,0:T(1,128)} %refs_9_.15) | copy-start | bytes 40
  32.9 6.0 %collective-permute-start.4 = (f32[24,8,256]{2,1,0:T(8,128)S(1)}, f32[24,8,256]{2,1,0:T(8,128)S(1)}, u32[]{:S(2)}, u32[]{:S(2)}) collective-permute-start(f32[24,8,256]{2,1,0:T(8,128)S(1)} %get-tuple-element.76), channel_id=1, source_target_pairs={{0,1},{2,3},{4,5},{6,7},{8,9},{10,11},{12,13},{14,15},{16,17},{18,... | collective-permute-start | bytes 589832 | tf_op jit(solution)/shard_map/ppermute | solution.py:374
  33.0 6.8 %collective-permute-start.5 = (f32[24,8,256]{2,1,0:T(8,128)S(1)}, f32[24,8,256]{2,1,0:T(8,128)S(1)}, u32[]{:S(2)}, u32[]{:S(2)}) collective-permute-start(f32[24,8,256]{2,1,0:T(8,128)S(1)} %get-tuple-element.77), channel_id=1, source_target_pairs={{1,2},{5,6},{9,10},{13,14},{17,18},{21,22},{25,26},{29,30},{2,1},{... | collective-permute-start | bytes 589832 | tf_op jit(solution)/shard_map/ppermute | solution.py:374
  35.0 11.8 %collective-permute-start.6 = (f32[4,64,256]{2,1,0:T(8,128)S(1)}, f32[4,64,256]{2,1,0:T(8,128)S(1)}, u32[]{:S(2)}, u32[]{:S(2)}) collective-permute-start(f32[4,64,256]{2,1,0:T(8,128)S(1)} %get-tuple-element.78), channel_id=1, source_target_pairs={{4,8},{5,9},{6,10},{7,11},{12,16},{13,17},{14,18},{15,19},{20,24},... | collective-permute-start | bytes 786440 | tf_op jit(solution)/shard_map/ppermute | solution.py:374
  38.8 7.9 %collective-permute-start.7 = (f32[4,64,256]{2,1,0:T(8,128)S(1)}, f32[4,64,256]{2,1,0:T(8,128)S(1)}, u32[]{:S(2)}, u32[]{:S(2)}) collective-permute-start(f32[4,64,256]{2,1,0:T(8,128)S(1)} %get-tuple-element.79), channel_id=1, source_target_pairs={{0,4},{1,5},{2,6},{3,7},{8,12},{9,13},{10,14},{11,15},{16,20},{17,... | collective-permute-start | bytes 786440 | tf_op jit(solution)/shard_map/ppermute | solution.py:374
  48.5 7.1 %collective-permute-start.8 = (f32[24,8,256]{2,1,0:T(8,128)S(1)}, f32[24,8,256]{2,1,0:T(8,128)S(1)}, u32[]{:S(2)}, u32[]{:S(2)}) collective-permute-start(f32[24,8,256]{2,1,0:T(8,128)S(1)} %get-tuple-element.89), channel_id=1, source_target_pairs={{0,1},{2,3},{4,5},{6,7},{8,9},{10,11},{12,13},{14,15},{16,17},{18,... | collective-permute-start | bytes 589832 | tf_op jit(solution)/shard_map/ppermute | solution.py:374
  48.6 7.0 %collective-permute-start.9 = (f32[24,8,256]{2,1,0:T(8,128)S(1)}, f32[24,8,256]{2,1,0:T(8,128)S(1)}, u32[]{:S(2)}, u32[]{:S(2)}) collective-permute-start(f32[24,8,256]{2,1,0:T(8,128)S(1)} %get-tuple-element.90), channel_id=1, source_target_pairs={{1,2},{5,6},{9,10},{13,14},{17,18},{21,22},{25,26},{29,30},{2,1},{... | collective-permute-start | bytes 589832 | tf_op jit(solution)/shard_map/ppermute | solution.py:374
  51.7 10.7 %collective-permute-start.10 = (f32[4,64,256]{2,1,0:T(8,128)S(1)}, f32[4,64,256]{2,1,0:T(8,128)S(1)}, u32[]{:S(2)}, u32[]{:S(2)}) collective-permute-start(f32[4,64,256]{2,1,0:T(8,128)S(1)} %get-tuple-element.91), channel_id=1, source_target_pairs={{4,8},{5,9},{6,10},{7,11},{12,16},{13,17},{14,18},{15,19},{20,24},... | collective-permute-start | bytes 786440 | tf_op jit(solution)/shard_map/ppermute | solution.py:374
  55.5 6.9 %collective-permute-start.11 = (f32[4,64,256]{2,1,0:T(8,128)S(1)}, f32[4,64,256]{2,1,0:T(8,128)S(1)}, u32[]{:S(2)}, u32[]{:S(2)}) collective-permute-start(f32[4,64,256]{2,1,0:T(8,128)S(1)} %get-tuple-element.92), channel_id=1, source_target_pairs={{0,4},{1,5},{2,6},{3,7},{8,12},{9,13},{10,14},{11,15},{16,20},{17,... | collective-permute-start | bytes 786440 | tf_op jit(solution)/shard_map/ppermute | solution.py:374
  64.2 19.0 %collective-permute-start.14 = (f32[4,64,256]{2,1,0:T(8,128)S(1)}, f32[4,64,256]{2,1,0:T(8,128)S(1)}, u32[]{:S(2)}, u32[]{:S(2)}) collective-permute-start(f32[4,64,256]{2,1,0:T(8,128)S(1)} %get-tuple-element.100), channel_id=1, source_target_pairs={{4,8},{5,9},{6,10},{7,11},{12,16},{13,17},{14,18},{15,19},{20,24},... | collective-permute-start | bytes 786440 | tf_op jit(solution)/shard_map/ppermute | solution.py:374
  68.4 14.8 %collective-permute-start.15 = (f32[4,64,256]{2,1,0:T(8,128)S(1)}, f32[4,64,256]{2,1,0:T(8,128)S(1)}, u32[]{:S(2)}, u32[]{:S(2)}) collective-permute-start(f32[4,64,256]{2,1,0:T(8,128)S(1)} %get-tuple-element.101), channel_id=1, source_target_pairs={{0,4},{1,5},{2,6},{3,7},{8,12},{9,13},{10,14},{11,15},{16,20},{17,... | collective-permute-start | bytes 786440 | tf_op jit(solution)/shard_map/ppermute | solution.py:374
  68.5 4.6 %collective-permute-start.12 = (f32[24,8,256]{2,1,0:T(8,128)S(1)}, f32[24,8,256]{2,1,0:T(8,128)S(1)}, u32[]{:S(2)}, u32[]{:S(2)}) collective-permute-start(f32[24,8,256]{2,1,0:T(8,128)S(1)} %get-tuple-element.98), channel_id=1, source_target_pairs={{0,1},{2,3},{4,5},{6,7},{8,9},{10,11},{12,13},{14,15},{16,17},{18,... | collective-permute-start | bytes 589832 | tf_op jit(solution)/shard_map/ppermute | solution.py:374
  68.6 6.4 %collective-permute-start.13 = (f32[24,8,256]{2,1,0:T(8,128)S(1)}, f32[24,8,256]{2,1,0:T(8,128)S(1)}, u32[]{:S(2)}, u32[]{:S(2)}) collective-permute-start(f32[24,8,256]{2,1,0:T(8,128)S(1)} %get-tuple-element.99), channel_id=1, source_target_pairs={{1,2},{5,6},{9,10},{13,14},{17,18},{21,22},{25,26},{29,30},{2,1},{... | collective-permute-start | bytes 589832 | tf_op jit(solution)/shard_map/ppermute | solution.py:374
  77.9 11.9 %collective-permute-start.22 = (f32[8,64,256]{2,1,0:T(8,128)S(1)}, f32[8,64,256]{2,1,0:T(8,128)S(1)}, u32[]{:S(2)}, u32[]{:S(2)}) collective-permute-start(f32[8,64,256]{2,1,0:T(8,128)S(1)} %get-tuple-element.110), channel_id=1, source_target_pairs={{0,32},{32,0},{64,96},{96,64},{1,33},{33,1},{65,97},{97,65},{2,34}... | collective-permute-start | bytes 1572872 | tf_op jit(solution)/shard_map/ppermute | solution.py:385
  89.2 2.0 %collective-permute-start.19 = (f32[8,64,256]{2,1,0:T(8,128)S(1)}, f32[8,64,256]{2,1,0:T(8,128)S(1)}, u32[]{:S(2)}, u32[]{:S(2)}) collective-permute-start(f32[8,64,256]{2,1,0:T(8,128)S(1)} %get-tuple-element.108), channel_id=1, source_target_pairs={{0,32},{32,0},{64,96},{96,64},{1,33},{33,1},{65,97},{97,65},{2,34}... | collective-permute-start | bytes 1572872 | tf_op jit(solution)/shard_map/ppermute | solution.py:385
  89.3 2.6 %collective-permute-start.16 = (f32[8,64,256]{2,1,0:T(8,128)S(1)}, f32[8,64,256]{2,1,0:T(8,128)S(1)}, u32[]{:S(2)}, u32[]{:S(2)}) collective-permute-start(f32[8,64,256]{2,1,0:T(8,128)S(1)} %get-tuple-element.106), channel_id=1, source_target_pairs={{0,32},{32,0},{64,96},{96,64},{1,33},{33,1},{65,97},{97,65},{2,34}... | collective-permute-start | bytes 1572872 | tf_op jit(solution)/shard_map/ppermute | solution.py:385
  89.9 13.6 %collective-permute-start.23 = (f32[8,64,256]{2,1,0:T(8,128)S(1)}, f32[8,64,256]{2,1,0:T(8,128)S(1)}, u32[]{:S(2)}, u32[]{:S(2)}) collective-permute-start(f32[8,64,256]{2,1,0:T(8,128)S(1)} %add_cores.5.a), channel_id=1, source_target_pairs={{0,64},{32,96},{64,0},{96,32},{1,65},{33,97},{65,1},{97,33},{2,66}... | collective-permute-start | bytes 1572872 | tf_op jit(solution)/shard_map/ppermute | solution.py:386
  91.3 23.4 %collective-permute-start.20 = (f32[8,64,256]{2,1,0:T(8,128)S(1)}, f32[8,64,256]{2,1,0:T(8,128)S(1)}, u32[]{:S(2)}, u32[]{:S(2)}) collective-permute-start(f32[8,64,256]{2,1,0:T(8,128)S(1)} %add_cores.4.a), channel_id=1, source_target_pairs={{0,64},{32,96},{64,0},{96,32},{1,65},{33,97},{65,1},{97,33},{2,66}... | collective-permute-start | bytes 1572872 | tf_op jit(solution)/shard_map/ppermute | solution.py:386
  92.0 33.9 %collective-permute-start.17 = (f32[8,64,256]{2,1,0:T(8,128)S(1)}, f32[8,64,256]{2,1,0:T(8,128)S(1)}, u32[]{:S(2)}, u32[]{:S(2)}) collective-permute-start(f32[8,64,256]{2,1,0:T(8,128)S(1)} %add_cores.3.a), channel_id=1, source_target_pairs={{0,64},{32,96},{64,0},{96,32},{1,65},{33,97},{65,1},{97,33},{2,66}... | collective-permute-start | bytes 1572872 | tf_op jit(solution)/shard_map/ppermute | solution.py:386
  103.5 25.1 %collective-permute-start.24 = (f32[8,64,256]{2,1,0:T(8,128)S(1)}, f32[8,64,256]{2,1,0:T(8,128)S(1)}, u32[]{:S(2)}, u32[]{:S(2)}) collective-permute-start(f32[8,64,256]{2,1,0:T(8,128)S(1)} %add_chips.5.mine), channel_id=1, source_target_pairs={{0,32},{32,0},{64,96},{96,64},{1,33},{33,1},{65,97},{97,65},{2,34}... | collective-permute-start | bytes 1572872 | tf_op jit(solution)/shard_map/ppermute | solution.py:387
  114.7 15.4 %collective-permute-start.21 = (f32[8,64,256]{2,1,0:T(8,128)S(1)}, f32[8,64,256]{2,1,0:T(8,128)S(1)}, u32[]{:S(2)}, u32[]{:S(2)}) collective-permute-start(f32[8,64,256]{2,1,0:T(8,128)S(1)} %add_chips.4.mine), channel_id=1, source_target_pairs={{0,32},{32,0},{64,96},{96,64},{1,33},{33,1},{65,97},{97,65},{2,34}... | collective-permute-start | bytes 1572872 | tf_op jit(solution)/shard_map/ppermute | solution.py:387
  125.9 5.7 %collective-permute-start.18 = (f32[8,64,256]{2,1,0:T(8,128)S(1)}, f32[8,64,256]{2,1,0:T(8,128)S(1)}, u32[]{:S(2)}, u32[]{:S(2)}) collective-permute-start(f32[8,64,256]{2,1,0:T(8,128)S(1)} %add_chips.3.mine), channel_id=1, source_target_pairs={{0,32},{32,0},{64,96},{96,64},{1,33},{33,1},{65,97},{97,65},{2,34}... | collective-permute-start | bytes 1572872 | tf_op jit(solution)/shard_map/ppermute | solution.py:387

commit v3 on v2

--- a/solution.py
+++ b/solution.py
@@ -15,7 +15,7 @@
 RADIUS = 4
 
 SECOND = (8064.0, -1008.0, 128.0, -9.0)
-SECOND_CENTRE = -14350.0
+SECOND_CENTRE_Y, SECOND_CENTRE_Z = -43008.0, -42.0
 SECOND_SCALE = 5040.0
 FIRST = (672.0, -168.0, 32.0, -3.0)
 FIRST_SCALE = 840.0
@@ -24,9 +24,10 @@
 BF16 = jnp.bfloat16
 
 
-def banded(size, weights, odd):
+def banded(size, weights, odd, centre=0.0):
     matrix = np.zeros((size, size + 2 * RADIUS), np.float32)
     for i in range(size):
+        matrix[i, i + RADIUS] = centre
         for k, w in enumerate(weights, 1):
             matrix[i, i + RADIUS + k] = w
             matrix[i, i + RADIUS - k] = -w if odd else w
@@ -34,7 +35,7 @@
 
 
 def y_matrices(size):
-    both = np.concatenate([banded(size, SECOND, False), banded(size, FIRST, True)])
+    both = np.concatenate([banded(size, SECOND, False, SECOND_CENTRE_Y), banded(size, FIRST, True)])
     own = both[:, RADIUS:-RADIUS]
     result = []
     for tile, parity in ((0, 0), (0, 1), (1, 0), (1, 1)):
@@ -47,7 +48,7 @@
 
 
 def z_matrix(size):
-    second = banded(size, SECOND, False)[:, RADIUS:-RADIUS].T
+    second = banded(size, SECOND, False, SECOND_CENTRE_Z)[:, RADIUS:-RADIUS].T
     first = banded(size, FIRST, True)[:, RADIUS:-RADIUS].T
     both = np.concatenate([second, first], axis=1)
     return np.concatenate([both, both], axis=0).astype(ml_dtypes.bfloat16)
@@ -129,6 +130,7 @@
     count = (len(refs) - 3) // 2
     sources, targets = refs[:count], refs[count + 1 : 2 * count + 1]
     out, (weights, sems) = refs[count], refs[2 * count + 1 :]
+    sources = [a if a.shape == b.shape else a.at[0] for a, b in zip(sources, targets)]
     copies = [pltpu.make_async_copy(a, b, sems.at[n]) for n, (a, b) in enumerate(zip(sources, targets))]
     for copy in copies:
         copy.start()
@@ -170,12 +172,17 @@
 def make_coefficients(base, count, plane, r, ya, yb, ymat, zmat, ys, zs, stiff, buoy, coef, scale):
     size_y = r["size_y"]
     pairs = buoy.shape[0] // 2
+    along_z = []
     for g in range(count):
         high, low = parts(buoy[base + g])
         if g % 2 == 0:
             hh, hl = halo_parts(ya, yb, pairs + (base + g) // 2)
         ys[g, 0:size_y] = dot(ymat[r["variant"] + g % 2, size_y:], jnp.concatenate([high, low, hh, hl], axis=0))
-        zs[g, :, 0:256] = dot(jnp.concatenate([high, low], axis=1), zmat[:, 256:])
+        along_z.append(jnp.concatenate([high, low], axis=1))
+        if len(along_z) == 4:
+            found = dot(jnp.concatenate(along_z, axis=0), zmat[:, 256:])
+            zs[g - 3 : g + 1, :, 0:256] = found.reshape(4, size_y, 256)
+            along_z = []
     for row in range(0, size_y, 16):
         for lane in range(0, 256, 128):
             at = (slice(row, row + 16), slice(lane, lane + 128))
@@ -212,7 +219,7 @@
                 here = (base + g,) + at
                 centre = window[g + RADIUS]
                 second, first = x_both(window, g)
-                second = (second + 3.0 * SECOND_CENTRE * centre) + (ys[(g,) + at] + zs[(g,) + at])
+                second = second + (ys[(g,) + at] + zs[(g,) + at])
                 change = coef[0][here] * second + coef[1][here] * first
                 change = change + coef[2][here] * ys[(g,) + below] + coef[3][here] * zs[(g,) + beside]
                 kept = (centre + centre) - p[here]
@@ -266,6 +273,21 @@
         copy = pltpu.make_async_copy(r["snaps"].at[step + 1], r["snap_next"], r["sem"])
         copy.start()
 
+    def inflow(start, size, n):
+        pairs = ((r["p_far"], r["p"]), (r["stiff_far"], r["stiff"]))
+        at = pl.ds(start, size)
+        return [pltpu.make_async_copy(a.at[at], b.at[at], r["sems"].at[k, n]) for k, (a, b) in enumerate(pairs)]
+
+    arriving = []
+    if "sems" in r:
+        low, high = ranges[0]
+        groups = (high - low) // G
+        for i in range(groups):
+            arriving += inflow(low + i * G, G, i)
+        arriving += inflow(0, RADIUS, groups) + inflow(high, RADIUS, groups + 1)
+        for copy_in in arriving:
+            copy_in.start()
+
     def reader(field, base, offset):
         def plane(j, at):
             where = base - RADIUS + j
@@ -291,10 +313,15 @@
         count = G if (high - low) % G == 0 else 4
 
         def body(i, carry):
+            if arriving:
+                for copy_in in inflow(low + i * count, count, i):
+                    copy_in.wait()
             group(low + i * count, count)
             return carry
 
         lax.fori_loop(0, (high - low) // count, body, 0)
+    for copy_in in arriving[-4:]:
+        copy_in.wait()
     if edges:
         r["halo"][corner[3]] = r["xa"][...]
         r["halo"][1 - corner[3]] = r["xb"][...]
@@ -303,6 +330,7 @@
         ranges = ranges + [(0, RADIUS), (size_x - RADIUS, size_x)]
     if step == STEPS - 1:
         mute(r["image"], r["source"], corner, ranges)
+    if step == STEPS - 1:
         for n, halves in enumerate(splits):
             split_image(r["image"], r["sent%d" % n], r["kept%d" % n], corner[2], halves)
     elif edges:
@@ -314,18 +342,18 @@
         copy.wait()
 
 
-def add_kernel(a, b, out):
-    out[...] = a[...] + b[...]
-
-
-def gather_kernel(ranges, corner, mine, other, *refs):
+def add_kernel(a, b, *rest):
+    rest[-1][...] = a[...] + b[...]
+
+
+def gather_kernel(splits, corner, *refs):
     out, sems = refs[-2:]
     core = corner[2]
-    (lower, _), (upper, _) = ranges
     copies = []
-    for k, (source, first, second) in enumerate(((mine, lower, upper), (other, upper, lower))):
-        at = jnp.where(core == 0, first, second)
-        copies.append(pltpu.make_async_copy(source, out.at[pl.ds(at, source.shape[0])], sems.at[k]))
+    for n, ((lower, _), (upper, _)) in enumerate(splits):
+        for k, (source, first, second) in enumerate(((refs[2 * n], lower, upper), (refs[2 * n + 1], upper, lower))):
+            at = pl.ds(jnp.where(core == 0, first, second), source.shape[0])
+            copies.append(pltpu.make_async_copy(source, out.at[at], sems.at[n, k]))
     for copy in copies:
         copy.start()
     for copy in copies:
@@ -378,13 +406,20 @@
     return xa, xb, ya, yb
 
 
-def sum_over_shots(sent, kept):
-    cores = [(i, i ^ 1) for i in range(4)]
-    chips = [(i, i ^ 2) for i in range(4)]
-    shape = sent.shape
-    (mine,) = call(add_kernel, "add_cores", (kept, lax.ppermute(sent, "shot", cores)), [VMEM] * 2, [shape])
-    (mine,) = call(add_kernel, "add_chips", (mine, lax.ppermute(mine, "shot", chips)), [VMEM] * 2, [shape])
-    return mine, lax.ppermute(mine, "shot", cores)
+CORES = [(i, i ^ 1) for i in range(4)]
+CHIPS = [(i, i ^ 2) for i in range(4)]
+
+
+def add_cores(sent, kept):
+    arrived = lax.ppermute(sent, "shot", CORES)
+    return call(add_kernel, "add_cores", (kept, arrived), [VMEM] * 2, [kept.shape])[0]
+
+
+def add_chips(mine, after):
+    arrived = lax.ppermute(mine, "shot", CHIPS)
+    args, specs = [mine, arrived] + after, [VMEM] * 2 + [HBM] * len(after)
+    (mine,) = call(add_kernel, "add_chips", args, specs, [mine.shape])
+    return mine, lax.ppermute(mine, "shot", CORES)
 
 
 def on_device(wave_prev, wave_now, stiffness, buoyancy, snapshots, traces, aperture, receivers, sources):
@@ -402,24 +437,28 @@
         scratch=[pltpu.VMEM((2, 2, size_x, 8, size_z), F32), pltpu.SemaphoreType.DMA((8,))],
     )
     halos = exchange(strips)
-    fetched = [wave_now[0, 0], wave_prev[0, 0], buoyancy[0], stiffness[0], ymat, zmat]
+    fetched = [wave_now[0, 0], buoyancy[0], ymat, zmat, snaps]
+    shapes = [a.shape for a in fetched[:-1]] + [grid]
     args = [places, traces[0], aperture, corner] + fetched
-    inject, q, p, buoy, stiff, ymat, zmat = call(
+    inject, q, buoy, ymat, zmat, snap = call(
         fetch_kernel, "fetch", args, [VMEM, VMEM, SMEM, SMEM] + [HBM] * len(fetched),
-        [(size_x, size_y, 128)] + [pltpu.VMEM(a.shape, a.dtype) for a in fetched],
+        [(size_x, size_y, 128)] + [pltpu.VMEM(shape, a.dtype) for shape, a in zip(shapes, fetched)],
         scratch=[pltpu.VMEM((traces.shape[2], 128), BF16), pltpu.SemaphoreType.DMA((len(fetched),))],
     )
 
     held = dict(inject=inject, ymat=ymat, zmat=zmat, openness=aperture, source=sources, corner=corner, snaps=snaps)
-    held.update(buoy=buoy, stiff=stiff, snap=snapshots[0, 0, 0])
-    places_of = dict(openness=SMEM, source=SMEM, corner=SMEM, snaps=HBM)
+    held.update(q=q, buoy=buoy, snap=snap, p_far=wave_prev[0, 0], stiff_far=stiffness[0])
+    places_of = dict(openness=SMEM, source=SMEM, corner=SMEM, snaps=HBM, p_far=HBM, stiff_far=HBM)
 
     def run(step, ranges, edges, started, extra, splits=(), weight=1):
         ahead = not edges and step < STEPS - 1
-        ins = ["q", "p", "snap", "inject", "ya", "yb", "ymat", "zmat", "openness", "source", "corner"]
+        fresh = step == 0 and not edges
+        ins = ["q", "snap", "inject", "ya", "yb", "ymat", "zmat", "openness", "source", "corner"]
         ins += (["xa", "xb"] if edges else []) + (["snaps"] if ahead else [])
-        ins += ["stiff", "buoy"] if step == 0 else ["c0", "c1", "c2", "c3"]
-        results = ["out", "image"] + (["c0", "c1", "c2", "c3"] if step == 0 else [])
+        ins += ["p_far", "stiff_far"] if fresh else ["p"]
+        ins += ["buoy"] if step == 0 else ["c0", "c1", "c2", "c3"]
+        ins += ["stiff"] if step == 0 and edges else []
+        results = ["out", "image"] + (["c0", "c1", "c2", "c3"] if step == 0 else []) + (["p", "stiff"] if fresh else [])
         given = [n for n in results if n in started]
         extra = dict(extra)
         scratch = dict(
@@ -428,6 +467,8 @@
         if ahead:
             extra["snap_next"] = pltpu.VMEM(grid, snaps.dtype)
             scratch["sem"] = pltpu.SemaphoreType.DMA
+        if fresh:
+            scratch["sems"] = pltpu.SemaphoreType.DMA((2, size_x // G + 1))
         if edges:
             scratch["halo"] = pltpu.VMEM((2,) + held["xa"].shape, F32)
         names = ins + [n + "_in" for n in given] + results + list(extra) + list(scratch)
@@ -443,7 +484,6 @@
     inner = [(RADIUS, size_x - RADIUS)]
     strip_x, strip_y = (RADIUS, size_y, size_z), (size_x // 2, 8, size_z)
     first = ("out", "image", "c0", "c1", "c2", "c3")
-    held.update(q=q, p=p)
     for step in range(STEPS - 1):
         held.update(zip(("xa", "xb", "ya", "yb"), halos))
         (snap_next,) = run(step, inner, False, ("image",) if step else (), {}, weight=4 << 30)
@@ -452,27 +492,27 @@
         held.update(q=held["out"], p=held["q"], snap=snap_next)
 
     held.update(zip(("xa", "xb", "ya", "yb"), halos))
-    kernels = [
-        ([(16, 32)], False, [((16, 24), (24, 32))]),
-        ([(4, 16), (32, 44)], True, [((8, 16), (32, 40)), ((0, 8), (40, 48))]),
-    ]
-    gradient = None
-    for n, (ranges, edges, splits) in enumerate(kernels):
-        halves = {}
-        for i, (lower, _) in enumerate(splits):
-            half = (lower[1] - lower[0], size_y, size_z)
-            halves.update({"sent%d" % i: half, "kept%d" % i: half})
-        halves = run(STEPS - 1, ranges, edges, ("out", "image") if n else ("image",), halves, splits)
-        for i, ranges in enumerate(splits):
-            mine, other = sum_over_shots(*halves[2 * i : 2 * i + 2])
-            started = [] if gradient is None else [gradient]
-            (gradient,) = call(
-                functools.partial(gather_kernel, ranges), "gather", [corner, mine, other] + started,
-                [SMEM, VMEM, VMEM] + [HBM] * len(started), [pltpu.HBM(grid, F32)], {3: 0} if started else {},
-                [pltpu.SemaphoreType.DMA((2,))],
+    run(STEPS - 1, inner, False, ("image",), {}, weight=4 << 30)
+    splits, halves, at = [], {}, 0
+    for i, size in enumerate((4, 8, 8, 4)):
+        splits.append(((at, at + size), (size_x - at - size, size_x - at)))
+        halves.update({"sent%d" % i: (size, size_y, size_z), "kept%d" % i: (size, size_y, size_z)})
+        at += size
+    halves = run(STEPS - 1, [], True, ("out", "image"), halves, splits)
+    sums = [add_cores(*halves[2 * i : 2 * i + 2]) for i in range(len(splits))]
+    (last,) = call(store_kernel, "store", [held["out"]], [VMEM], [pltpu.HBM(grid, F32)], {}, [pltpu.SemaphoreType.DMA])
+    started, chunks = [], []
+    for n, mine in enumerate(sums):
+        chunks += add_chips(mine, started + [last] if n == 3 else [])
+        if n % 2:
+            ranges = splits[n - 1 : n + 1]
+            started = call(
+                functools.partial(gather_kernel, ranges), "gather", [corner] + chunks + started,
+                [SMEM] + [VMEM] * 4 + [HBM] * len(started), [pltpu.HBM(grid, F32)], {5: 0} if started else {},
+                [pltpu.SemaphoreType.DMA((2, 2))],
             )
-    (last,) = call(store_kernel, "store", [held["out"]], [VMEM], [pltpu.HBM(grid, F32)], {}, [pltpu.SemaphoreType.DMA])
-    return gradient[None], last[None, None]
+            chunks = []
+    return started[0][None], last[None, None]
 
 
 def solution(mesh):

time: 135 us -> 128 us (0.948)
  waiting for transfers between devices: 37.8 us -> 33.3 us
  Pallas kernels: 50.5 us -> 47.3 us
  starting transfers between devices: 41.6 us -> 44.7 us
  local copies, waits for them, and re-layouts: 1.63 us -> 0.12 us
    ppermute x16, waiting for transfers between devices: 6.89 us -> 2.2 us  [swap(): return lax.ppermute(strip, 'dom', pairs + [(b, a) for a, b in pairs])]
    pallas_call x20 -> x21, Pallas kernels: 50.5 us -> 47.3 us  [call(): pl.pallas_call(kernel, name=name, in_specs=specs, out_specs=[pl.BlockSpec...]
    ppermute x9 -> x12, starting transfers between devices: 11.7 us -> 14 us  [the longest x4 6.77 us: add_cores(): arrived = lax.ppermute(sent, 'shot', CORES)]
    squeeze x1 -> x0, local copies, waits for them, and re-layouts: 1.51 us -> none  [on_device(): held.update(buoy=buoy, stiff=stiff, snap=snapshots[0, 0, 0])]
    ppermute x9 -> x12, waiting for transfers between devices: 30.9 us -> 31.1 us  [the longest x4 28.3 us: add_chips(): arrived = lax.ppermute(mine, 'shot', CHIPS)]
  transfers between devices with their start and end apart: 25 -> 28, of which waited for: 10 -> 9; matrix products, arithmetic and copies ran while one was open for 1% -> 0% of each run, Pallas kernels for 30% -> 28%
where the time goes in v3:
time: 128 us; the launch traced here: 127 us
  Pallas kernels  47.3 us (37%)
  starting transfers between devices  44.7 us (35%)
  waiting for transfers between devices  33.3 us (26%)
  between operations  1.88 us (1%)
    pallas_call x21, Pallas kernels, call(): pl.pallas_call(kernel, name=name, in_specs=specs, out_specs=[pl.BlockSpec...  47.3 us
    ppermute x16, starting transfers between devices, swap(): return lax.ppermute(strip, 'dom', pairs + [(b, a) for a, b in pairs])  30.7 us
    ppermute x4, waiting for transfers between devices, add_chips(): arrived = lax.ppermute(mine, 'shot', CHIPS)  28.3 us
    ppermute x4, starting transfers between devices, add_cores(): arrived = lax.ppermute(sent, 'shot', CORES)  6.77 us
    ppermute x4, starting transfers between devices, add_chips(): return (mine, lax.ppermute(mine, 'shot', CORES))  4.75 us
  transfers between devices with their start and end apart: 28, of which 9 were waited for; matrix products, arithmetic and copies ran while one was open for 0% of the time, Pallas kernels for 28%

profile of v3, /device:TPU:57, one launch (start us, length us, event | category | flops | bytes accessed | tf_op | source)
XLA Modules:
  0.0 127.3 jit_solution(14543772983700883673)
XLA Ops:
  0.7 0.1 stack.23.corner.refs_9_
  0.8 2.3 %strips.1 = (f32[8,64,256]{2,1,0:T(8,128)S(1)}, f32[8,64,256]{2,1,0:T(8,128)S(1)}, f32[48,8,256]{2,1,0:T(8,128)S(1)}, f32[48,8,256]{2,1,0:T(8,128)S(1)}) custom-call(f32[48,64,256]{2,1,0:T(8,128)} %bitcast.25, f32[48,64,256]{2,1,0:T(8,128)} %bitcast.27, s32[5]{0:T(128)S(1)} %stack.23.corner.refs_9_), custom_call_target="tpu_custom_call" | custom-call | flops 1 | bytes 1 | tf_op jit(solution)/shard_map/strips/pallas_call | solution.py:380
  3.1 0.1 collective-permute-start
  3.2 4.9 %collective-permute-start.1 = (f32[48,8,256]{2,1,0:T(8,128)S(1)}, f32[48,8,256]{2,1,0:T(8,128)S(1)}, u32[]{:S(2)}, u32[]{:S(2)}) collective-permute-start(f32[48,8,256]{2,1,0:T(8,128)S(1)} %get-tuple-element.64), channel_id=1, source_target_pairs={{1,2},{5,6},{9,10},{13,14},{17,18},{21,22},{25,26},{29,30},{2,1},{... | collective-permute-start | bytes 1179656 | tf_op jit(solution)/shard_map/ppermute | solution.py:402
  8.0 5.1 %collective-permute-start.2 = (f32[8,64,256]{2,1,0:T(8,128)S(1)}, f32[8,64,256]{2,1,0:T(8,128)S(1)}, u32[]{:S(2)}, u32[]{:S(2)}) collective-permute-start(f32[8,64,256]{2,1,0:T(8,128)S(1)} %get-tuple-element.67), channel_id=1, source_target_pairs={{4,8},{5,9},{6,10},{7,11},{12,16},{13,17},{14,18},{15,19},{20,24},... | collective-permute-start | bytes 1572872 | tf_op jit(solution)/shard_map/ppermute | solution.py:402
  13.1 0.1 collective-permute-start.3
  13.9 0.0 copy-start
  13.9 4.1 %fetch.1 = (f32[48,64,128]{2,1,0:T(8,128)S(1)}, f32[48,64,256]{2,1,0:T(8,128)S(1)}, f32[48,64,256]{2,1,0:T(8,128)S(1)}, bf16[4,128,160]{2,1,0:T(8,128)(2,1)S(1)}...) custom-call(s32[3,1,1024]{2,1,0:T(1,128)S(1)} %broadcast_in_dim.9.places, f32[4,1024]{1,0:T(4,128)S(1)} %bitcast.18, ...), custom_call_target="tpu_custom_call" | custom-call | flops 1 | bytes 1 | tf_op jit(solution)/shard_map/fetch/pallas_call | solution.py:380
  18.0 0.0 collective-permute-done.1.refs_4_
  18.0 9.7 %step0.2 = (f32[48,64,256]{2,1,0:T(8,128)S(1)}, f32[48,64,256]{2,1,0:T(8,128)S(1)}, f32[48,64,256]{2,1,0:T(8,128)S(1)}, f32[48,64,256]{2,1,0:T(8,128)S(1)}, f32[...) custom-call(f32[48,64,256]{2,1,0:T(8,128)S(1)} %get-tuple-element.60, ...), custom_call_target="tpu_custom_call" | custom-call | flops 4294967296 | bytes 1 | tf_op jit(solution)/shard_map/step0/pallas_call | solution.py:380
  27.8 0.0 collective-permute-done.3.refs_11_
  27.8 2.4 %step0.3 = (f32[48,64,256]{2,1,0:T(8,128)S(1)}, f32[48,64,256]{2,1,0:T(8,128)S(1)}, f32[48,64,256]{2,1,0:T(8,128)S(1)}, f32[48,64,256]{2,1,0:T(8,128)S(1)}, f32[...) custom-call(f32[48,64,256]{2,1,0:T(8,128)S(1)} %get-tuple-element.60, ...), custom_call_target="tpu_custom_call", output_to_operand_aliasing={{0}: (15, {}), {1}: (16, {}), {2}: (17, {}), {3}: (18, {}),... | custom-call | flops 1 | bytes 1 | tf_op jit(solution)/shard_map/step0/pallas_call | solution.py:380
  30.2 0.1 collective-permute-start.4
  30.3 1.9 %collective-permute-start.5 = (f32[24,8,256]{2,1,0:T(8,128)S(1)}, f32[24,8,256]{2,1,0:T(8,128)S(1)}, u32[]{:S(2)}, u32[]{:S(2)}) collective-permute-start(f32[24,8,256]{2,1,0:T(8,128)S(1)} %get-tuple-element.81), channel_id=1, source_target_pairs={{1,2},{5,6},{9,10},{13,14},{17,18},{21,22},{25,26},{29,30},{2,1},{... | collective-permute-start | bytes 589832 | tf_op jit(solution)/shard_map/ppermute | solution.py:402
  32.2 4.7 %collective-permute-start.6 = (f32[4,64,256]{2,1,0:T(8,128)S(1)}, f32[4,64,256]{2,1,0:T(8,128)S(1)}, u32[]{:S(2)}, u32[]{:S(2)}) collective-permute-start(f32[4,64,256]{2,1,0:T(8,128)S(1)} %get-tuple-element.82), channel_id=1, source_target_pairs={{4,8},{5,9},{6,10},{7,11},{12,16},{13,17},{14,18},{15,19},{20,24},... | collective-permute-start | bytes 786440 | tf_op jit(solution)/shard_map/ppermute | solution.py:402
  36.9 0.1 collective-permute-start.7
  37.0 0.0 collective-permute-done.4.refs_3_
  37.1 0.0 collective-permute-done.5.refs_4_
  37.1 5.7 %step1.2 = (f32[48,64,256]{2,1,0:T(8,128)S(1)}, f32[48,64,256]{2,1,0:T(8,128)S(1)}, bf16[48,64,256]{2,1,0:T(8,128)(2,1)S(1)}) custom-call(f32[48,64,256]{2,1,0:T(8,128)S(1)} %get-tuple-element.78.refs_0_.refs_11_.refs_12_, bf16[48,64,256]{2,1,0:T(8,128)(2,1)S(1)} %get-tuple-element.79.refs_1_, ...), custom_call_target="tpu_custom_call", output_to_operand_aliasing={{1}: (16, {})} | custom-call | flops 4294967296 | bytes 1 | tf_op jit(solution)/shard_map/step1/pallas_call | solution.py:380
  42.8 1.0 collective-permute-done.6.refs_10_
  43.8 0.0 collective-permute-done.7.refs_11_
  43.8 1.7 %step1.3 = (f32[48,64,256]{2,1,0:T(8,128)S(1)}, f32[48,64,256]{2,1,0:T(8,128)S(1)}, f32[4,64,256]{2,1,0:T(8,128)S(1)}, f32[4,64,256]{2,1,0:T(8,128)S(1)}, f32[24...) custom-call(f32[48,64,256]{2,1,0:T(8,128)S(1)} %get-tuple-element.78.refs_0_.refs_1, ...), custom_call_target="tpu_custom_call", output_to_operand_aliasing={{0}: (17, {}), {1}: (18, {})} | custom-call | flops 1 | bytes 1 | tf_op jit(solution)/shard_map/step1/pallas_call | solution.py:380
  45.5 0.3 collective-permute-start.8
  45.8 3.2 %collective-permute-start.9 = (f32[24,8,256]{2,1,0:T(8,128)S(1)}, f32[24,8,256]{2,1,0:T(8,128)S(1)}, u32[]{:S(2)}, u32[]{:S(2)}) collective-permute-start(f32[24,8,256]{2,1,0:T(8,128)S(1)} %get-tuple-element.94), channel_id=1, source_target_pairs={{1,2},{5,6},{9,10},{13,14},{17,18},{21,22},{25,26},{29,30},{2,1},{... | collective-permute-start | bytes 589832 | tf_op jit(solution)/shard_map/ppermute | solution.py:402
  49.0 3.8 %collective-permute-start.10 = (f32[4,64,256]{2,1,0:T(8,128)S(1)}, f32[4,64,256]{2,1,0:T(8,128)S(1)}, u32[]{:S(2)}, u32[]{:S(2)}) collective-permute-start(f32[4,64,256]{2,1,0:T(8,128)S(1)} %get-tuple-element.95), channel_id=1, source_target_pairs={{4,8},{5,9},{6,10},{7,11},{12,16},{13,17},{14,18},{15,19},{20,24},... | collective-permute-start | bytes 786440 | tf_op jit(solution)/shard_map/ppermute | solution.py:402
  52.8 0.1 collective-permute-start.11
  52.9 0.0 collective-permute-done.8.refs_3_
  52.9 0.0 collective-permute-done.9.refs_4_
  52.9 5.9 %step2.2 = (f32[48,64,256]{2,1,0:T(8,128)S(1)}, f32[48,64,256]{2,1,0:T(8,128)S(1)}, bf16[48,64,256]{2,1,0:T(8,128)(2,1)S(1)}) custom-call(f32[48,64,256]{2,1,0:T(8,128)S(1)} %get-tuple-element.91.refs_0_.refs_10_.refs_12_, bf16[48,64,256]{2,1,0:T(8,128)(2,1)S(1)} %get-tuple-element.92.refs_1_, ...), custom_call_target="tpu_custom_call", output_to_operand_aliasing={{1}: (16, {})} | custom-call | flops 4294967296 | bytes 1 | tf_op jit(solution)/shard_map/step2/pallas_call | solution.py:380
  58.8 0.9 collective-permute-done.10.refs_10_
  59.7 1.7 %step2.3 = (f32[48,64,256]{2,1,0:T(8,128)S(1)}, f32[48,64,256]{2,1,0:T(8,128)S(1)}, f32[4,64,256]{2,1,0:T(8,128)S(1)}, f32[4,64,256]{2,1,0:T(8,128)S(1)}, f32[24...) custom-call(f32[48,64,256]{2,1,0:T(8,128)S(1)} %get-tuple-element.91.refs_0_.refs_1, ...), custom_call_target="tpu_custom_call", output_to_operand_aliasing={{0}: (17, {}), {1}: (18, {})} | custom-call | flops 1 | bytes 1 | tf_op jit(solution)/shard_map/step2/pallas_call | solution.py:380
  61.4 0.1 collective-permute-start.12
  61.5 2.1 %collective-permute-start.13 = (f32[24,8,256]{2,1,0:T(8,128)S(1)}, f32[24,8,256]{2,1,0:T(8,128)S(1)}, u32[]{:S(2)}, u32[]{:S(2)}) collective-permute-start(f32[24,8,256]{2,1,0:T(8,128)S(1)} %get-tuple-element.103), channel_id=1, source_target_pairs={{1,2},{5,6},{9,10},{13,14},{17,18},{21,22},{25,26},{29,30},{2,1},{... | collective-permute-start | bytes 589832 | tf_op jit(solution)/shard_map/ppermute | solution.py:402
  63.6 4.2 %collective-permute-start.14 = (f32[4,64,256]{2,1,0:T(8,128)S(1)}, f32[4,64,256]{2,1,0:T(8,128)S(1)}, u32[]{:S(2)}, u32[]{:S(2)}) collective-permute-start(f32[4,64,256]{2,1,0:T(8,128)S(1)} %get-tuple-element.104), channel_id=1, source_target_pairs={{4,8},{5,9},{6,10},{7,11},{12,16},{13,17},{14,18},{15,19},{20,24},... | collective-permute-start | bytes 786440 | tf_op jit(solution)/shard_map/ppermute | solution.py:402
  67.8 0.1 collective-permute-start.15
  67.9 0.0 collective-permute-done.13.refs_4_
  67.9 6.2 %step3.2 = (f32[48,64,256]{2,1,0:T(8,128)S(1)}, f32[48,64,256]{2,1,0:T(8,128)S(1)}) custom-call(f32[48,64,256]{2,1,0:T(8,128)S(1)} %get-tuple-element.100.refs_0_, bf16[48,64,256]{2,1,0:T(8,128)(2,1)S(1)} %get-tuple-element.101.refs_1_, f32[48,64,128]{2,1,0:T(8,128)S(1)} %get-tuple-element.62.refs_2_, ...), custom_call_target="tpu_custom_call", output_to_operand_aliasing={{1}: (15, {})} | custom-call | flops 4294967296 | bytes 1 | tf_op jit(solution)/shard_map/step3/pallas_call | solution.py:380
  74.1 0.2 collective-permute-done.14.refs_10_
  74.4 2.1 %step3.3 = (f32[48,64,256]{2,1,0:T(8,128)S(1)}, f32[48,64,256]{2,1,0:T(8,128)S(1)}, f32[4,64,256]{2,1,0:T(8,128)S(1)}, f32[4,64,256]{2,1,0:T(8,128)S(1)}, f32[8,...) custom-call(f32[48,64,256]{2,1,0:T(8,128)S(1)} %get-tuple-element.10, ...), custom_call_target="tpu_custom_call", output_to_operand_aliasing={{0}: (17, {}), {1}: (18, {})} | custom-call | flops 1 | bytes 1 | tf_op jit(solution)/shard_map/step3/pallas_call | solution.py:380
  76.5 5.9 %collective-permute-start.24 = (f32[8,64,256]{2,1,0:T(8,128)S(1)}, f32[8,64,256]{2,1,0:T(8,128)S(1)}, u32[]{:S(2)}, u32[]{:S(2)}) collective-permute-start(f32[8,64,256]{2,1,0:T(8,128)S(1)} %get-tuple-element.116), channel_id=1, source_target_pairs={{0,32},{32,0},{64,96},{96,64},{1,33},{33,1},{65,97},{97,65},{2,34}... | collective-permute-start | bytes 1572872 | tf_op jit(solution)/shard_map/ppermute | solution.py:414
  82.4 0.1 collective-permute-start.16
  82.5 1.4 %collective-permute-done.24.b = f32[8,64,256]{2,1,0:T(8,128)S(1)} collective-permute-done((f32[8,64,256]{2,1,0:T(8,128)S(1)}, f32[8,64,256]{2,1,0:T(8,128)S(1)}, u32[]{:S(2)}, u32[]{:S(2)}) %collective-permute-start.24) | collective-permute-done | bytes 524320 | tf_op jit(solution)/shard_map/ppermute | solution.py:414
  83.9 0.1 add_cores.7.a
  84.0 0.1 collective-permute-start.25
  84.1 0.5 collective-permute-start.21
  84.5 0.1 collective-permute-done.16.b
  84.7 0.1 add_cores.4.a
  84.7 1.6 %collective-permute-start.17 = (f32[8,64,256]{2,1,0:T(8,128)S(1)}, f32[8,64,256]{2,1,0:T(8,128)S(1)}, u32[]{:S(2)}, u32[]{:S(2)}) collective-permute-start(f32[8,64,256]{2,1,0:T(8,128)S(1)} %add_cores.4.a), channel_id=1, source_target_pairs={{0,64},{32,96},{64,0},{96,32},{1,65},{33,97},{65,1},{97,33},{2,66}... | collective-permute-start | bytes 1572872 | tf_op jit(solution)/shard_map/ppermute | solution.py:419
  86.3 0.3 collective-permute-start.19
  86.7 0.8 collective-permute-start.22
  87.5 9.7 %collective-permute-done.25.b = f32[8,64,256]{2,1,0:T(8,128)S(1)} collective-permute-done((f32[8,64,256]{2,1,0:T(8,128)S(1)}, f32[8,64,256]{2,1,0:T(8,128)S(1)}, u32[]{:S(2)}, u32[]{:S(2)}) %collective-permute-start.25) | collective-permute-done | bytes 524320 | tf_op jit(solution)/shard_map/ppermute | solution.py:419
  97.2 0.1 add_chips.6.refs_2_
  97.3 2.1 %collective-permute-start.26 = (f32[8,64,256]{2,1,0:T(8,128)S(1)}, f32[8,64,256]{2,1,0:T(8,128)S(1)}, u32[]{:S(2)}, u32[]{:S(2)}) collective-permute-start(f32[8,64,256]{2,1,0:T(8,128)S(1)} %add_chips.6.refs_2_), channel_id=1, source_target_pairs={{0,32},{32,0},{64,96},{96,64},{1,33},{33,1},{65,97},{97,65},{2,34}... | collective-permute-start | bytes 1572872 | tf_op jit(solution)/shard_map/ppermute | solution.py:422
  99.4 14.7 %collective-permute-done.22.b = f32[4,64,256]{2,1,0:T(8,128)S(1)} collective-permute-done((f32[4,64,256]{2,1,0:T(8,128)S(1)}, f32[4,64,256]{2,1,0:T(8,128)S(1)}, u32[]{:S(2)}, u32[]{:S(2)}) %collective-permute-start.22) | collective-permute-done | bytes 262176 | tf_op jit(solution)/shard_map/ppermute | solution.py:419
  114.1 1.3 %collective-permute-start.23 = (f32[4,64,256]{2,1,0:T(8,128)S(1)}, f32[4,64,256]{2,1,0:T(8,128)S(1)}, u32[]{:S(2)}, u32[]{:S(2)}) collective-permute-start(f32[4,64,256]{2,1,0:T(8,128)S(1)} %add_chips.5.refs_0_), channel_id=1, source_target_pairs={{0,32},{32,0},{64,96},{96,64},{1,33},{33,1},{65,97},{97,65},{2,34}... | collective-permute-start | bytes 786440 | tf_op jit(solution)/shard_map/ppermute | solution.py:422
  115.4 0.0 collective-permute-start.20
  115.4 0.1 add_chips.4.refs_0_
  115.5 0.4 collective-permute-start.18
  115.9 1.7 %store.1.rest_1_ = f32[48,64,256]{2,1,0:T(8,128)} custom-call(f32[48,64,256]{2,1,0:T(8,128)S(1)} %get-tuple-element.117.source), custom_call_target="tpu_custom_call" | custom-call | flops 1 | bytes 1 | tf_op jit(solution)/shard_map/store/pallas_call | solution.py:380
  117.6 1.7 %gather.2.rest_0_.refs_4_ = f32[48,64,256]{2,1,0:T(8,128)} custom-call(s32[5]{0:T(128)S(1)} %stack.23.corner.refs_9_, f32[4,64,256]{2,1,0:T(8,128)S(1)} %add_chips.5.refs_0_, f32[4,64,256]{2,1,0:T(8,128)S(1)} %collective-permute-done.23.refs_1_, f32[8,64,256]{2,1,0:T(8,128)S(1)} %add_chips.6.refs_2_, f32[8,64,256]{2,1,0:T(8,128)S(1)} %collective-permute-done.26.refs_3_), custom_call_target="tpu_custom_call" | custom-call | flops 1 | bytes 1 | tf_op jit(solution)/shard_map/gather/pallas_call | solution.py:380
  119.3 3.9 %collective-permute-done.20.b = f32[4,64,256]{2,1,0:T(8,128)S(1)} collective-permute-done((f32[4,64,256]{2,1,0:T(8,128)S(1)}, f32[4,64,256]{2,1,0:T(8,128)S(1)}, u32[]{:S(2)}, u32[]{:S(2)}) %collective-permute-start.20) | collective-permute-done | bytes 262176 | tf_op jit(solution)/shard_map/ppermute | solution.py:419
  123.3 1.0 collective-permute-start.27
  124.2 1.2 collective-permute-done.27.refs_3_
  125.4 1.7 %gather.3 = f32[48,64,256]{2,1,0:T(8,128)} custom-call(s32[5]{0:T(128)S(1)} %stack.23.corner.refs_9_, f32[8,64,256]{2,1,0:T(8,128)S(1)} %add_chips.4.refs_0_, f32[8,64,256]{2,1,0:T(8,128)S(1)} %collective-permute-done.18.refs_1_, f32[4,64,256]{2,1,0:T(8,128)S(1)} %add_chips.7.refs_2_, ...), custom_call_target="tpu_custom_call", output_to_operand_aliasing={{}: (5, {})} | custom-call | flops 1 | bytes 1 | tf_op jit(solution)/shard_map/gather/pallas_call | solution.py:380
  (22 shorter events, 0.2 us)
Async XLA Ops:
  0.8 13.1 %copy-start.2 = (s32[1,1024,3]{1,0,2:T(1,128)S(1)}, s32[1,1024,3]{1,0,2:T(1,128)}, u32[]{:S(2)}) copy-start(s32[1,1024,3]{1,0,2:T(1,128)} %param.18) | copy-start | bytes 36868
  0.8 13.1 %copy-start.1 = (f32[1,4,1024]{2,1,0:T(4,128)S(1)}, f32[1,4,1024]{2,1,0:T(4,128)}, u32[]{:S(2)}) copy-start(f32[1,4,1024]{2,1,0:T(4,128)} %param.16) | copy-start | bytes 49156
  3.1 14.9 %collective-permute-start = (f32[48,8,256]{2,1,0:T(8,128)S(1)}, f32[48,8,256]{2,1,0:T(8,128)S(1)}, u32[]{:S(2)}, u32[]{:S(2)}) collective-permute-start(f32[48,8,256]{2,1,0:T(8,128)S(1)} %get-tuple-element.63), channel_id=1, source_target_pairs={{0,1},{2,3},{4,5},{6,7},{8,9},{10,11},{12,13},{14,15},{16,17},{18,... | collective-permute-start | bytes 1179656 | tf_op jit(solution)/shard_map/ppermute | solution.py:402
  3.2 14.8 %collective-permute-start.1 = (f32[48,8,256]{2,1,0:T(8,128)S(1)}, f32[48,8,256]{2,1,0:T(8,128)S(1)}, u32[]{:S(2)}, u32[]{:S(2)}) collective-permute-start(f32[48,8,256]{2,1,0:T(8,128)S(1)} %get-tuple-element.64), channel_id=1, source_target_pairs={{1,2},{5,6},{9,10},{13,14},{17,18},{21,22},{25,26},{29,30},{2,1},{... | collective-permute-start | bytes 1179656 | tf_op jit(solution)/shard_map/ppermute | solution.py:402
  8.0 19.7 %collective-permute-start.2 = (f32[8,64,256]{2,1,0:T(8,128)S(1)}, f32[8,64,256]{2,1,0:T(8,128)S(1)}, u32[]{:S(2)}, u32[]{:S(2)}) collective-permute-start(f32[8,64,256]{2,1,0:T(8,128)S(1)} %get-tuple-element.67), channel_id=1, source_target_pairs={{4,8},{5,9},{6,10},{7,11},{12,16},{13,17},{14,18},{15,19},{20,24},... | collective-permute-start | bytes 1572872 | tf_op jit(solution)/shard_map/ppermute | solution.py:402
  13.1 14.7 %collective-permute-start.3 = (f32[8,64,256]{2,1,0:T(8,128)S(1)}, f32[8,64,256]{2,1,0:T(8,128)S(1)}, u32[]{:S(2)}, u32[]{:S(2)}) collective-permute-start(f32[8,64,256]{2,1,0:T(8,128)S(1)} %get-tuple-element.68), channel_id=1, source_target_pairs={{0,4},{1,5},{2,6},{3,7},{8,12},{9,13},{10,14},{11,15},{16,20},{17,... | collective-permute-start | bytes 1572872 | tf_op jit(solution)/shard_map/ppermute | solution.py:402
  13.9 4.1 %copy-start = (s32[1,3]{1,0:T(1,128)S(1)}, s32[1,3]{1,0:T(1,128)}, u32[]{:S(2)}) copy-start(s32[1,3]{1,0:T(1,128)} %refs_8_.15) | copy-start | bytes 40
  30.2 6.8 %collective-permute-start.4 = (f32[24,8,256]{2,1,0:T(8,128)S(1)}, f32[24,8,256]{2,1,0:T(8,128)S(1)}, u32[]{:S(2)}, u32[]{:S(2)}) collective-permute-start(f32[24,8,256]{2,1,0:T(8,128)S(1)} %get-tuple-element.80), channel_id=1, source_target_pairs={{0,1},{2,3},{4,5},{6,7},{8,9},{10,11},{12,13},{14,15},{16,17},{18,... | collective-permute-start | bytes 589832 | tf_op jit(solution)/shard_map/ppermute | solution.py:402
  30.3 6.8 %collective-permute-start.5 = (f32[24,8,256]{2,1,0:T(8,128)S(1)}, f32[24,8,256]{2,1,0:T(8,128)S(1)}, u32[]{:S(2)}, u32[]{:S(2)}) collective-permute-start(f32[24,8,256]{2,1,0:T(8,128)S(1)} %get-tuple-element.81), channel_id=1, source_target_pairs={{1,2},{5,6},{9,10},{13,14},{17,18},{21,22},{25,26},{29,30},{2,1},{... | collective-permute-start | bytes 589832 | tf_op jit(solution)/shard_map/ppermute | solution.py:402
  32.2 11.5 %collective-permute-start.6 = (f32[4,64,256]{2,1,0:T(8,128)S(1)}, f32[4,64,256]{2,1,0:T(8,128)S(1)}, u32[]{:S(2)}, u32[]{:S(2)}) collective-permute-start(f32[4,64,256]{2,1,0:T(8,128)S(1)} %get-tuple-element.82), channel_id=1, source_target_pairs={{4,8},{5,9},{6,10},{7,11},{12,16},{13,17},{14,18},{15,19},{20,24},... | collective-permute-start | bytes 786440 | tf_op jit(solution)/shard_map/ppermute | solution.py:402
  36.9 6.8 %collective-permute-start.7 = (f32[4,64,256]{2,1,0:T(8,128)S(1)}, f32[4,64,256]{2,1,0:T(8,128)S(1)}, u32[]{:S(2)}, u32[]{:S(2)}) collective-permute-start(f32[4,64,256]{2,1,0:T(8,128)S(1)} %get-tuple-element.83), channel_id=1, source_target_pairs={{0,4},{1,5},{2,6},{3,7},{8,12},{9,13},{10,14},{11,15},{16,20},{17,... | collective-permute-start | bytes 786440 | tf_op jit(solution)/shard_map/ppermute | solution.py:402
  45.5 7.4 %collective-permute-start.8 = (f32[24,8,256]{2,1,0:T(8,128)S(1)}, f32[24,8,256]{2,1,0:T(8,128)S(1)}, u32[]{:S(2)}, u32[]{:S(2)}) collective-permute-start(f32[24,8,256]{2,1,0:T(8,128)S(1)} %get-tuple-element.93), channel_id=1, source_target_pairs={{0,1},{2,3},{4,5},{6,7},{8,9},{10,11},{12,13},{14,15},{16,17},{18,... | collective-permute-start | bytes 589832 | tf_op jit(solution)/shard_map/ppermute | solution.py:402
  45.8 7.2 %collective-permute-start.9 = (f32[24,8,256]{2,1,0:T(8,128)S(1)}, f32[24,8,256]{2,1,0:T(8,128)S(1)}, u32[]{:S(2)}, u32[]{:S(2)}) collective-permute-start(f32[24,8,256]{2,1,0:T(8,128)S(1)} %get-tuple-element.94), channel_id=1, source_target_pairs={{1,2},{5,6},{9,10},{13,14},{17,18},{21,22},{25,26},{29,30},{2,1},{... | collective-permute-start | bytes 589832 | tf_op jit(solution)/shard_map/ppermute | solution.py:402
  49.0 10.7 %collective-permute-start.10 = (f32[4,64,256]{2,1,0:T(8,128)S(1)}, f32[4,64,256]{2,1,0:T(8,128)S(1)}, u32[]{:S(2)}, u32[]{:S(2)}) collective-permute-start(f32[4,64,256]{2,1,0:T(8,128)S(1)} %get-tuple-element.95), channel_id=1, source_target_pairs={{4,8},{5,9},{6,10},{7,11},{12,16},{13,17},{14,18},{15,19},{20,24},... | collective-permute-start | bytes 786440 | tf_op jit(solution)/shard_map/ppermute | solution.py:402
  52.8 6.9 %collective-permute-start.11 = (f32[4,64,256]{2,1,0:T(8,128)S(1)}, f32[4,64,256]{2,1,0:T(8,128)S(1)}, u32[]{:S(2)}, u32[]{:S(2)}) collective-permute-start(f32[4,64,256]{2,1,0:T(8,128)S(1)} %get-tuple-element.96), channel_id=1, source_target_pairs={{0,4},{1,5},{2,6},{3,7},{8,12},{9,13},{10,14},{11,15},{16,20},{17,... | collective-permute-start | bytes 786440 | tf_op jit(solution)/shard_map/ppermute | solution.py:402
  61.4 6.5 %collective-permute-start.12 = (f32[24,8,256]{2,1,0:T(8,128)S(1)}, f32[24,8,256]{2,1,0:T(8,128)S(1)}, u32[]{:S(2)}, u32[]{:S(2)}) collective-permute-start(f32[24,8,256]{2,1,0:T(8,128)S(1)} %get-tuple-element.102), channel_id=1, source_target_pairs={{0,1},{2,3},{4,5},{6,7},{8,9},{10,11},{12,13},{14,15},{16,17},{18,... | collective-permute-start | bytes 589832 | tf_op jit(solution)/shard_map/ppermute | solution.py:402
  61.5 6.4 %collective-permute-start.13 = (f32[24,8,256]{2,1,0:T(8,128)S(1)}, f32[24,8,256]{2,1,0:T(8,128)S(1)}, u32[]{:S(2)}, u32[]{:S(2)}) collective-permute-start(f32[24,8,256]{2,1,0:T(8,128)S(1)} %get-tuple-element.103), channel_id=1, source_target_pairs={{1,2},{5,6},{9,10},{13,14},{17,18},{21,22},{25,26},{29,30},{2,1},{... | collective-permute-start | bytes 589832 | tf_op jit(solution)/shard_map/ppermute | solution.py:402
  63.6 10.7 %collective-permute-start.14 = (f32[4,64,256]{2,1,0:T(8,128)S(1)}, f32[4,64,256]{2,1,0:T(8,128)S(1)}, u32[]{:S(2)}, u32[]{:S(2)}) collective-permute-start(f32[4,64,256]{2,1,0:T(8,128)S(1)} %get-tuple-element.104), channel_id=1, source_target_pairs={{4,8},{5,9},{6,10},{7,11},{12,16},{13,17},{14,18},{15,19},{20,24},... | collective-permute-start | bytes 786440 | tf_op jit(solution)/shard_map/ppermute | solution.py:402
  67.8 6.5 %collective-permute-start.15 = (f32[4,64,256]{2,1,0:T(8,128)S(1)}, f32[4,64,256]{2,1,0:T(8,128)S(1)}, u32[]{:S(2)}, u32[]{:S(2)}) collective-permute-start(f32[4,64,256]{2,1,0:T(8,128)S(1)} %get-tuple-element.105), channel_id=1, source_target_pairs={{0,4},{1,5},{2,6},{3,7},{8,12},{9,13},{10,14},{11,15},{16,20},{17,... | collective-permute-start | bytes 786440 | tf_op jit(solution)/shard_map/ppermute | solution.py:402
  76.5 7.5 %collective-permute-start.24 = (f32[8,64,256]{2,1,0:T(8,128)S(1)}, f32[8,64,256]{2,1,0:T(8,128)S(1)}, u32[]{:S(2)}, u32[]{:S(2)}) collective-permute-start(f32[8,64,256]{2,1,0:T(8,128)S(1)} %get-tuple-element.116), channel_id=1, source_target_pairs={{0,32},{32,0},{64,96},{96,64},{1,33},{33,1},{65,97},{97,65},{2,34}... | collective-permute-start | bytes 1572872 | tf_op jit(solution)/shard_map/ppermute | solution.py:414
  82.4 2.3 %collective-permute-start.16 = (f32[8,64,256]{2,1,0:T(8,128)S(1)}, f32[8,64,256]{2,1,0:T(8,128)S(1)}, u32[]{:S(2)}, u32[]{:S(2)}) collective-permute-start(f32[8,64,256]{2,1,0:T(8,128)S(1)} %get-tuple-element.110), channel_id=1, source_target_pairs={{0,32},{32,0},{64,96},{96,64},{1,33},{33,1},{65,97},{97,65},{2,34}... | collective-permute-start | bytes 1572872 | tf_op jit(solution)/shard_map/ppermute | solution.py:414
  84.0 13.2 %collective-permute-start.25 = (f32[8,64,256]{2,1,0:T(8,128)S(1)}, f32[8,64,256]{2,1,0:T(8,128)S(1)}, u32[]{:S(2)}, u32[]{:S(2)}) collective-permute-start(f32[8,64,256]{2,1,0:T(8,128)S(1)} %add_cores.7.a), channel_id=1, source_target_pairs={{0,64},{32,96},{64,0},{96,32},{1,65},{33,97},{65,1},{97,33},{2,66}... | collective-permute-start | bytes 1572872 | tf_op jit(solution)/shard_map/ppermute | solution.py:419
  84.1 2.5 %collective-permute-start.21 = (f32[4,64,256]{2,1,0:T(8,128)S(1)}, f32[4,64,256]{2,1,0:T(8,128)S(1)}, u32[]{:S(2)}, u32[]{:S(2)}) collective-permute-start(f32[4,64,256]{2,1,0:T(8,128)S(1)} %get-tuple-element.114), channel_id=1, source_target_pairs={{0,32},{32,0},{64,96},{96,64},{1,33},{33,1},{65,97},{97,65},{2,34}... | collective-permute-start | bytes 786440 | tf_op jit(solution)/shard_map/ppermute | solution.py:414
  84.7 30.6 %collective-permute-start.17 = (f32[8,64,256]{2,1,0:T(8,128)S(1)}, f32[8,64,256]{2,1,0:T(8,128)S(1)}, u32[]{:S(2)}, u32[]{:S(2)}) collective-permute-start(f32[8,64,256]{2,1,0:T(8,128)S(1)} %add_cores.4.a), channel_id=1, source_target_pairs={{0,64},{32,96},{64,0},{96,32},{1,65},{33,97},{65,1},{97,33},{2,66}... | collective-permute-start | bytes 1572872 | tf_op jit(solution)/shard_map/ppermute | solution.py:419
  86.3 13.0 %collective-permute-start.19 = (f32[4,64,256]{2,1,0:T(8,128)S(1)}, f32[4,64,256]{2,1,0:T(8,128)S(1)}, u32[]{:S(2)}, u32[]{:S(2)}) collective-permute-start(f32[4,64,256]{2,1,0:T(8,128)S(1)} %get-tuple-element.112), channel_id=1, source_target_pairs={{0,32},{32,0},{64,96},{96,64},{1,33},{33,1},{65,97},{97,65},{2,34}... | collective-permute-start | bytes 786440 | tf_op jit(solution)/shard_map/ppermute | solution.py:414
  86.7 27.4 %collective-permute-start.22 = (f32[4,64,256]{2,1,0:T(8,128)S(1)}, f32[4,64,256]{2,1,0:T(8,128)S(1)}, u32[]{:S(2)}, u32[]{:S(2)}) collective-permute-start(f32[4,64,256]{2,1,0:T(8,128)S(1)} %add_cores.6.a), channel_id=1, source_target_pairs={{0,64},{32,96},{64,0},{96,32},{1,65},{33,97},{65,1},{97,33},{2,66}... | collective-permute-start | bytes 786440 | tf_op jit(solution)/shard_map/ppermute | solution.py:419
  97.3 20.3 %collective-permute-start.26 = (f32[8,64,256]{2,1,0:T(8,128)S(1)}, f32[8,64,256]{2,1,0:T(8,128)S(1)}, u32[]{:S(2)}, u32[]{:S(2)}) collective-permute-start(f32[8,64,256]{2,1,0:T(8,128)S(1)} %add_chips.6.refs_2_), channel_id=1, source_target_pairs={{0,32},{32,0},{64,96},{96,64},{1,33},{33,1},{65,97},{97,65},{2,34}... | collective-permute-start | bytes 1572872 | tf_op jit(solution)/shard_map/ppermute | solution.py:422
  114.1 3.5 %collective-permute-start.23 = (f32[4,64,256]{2,1,0:T(8,128)S(1)}, f32[4,64,256]{2,1,0:T(8,128)S(1)}, u32[]{:S(2)}, u32[]{:S(2)}) collective-permute-start(f32[4,64,256]{2,1,0:T(8,128)S(1)} %add_chips.5.refs_0_), channel_id=1, source_target_pairs={{0,32},{32,0},{64,96},{96,64},{1,33},{33,1},{65,97},{97,65},{2,34}... | collective-permute-start | bytes 786440 | tf_op jit(solution)/shard_map/ppermute | solution.py:422
  115.4 7.9 %collective-permute-start.20 = (f32[4,64,256]{2,1,0:T(8,128)S(1)}, f32[4,64,256]{2,1,0:T(8,128)S(1)}, u32[]{:S(2)}, u32[]{:S(2)}) collective-permute-start(f32[4,64,256]{2,1,0:T(8,128)S(1)} %add_cores.5.a), channel_id=1, source_target_pairs={{0,64},{32,96},{64,0},{96,32},{1,65},{33,97},{65,1},{97,33},{2,66}... | collective-permute-start | bytes 786440 | tf_op jit(solution)/shard_map/ppermute | solution.py:419
  115.5 8.8 %collective-permute-start.18 = (f32[8,64,256]{2,1,0:T(8,128)S(1)}, f32[8,64,256]{2,1,0:T(8,128)S(1)}, u32[]{:S(2)}, u32[]{:S(2)}) collective-permute-start(f32[8,64,256]{2,1,0:T(8,128)S(1)} %add_chips.4.refs_0_), channel_id=1, source_target_pairs={{0,32},{32,0},{64,96},{96,64},{1,33},{33,1},{65,97},{97,65},{2,34}... | collective-permute-start | bytes 1572872 | tf_op jit(solution)/shard_map/ppermute | solution.py:422
  123.3 2.1 %collective-permute-start.27 = (f32[4,64,256]{2,1,0:T(8,128)S(1)}, f32[4,64,256]{2,1,0:T(8,128)S(1)}, u32[]{:S(2)}, u32[]{:S(2)}) collective-permute-start(f32[4,64,256]{2,1,0:T(8,128)S(1)} %add_chips.7.refs_2_), channel_id=1, source_target_pairs={{0,32},{32,0},{64,96},{96,64},{1,33},{33,1},{65,97},{97,65},{2,34}... | collective-permute-start | bytes 786440 | tf_op jit(solution)/shard_map/ppermute | solution.py:422

commit v4 on v3

--- a/solution.py
+++ b/solution.py
@@ -14,11 +14,11 @@
 G = 8
 RADIUS = 4
 
-SECOND = (8064.0, -1008.0, 128.0, -9.0)
-SECOND_CENTRE_Y, SECOND_CENTRE_Z = -43008.0, -42.0
-SECOND_SCALE = 5040.0
-FIRST = (672.0, -168.0, 32.0, -3.0)
-FIRST_SCALE = 840.0
+SECOND = (63.0, -7.875, 1.0, -0.0703125)
+SECOND_CENTRE_Y, SECOND_CENTRE_Z = -336.0, -0.328125
+SECOND_SCALE = 5040.0 / 128.0
+FIRST = (21.0, -5.25, 1.0, -0.09375)
+FIRST_SCALE = 840.0 / 32.0
 
 F32 = jnp.float32
 BF16 = jnp.bfloat16
@@ -64,23 +64,17 @@
     return jnp.dot(a, b, preferred_element_type=F32)
 
 
+def weighted(weights, terms):
+    terms = [t if w == 1.0 else w * t for w, t in zip(weights, terms)]
+    return functools.reduce(lambda a, b: a + b, terms)
+
+
 def x_first(window, g):
-    total = None
-    for k, w in enumerate(FIRST, 1):
-        term = w * (window[g + RADIUS + k] - window[g + RADIUS - k])
-        total = term if total is None else total + term
-    return total
-
-
-def x_both(window, g):
-    second = first = None
-    for k in range(1, RADIUS + 1):
-        upper, lower = window[g + RADIUS + k], window[g + RADIUS - k]
-        s = SECOND[k - 1] * (upper + lower)
-        f = FIRST[k - 1] * (upper - lower)
-        second = s if second is None else second + s
-        first = f if first is None else first + f
-    return second, first
+    return weighted(FIRST, [window[g + RADIUS + k] - window[g + RADIUS - k] for k in range(1, RADIUS + 1)])
+
+
+def x_second(window, g):
+    return weighted(SECOND, [window[g + RADIUS + k] + window[g + RADIUS - k] for k in range(1, RADIUS + 1)])
 
 
 def halo_parts(first_ref, second_ref, pair):
@@ -218,8 +212,8 @@
             for g in range(count):
                 here = (base + g,) + at
                 centre = window[g + RADIUS]
-                second, first = x_both(window, g)
-                second = second + (ys[(g,) + at] + zs[(g,) + at])
+                first = x_first(window, g)
+                second = x_second(window, g) + (ys[(g,) + at] + zs[(g,) + at])
                 change = coef[0][here] * second + coef[1][here] * first
                 change = change + coef[2][here] * ys[(g,) + below] + coef[3][here] * zs[(g,) + beside]
                 kept = (centre + centre) - p[here]
@@ -410,9 +404,10 @@
 CHIPS = [(i, i ^ 2) for i in range(4)]
 
 
-def add_cores(sent, kept):
+def add_cores(sent, kept, after=()):
     arrived = lax.ppermute(sent, "shot", CORES)
-    return call(add_kernel, "add_cores", (kept, arrived), [VMEM] * 2, [kept.shape])[0]
+    args = [kept, arrived] + list(after)
+    return call(add_kernel, "add_cores", args, [VMEM] * len(args), [kept.shape])[0]
 
 
 def add_chips(mine, after):
@@ -492,27 +487,29 @@
         held.update(q=held["out"], p=held["q"], snap=snap_next)
 
     held.update(zip(("xa", "xb", "ya", "yb"), halos))
-    run(STEPS - 1, inner, False, ("image",), {}, weight=4 << 30)
-    splits, halves, at = [], {}, 0
-    for i, size in enumerate((4, 8, 8, 4)):
-        splits.append(((at, at + size), (size_x - at - size, size_x - at)))
-        halves.update({"sent%d" % i: (size, size_y, size_z), "kept%d" % i: (size, size_y, size_z)})
+    splits, at = [], 0
+    for size in (8, 10, 6):
+        splits.insert(0, ((at, at + size), (size_x - at - size, size_x - at)))
         at += size
-    halves = run(STEPS - 1, [], True, ("out", "image"), halves, splits)
-    sums = [add_cores(*halves[2 * i : 2 * i + 2]) for i in range(len(splits))]
+
+    def halves(splits):
+        shapes = [(lower[1] - lower[0], size_y, size_z) for lower, _ in splits]
+        return {name + str(i): shape for i, shape in enumerate(shapes) for name in ("sent", "kept")}
+
+    early = run(STEPS - 1, inner, False, ("image",), halves(splits[:1]), splits[:1], weight=4 << 30)
+    late = run(STEPS - 1, [], True, ("out", "image"), halves(splits[1:]), splits[1:], weight=4 << 30)
+    sums = [add_cores(*early, after=late[:1]), add_cores(*late[:2]), add_cores(*late[2:])]
     (last,) = call(store_kernel, "store", [held["out"]], [VMEM], [pltpu.HBM(grid, F32)], {}, [pltpu.SemaphoreType.DMA])
-    started, chunks = [], []
-    for n, mine in enumerate(sums):
-        chunks += add_chips(mine, started + [last] if n == 3 else [])
-        if n % 2:
-            ranges = splits[n - 1 : n + 1]
-            started = call(
-                functools.partial(gather_kernel, ranges), "gather", [corner] + chunks + started,
-                [SMEM] + [VMEM] * 4 + [HBM] * len(started), [pltpu.HBM(grid, F32)], {5: 0} if started else {},
-                [pltpu.SemaphoreType.DMA((2, 2))],
-            )
-            chunks = []
-    return started[0][None], last[None, None]
+    def gather(splits, chunks, started):
+        return call(
+            functools.partial(gather_kernel, splits), "gather", [corner] + chunks + started,
+            [SMEM] + [VMEM] * len(chunks) + [HBM] * len(started), [pltpu.HBM(grid, F32)],
+            {1 + len(chunks): 0} if started else {}, [pltpu.SemaphoreType.DMA((len(splits), 2))],
+        )
+
+    started = gather(splits[:2], [*add_chips(sums[0], []), *add_chips(sums[1], [])], [])
+    (gradient,) = gather(splits[2:], [*add_chips(sums[2], started + [last])], started)
+    return gradient[None], last[None, None]
 
 
 def solution(mesh):

time: 128 us -> 125 us (0.977)
  waiting for transfers between devices: 33.3 us -> 30 us
    ppermute x4 -> x3, waiting for transfers between devices: 28.3 us -> 24 us  [add_chips(): arrived = lax.ppermute(mine, 'shot', CHIPS)]
    ppermute x4 -> x3, waiting for transfers between devices: 1.59 us -> 2.94 us  [add_cores(): arrived = lax.ppermute(sent, 'shot', CORES)]
    ppermute x4 -> x3, starting transfers between devices: 4.75 us -> 5.44 us  [add_chips(): return (mine, lax.ppermute(mine, 'shot', CORES))]
    ppermute x4 -> x3, starting transfers between devices: 6.77 us -> 6.33 us  [add_cores(): arrived = lax.ppermute(sent, 'shot', CORES)]
    pallas_call x21 -> x19, Pallas kernels: 47.3 us -> 47.5 us  [call(): pl.pallas_call(kernel, name=name, in_specs=specs, out_specs=[pl.BlockSpec...]
  transfers between devices with their start and end apart: 28 -> 25, of which waited for: 9 -> 8; matrix products, arithmetic and copies ran while one was open for 0% -> 0% of each run, Pallas kernels for 28% -> 29%
where the time goes in v4:
time: 125 us; the launch traced here: 124 us
  Pallas kernels  47.5 us (38%)
  starting transfers between devices  44.5 us (36%)
  waiting for transfers between devices  30 us (24%)
  between operations  1.9 us (2%)
    pallas_call x19, Pallas kernels, call(): pl.pallas_call(kernel, name=name, in_specs=specs, out_specs=[pl.BlockSpec...  47.5 us
    ppermute x16, starting transfers between devices, swap(): return lax.ppermute(strip, 'dom', pairs + [(b, a) for a, b in pairs])  30.8 us
    ppermute x3, waiting for transfers between devices, add_chips(): arrived = lax.ppermute(mine, 'shot', CHIPS)  24 us
    ppermute x3, starting transfers between devices, add_cores(): arrived = lax.ppermute(sent, 'shot', CORES)  6.33 us
    ppermute x3, starting transfers between devices, add_chips(): return (mine, lax.ppermute(mine, 'shot', CORES))  5.44 us
    ppermute x3, waiting for transfers between devices, add_cores(): arrived = lax.ppermute(sent, 'shot', CORES)  2.94 us
  transfers between devices with their start and end apart: 25, of which 8 were waited for; matrix products, arithmetic and copies ran while one was open for 0% of the time, Pallas kernels for 29%

profile of v4, /device:TPU:57, one launch (start us, length us, event | category | flops | bytes accessed | tf_op | source)
XLA Modules:
  0.0 124.1 jit_solution(14906984414964246699)
XLA Ops:
  0.7 0.1 stack.23.corner.refs_9_
  0.8 2.3 %strips.1 = (f32[8,64,256]{2,1,0:T(8,128)S(1)}, f32[8,64,256]{2,1,0:T(8,128)S(1)}, f32[48,8,256]{2,1,0:T(8,128)S(1)}, f32[48,8,256]{2,1,0:T(8,128)S(1)}) custom-call(f32[48,64,256]{2,1,0:T(8,128)} %bitcast.24, f32[48,64,256]{2,1,0:T(8,128)} %bitcast.26, s32[5]{0:T(128)S(1)} %stack.23.corner.refs_9_), custom_call_target="tpu_custom_call" | custom-call | flops 1 | bytes 1 | tf_op jit(solution)/shard_map/strips/pallas_call | solution.py:374
  3.1 0.1 collective-permute-start
  3.2 4.9 %collective-permute-start.1 = (f32[48,8,256]{2,1,0:T(8,128)S(1)}, f32[48,8,256]{2,1,0:T(8,128)S(1)}, u32[]{:S(2)}, u32[]{:S(2)}) collective-permute-start(f32[48,8,256]{2,1,0:T(8,128)S(1)} %get-tuple-element.62), channel_id=1, source_target_pairs={{1,2},{5,6},{9,10},{13,14},{17,18},{21,22},{25,26},{29,30},{2,1},{... | collective-permute-start | bytes 1179656 | tf_op jit(solution)/shard_map/ppermute | solution.py:396
  8.0 5.1 %collective-permute-start.2 = (f32[8,64,256]{2,1,0:T(8,128)S(1)}, f32[8,64,256]{2,1,0:T(8,128)S(1)}, u32[]{:S(2)}, u32[]{:S(2)}) collective-permute-start(f32[8,64,256]{2,1,0:T(8,128)S(1)} %get-tuple-element.65), channel_id=1, source_target_pairs={{4,8},{5,9},{6,10},{7,11},{12,16},{13,17},{14,18},{15,19},{20,24},... | collective-permute-start | bytes 1572872 | tf_op jit(solution)/shard_map/ppermute | solution.py:396
  13.1 0.1 collective-permute-start.3
  13.9 0.0 copy-start
  13.9 4.1 %fetch.1 = (f32[48,64,128]{2,1,0:T(8,128)S(1)}, f32[48,64,256]{2,1,0:T(8,128)S(1)}, f32[48,64,256]{2,1,0:T(8,128)S(1)}, bf16[4,128,160]{2,1,0:T(8,128)(2,1)S(1)}...) custom-call(s32[3,1,1024]{2,1,0:T(1,128)S(1)} %broadcast_in_dim.9.places, f32[4,1024]{1,0:T(4,128)S(1)} %bitcast.18, ...), custom_call_target="tpu_custom_call" | custom-call | flops 1 | bytes 1 | tf_op jit(solution)/shard_map/fetch/pallas_call | solution.py:374
  18.0 0.0 collective-permute-done.refs_3_
  18.0 0.0 collective-permute-done.1.refs_4_
  18.0 9.5 %step0.2 = (f32[48,64,256]{2,1,0:T(8,128)S(1)}, f32[48,64,256]{2,1,0:T(8,128)S(1)}, f32[48,64,256]{2,1,0:T(8,128)S(1)}, f32[48,64,256]{2,1,0:T(8,128)S(1)}, f32[...) custom-call(f32[48,64,256]{2,1,0:T(8,128)S(1)} %get-tuple-element.58, ...), custom_call_target="tpu_custom_call" | custom-call | flops 4294967296 | bytes 1 | tf_op jit(solution)/shard_map/step0/pallas_call | solution.py:374
  27.5 0.0 collective-permute-done.2.refs_10_
  27.5 0.0 collective-permute-done.3.refs_11_
  27.5 2.4 %step0.3 = (f32[48,64,256]{2,1,0:T(8,128)S(1)}, f32[48,64,256]{2,1,0:T(8,128)S(1)}, f32[48,64,256]{2,1,0:T(8,128)S(1)}, f32[48,64,256]{2,1,0:T(8,128)S(1)}, f32[...) custom-call(f32[48,64,256]{2,1,0:T(8,128)S(1)} %get-tuple-element.58, ...), custom_call_target="tpu_custom_call", output_to_operand_aliasing={{0}: (15, {}), {1}: (16, {}), {2}: (17, {}), {3}: (18, {}),... | custom-call | flops 1 | bytes 1 | tf_op jit(solution)/shard_map/step0/pallas_call | solution.py:374
  30.0 0.1 collective-permute-start.4
  30.1 1.9 %collective-permute-start.5 = (f32[24,8,256]{2,1,0:T(8,128)S(1)}, f32[24,8,256]{2,1,0:T(8,128)S(1)}, u32[]{:S(2)}, u32[]{:S(2)}) collective-permute-start(f32[24,8,256]{2,1,0:T(8,128)S(1)} %get-tuple-element.79), channel_id=1, source_target_pairs={{1,2},{5,6},{9,10},{13,14},{17,18},{21,22},{25,26},{29,30},{2,1},{... | collective-permute-start | bytes 589832 | tf_op jit(solution)/shard_map/ppermute | solution.py:396
  32.0 4.7 %collective-permute-start.6 = (f32[4,64,256]{2,1,0:T(8,128)S(1)}, f32[4,64,256]{2,1,0:T(8,128)S(1)}, u32[]{:S(2)}, u32[]{:S(2)}) collective-permute-start(f32[4,64,256]{2,1,0:T(8,128)S(1)} %get-tuple-element.80), channel_id=1, source_target_pairs={{4,8},{5,9},{6,10},{7,11},{12,16},{13,17},{14,18},{15,19},{20,24},... | collective-permute-start | bytes 786440 | tf_op jit(solution)/shard_map/ppermute | solution.py:396
  36.7 0.1 collective-permute-start.7
  36.8 0.0 collective-permute-done.4.refs_3_
  36.8 0.0 collective-permute-done.5.refs_4_
  36.8 5.9 %step1.2 = (f32[48,64,256]{2,1,0:T(8,128)S(1)}, f32[48,64,256]{2,1,0:T(8,128)S(1)}, bf16[48,64,256]{2,1,0:T(8,128)(2,1)S(1)}) custom-call(f32[48,64,256]{2,1,0:T(8,128)S(1)} %get-tuple-element.76.refs_0_.refs_11_.refs_12_, bf16[48,64,256]{2,1,0:T(8,128)(2,1)S(1)} %get-tuple-element.77.refs_1_, ...), custom_call_target="tpu_custom_call", output_to_operand_aliasing={{1}: (16, {})} | custom-call | flops 4294967296 | bytes 1 | tf_op jit(solution)/shard_map/step1/pallas_call | solution.py:374
  42.7 0.8 collective-permute-done.6.refs_10_
  43.5 0.0 collective-permute-done.7.refs_11_
  43.5 1.7 %step1.3 = (f32[48,64,256]{2,1,0:T(8,128)S(1)}, f32[48,64,256]{2,1,0:T(8,128)S(1)}, f32[4,64,256]{2,1,0:T(8,128)S(1)}, f32[4,64,256]{2,1,0:T(8,128)S(1)}, f32[24...) custom-call(f32[48,64,256]{2,1,0:T(8,128)S(1)} %get-tuple-element.76.refs_0_.refs_1, ...), custom_call_target="tpu_custom_call", output_to_operand_aliasing={{0}: (17, {}), {1}: (18, {})} | custom-call | flops 1 | bytes 1 | tf_op jit(solution)/shard_map/step1/pallas_call | solution.py:374
  45.2 0.3 collective-permute-start.8
  45.5 3.2 %collective-permute-start.9 = (f32[24,8,256]{2,1,0:T(8,128)S(1)}, f32[24,8,256]{2,1,0:T(8,128)S(1)}, u32[]{:S(2)}, u32[]{:S(2)}) collective-permute-start(f32[24,8,256]{2,1,0:T(8,128)S(1)} %get-tuple-element.92), channel_id=1, source_target_pairs={{1,2},{5,6},{9,10},{13,14},{17,18},{21,22},{25,26},{29,30},{2,1},{... | collective-permute-start | bytes 589832 | tf_op jit(solution)/shard_map/ppermute | solution.py:396
  48.7 3.8 %collective-permute-start.10 = (f32[4,64,256]{2,1,0:T(8,128)S(1)}, f32[4,64,256]{2,1,0:T(8,128)S(1)}, u32[]{:S(2)}, u32[]{:S(2)}) collective-permute-start(f32[4,64,256]{2,1,0:T(8,128)S(1)} %get-tuple-element.93), channel_id=1, source_target_pairs={{4,8},{5,9},{6,10},{7,11},{12,16},{13,17},{14,18},{15,19},{20,24},... | collective-permute-start | bytes 786440 | tf_op jit(solution)/shard_map/ppermute | solution.py:396
  52.5 0.1 collective-permute-start.11
  52.6 0.0 collective-permute-done.8.refs_3_
  52.6 0.0 collective-permute-done.9.refs_4_
  52.6 6.0 %step2.2 = (f32[48,64,256]{2,1,0:T(8,128)S(1)}, f32[48,64,256]{2,1,0:T(8,128)S(1)}, bf16[48,64,256]{2,1,0:T(8,128)(2,1)S(1)}) custom-call(f32[48,64,256]{2,1,0:T(8,128)S(1)} %get-tuple-element.89.refs_0_.refs_10_.refs_12_, bf16[48,64,256]{2,1,0:T(8,128)(2,1)S(1)} %get-tuple-element.90.refs_1_, ...), custom_call_target="tpu_custom_call", output_to_operand_aliasing={{1}: (16, {})} | custom-call | flops 4294967296 | bytes 1 | tf_op jit(solution)/shard_map/step2/pallas_call | solution.py:374
  58.7 0.7 collective-permute-done.10.refs_10_
  59.4 1.7 %step2.3 = (f32[48,64,256]{2,1,0:T(8,128)S(1)}, f32[48,64,256]{2,1,0:T(8,128)S(1)}, f32[4,64,256]{2,1,0:T(8,128)S(1)}, f32[4,64,256]{2,1,0:T(8,128)S(1)}, f32[24...) custom-call(f32[48,64,256]{2,1,0:T(8,128)S(1)} %get-tuple-element.89.refs_0_.refs_1, ...), custom_call_target="tpu_custom_call", output_to_operand_aliasing={{0}: (17, {}), {1}: (18, {})} | custom-call | flops 1 | bytes 1 | tf_op jit(solution)/shard_map/step2/pallas_call | solution.py:374
  61.1 0.1 collective-permute-start.12
  61.2 2.1 %collective-permute-start.13 = (f32[24,8,256]{2,1,0:T(8,128)S(1)}, f32[24,8,256]{2,1,0:T(8,128)S(1)}, u32[]{:S(2)}, u32[]{:S(2)}) collective-permute-start(f32[24,8,256]{2,1,0:T(8,128)S(1)} %get-tuple-element.101), channel_id=1, source_target_pairs={{1,2},{5,6},{9,10},{13,14},{17,18},{21,22},{25,26},{29,30},{2,1},{... | collective-permute-start | bytes 589832 | tf_op jit(solution)/shard_map/ppermute | solution.py:396
  63.3 4.4 %collective-permute-start.14 = (f32[4,64,256]{2,1,0:T(8,128)S(1)}, f32[4,64,256]{2,1,0:T(8,128)S(1)}, u32[]{:S(2)}, u32[]{:S(2)}) collective-permute-start(f32[4,64,256]{2,1,0:T(8,128)S(1)} %get-tuple-element.102), channel_id=1, source_target_pairs={{4,8},{5,9},{6,10},{7,11},{12,16},{13,17},{14,18},{15,19},{20,24},... | collective-permute-start | bytes 786440 | tf_op jit(solution)/shard_map/ppermute | solution.py:396
  67.7 0.1 collective-permute-start.15
  67.8 0.0 collective-permute-done.13.refs_4_
  67.8 6.4 %step3.2 = (f32[48,64,256]{2,1,0:T(8,128)S(1)}, f32[48,64,256]{2,1,0:T(8,128)S(1)}, f32[6,64,256]{2,1,0:T(8,128)S(1)}, f32[6,64,256]{2,1,0:T(8,128)S(1)}) custom-call(f32[48,64,256]{2,1,0:T(8,128)S(1)} %get-tuple-element.98.refs_0_, bf16[48,64,256]{2,1,0:T(8,128)(2,1)S(1)} %get-tuple-element.99.refs_1_, ...), custom_call_target="tpu_custom_call", output_to_operand_aliasing={{1}: (15, {})} | custom-call | flops 4294967296 | bytes 1 | tf_op jit(solution)/shard_map/step3/pallas_call | solution.py:374
  74.2 2.0 %step3.3 = (f32[48,64,256]{2,1,0:T(8,128)S(1)}, f32[48,64,256]{2,1,0:T(8,128)S(1)}, f32[10,64,256]{2,1,0:T(8,128)S(1)}, f32[10,64,256]{2,1,0:T(8,128)S(1)}, f32[...) custom-call(f32[48,64,256]{2,1,0:T(8,128)S(1)} %get-tuple-element.98.refs_0_, ...), custom_call_target="tpu_custom_call", output_to_operand_aliasing={{0}: (17, {}), {1}: (18, {})} | custom-call | flops 4294967296 | bytes 1 | tf_op jit(solution)/shard_map/step3/pallas_call | solution.py:374
  76.3 5.7 %collective-permute-start.21 = (f32[10,64,256]{2,1,0:T(8,128)S(1)}, f32[10,64,256]{2,1,0:T(8,128)S(1)}, u32[]{:S(2)}, u32[]{:S(2)}) collective-permute-start(f32[10,64,256]{2,1,0:T(8,128)S(1)} %get-tuple-element.111.rest_0_), channel_id=1, source_target_pairs={{0,32},{32,0},{64,96},{96,64},{1,33},{33,1},{65,97},{97,65},{2,34}... | collective-permute-start | bytes 1966088 | tf_op jit(solution)/shard_map/ppermute | solution.py:408
  82.0 1.7 %collective-permute-done.21.b = f32[10,64,256]{2,1,0:T(8,128)S(1)} collective-permute-done((f32[10,64,256]{2,1,0:T(8,128)S(1)}, f32[10,64,256]{2,1,0:T(8,128)S(1)}, u32[]{:S(2)}, u32[]{:S(2)}) %collective-permute-start.21) | collective-permute-done | bytes 655392 | tf_op jit(solution)/shard_map/ppermute | solution.py:408
  83.7 0.1 add_cores.5.a
  83.8 0.1 collective-permute-start.22
  83.9 0.5 collective-permute-start.18
  84.4 0.1 collective-permute-start.16
  84.5 1.2 collective-permute-done.18.b
  85.8 1.7 %collective-permute-start.19 = (f32[6,64,256]{2,1,0:T(8,128)S(1)}, f32[6,64,256]{2,1,0:T(8,128)S(1)}, u32[]{:S(2)}, u32[]{:S(2)}) collective-permute-start(f32[6,64,256]{2,1,0:T(8,128)S(1)} %add_cores.4.a), channel_id=1, source_target_pairs={{0,64},{32,96},{64,0},{96,32},{1,65},{33,97},{65,1},{97,33},{2,66}... | collective-permute-start | bytes 1179656 | tf_op jit(solution)/shard_map/ppermute | solution.py:414
  87.5 12.4 %collective-permute-done.22.b = f32[10,64,256]{2,1,0:T(8,128)S(1)} collective-permute-done((f32[10,64,256]{2,1,0:T(8,128)S(1)}, f32[10,64,256]{2,1,0:T(8,128)S(1)}, u32[]{:S(2)}, u32[]{:S(2)}) %collective-permute-start.22) | collective-permute-done | bytes 655392 | tf_op jit(solution)/shard_map/ppermute | solution.py:414
  99.8 0.1 add_chips.4.refs_2_
  99.9 2.1 %collective-permute-start.23 = (f32[10,64,256]{2,1,0:T(8,128)S(1)}, f32[10,64,256]{2,1,0:T(8,128)S(1)}, u32[]{:S(2)}, u32[]{:S(2)}) collective-permute-start(f32[10,64,256]{2,1,0:T(8,128)S(1)} %add_chips.4.refs_2_), channel_id=1, source_target_pairs={{0,32},{32,0},{64,96},{96,64},{1,33},{33,1},{65,97},{97,65},{2,34}... | collective-permute-start | bytes 1966088 | tf_op jit(solution)/shard_map/ppermute | solution.py:417
  102.0 0.0 collective-permute-done.16.b
  102.0 0.1 add_cores.3.a
  102.1 0.1 collective-permute-start.17
  102.2 6.1 %collective-permute-done.19.b = f32[6,64,256]{2,1,0:T(8,128)S(1)} collective-permute-done((f32[6,64,256]{2,1,0:T(8,128)S(1)}, f32[6,64,256]{2,1,0:T(8,128)S(1)}, u32[]{:S(2)}, u32[]{:S(2)}) %collective-permute-start.19) | collective-permute-done | bytes 393248 | tf_op jit(solution)/shard_map/ppermute | solution.py:414
  108.3 2.1 %collective-permute-start.20 = (f32[6,64,256]{2,1,0:T(8,128)S(1)}, f32[6,64,256]{2,1,0:T(8,128)S(1)}, u32[]{:S(2)}, u32[]{:S(2)}) collective-permute-start(f32[6,64,256]{2,1,0:T(8,128)S(1)} %add_chips.3.refs_0_), channel_id=1, source_target_pairs={{0,32},{32,0},{64,96},{96,64},{1,33},{33,1},{65,97},{97,65},{2,34}... | collective-permute-start | bytes 1179656 | tf_op jit(solution)/shard_map/ppermute | solution.py:417
  110.4 1.7 %store.1.rest_1_ = f32[48,64,256]{2,1,0:T(8,128)} custom-call(f32[48,64,256]{2,1,0:T(8,128)S(1)} %get-tuple-element.113.source), custom_call_target="tpu_custom_call" | custom-call | flops 1 | bytes 1 | tf_op jit(solution)/shard_map/store/pallas_call | solution.py:374
  112.1 0.0 collective-permute-done.20.refs_1_
  112.1 1.9 %gather.2.rest_0_.refs_2_ = f32[48,64,256]{2,1,0:T(8,128)} custom-call(s32[5]{0:T(128)S(1)} %stack.23.corner.refs_9_, f32[6,64,256]{2,1,0:T(8,128)S(1)} %add_chips.3.refs_0_, f32[6,64,256]{2,1,0:T(8,128)S(1)} %collective-permute-done.20.refs_1_, f32[10,64,256]{2,1,0:T(8,128)S(1)} %add_chips.4.refs_2_, f32[10,64,256]{2,1,0:T(8,128)S(1)} %collective-permute-done.23.refs_3_), custom_call_target="tpu_custom_call" | custom-call | flops 1 | bytes 1 | tf_op jit(solution)/shard_map/gather/pallas_call | solution.py:374
  114.0 5.5 %collective-permute-done.17.b = f32[8,64,256]{2,1,0:T(8,128)S(1)} collective-permute-done((f32[8,64,256]{2,1,0:T(8,128)S(1)}, f32[8,64,256]{2,1,0:T(8,128)S(1)}, u32[]{:S(2)}, u32[]{:S(2)}) %collective-permute-start.17) | collective-permute-done | bytes 524320 | tf_op jit(solution)/shard_map/ppermute | solution.py:414
  119.5 0.1 add_chips.5.refs_0_
  119.6 1.3 %collective-permute-start.24 = (f32[8,64,256]{2,1,0:T(8,128)S(1)}, f32[8,64,256]{2,1,0:T(8,128)S(1)}, u32[]{:S(2)}, u32[]{:S(2)}) collective-permute-start(f32[8,64,256]{2,1,0:T(8,128)S(1)} %add_chips.5.refs_0_), channel_id=1, source_target_pairs={{0,32},{32,0},{64,96},{96,64},{1,33},{33,1},{65,97},{97,65},{2,34}... | collective-permute-start | bytes 1572872 | tf_op jit(solution)/shard_map/ppermute | solution.py:417
  120.8 1.5 %collective-permute-done.24.refs_1_ = f32[8,64,256]{2,1,0:T(8,128)S(1)} collective-permute-done((f32[8,64,256]{2,1,0:T(8,128)S(1)}, f32[8,64,256]{2,1,0:T(8,128)S(1)}, u32[]{:S(2)}, u32[]{:S(2)}) %collective-permute-start.24) | collective-permute-done | bytes 524320 | tf_op jit(solution)/shard_map/ppermute | solution.py:417
  122.4 1.5 %gather.3 = f32[48,64,256]{2,1,0:T(8,128)} custom-call(s32[5]{0:T(128)S(1)} %stack.23.corner.refs_9_, f32[8,64,256]{2,1,0:T(8,128)S(1)} %add_chips.5.refs_0_, f32[8,64,256]{2,1,0:T(8,128)S(1)} %collective-permute-done.24.refs_1_, f32[48,64,256]{2,1,0:T(8,128)} %gather.2.rest_0_.refs_2_), custom_call_target="tpu_custom_call", output_to_operand_aliasing={{}: (3, {})} | custom-call | flops 1 | bytes 1 | tf_op jit(solution)/shard_map/gather/pallas_call | solution.py:374
  (14 shorter events, 0.1 us)
Async XLA Ops:
  0.8 13.1 %copy-start.2 = (s32[1,1024,3]{1,0,2:T(1,128)S(1)}, s32[1,1024,3]{1,0,2:T(1,128)}, u32[]{:S(2)}) copy-start(s32[1,1024,3]{1,0,2:T(1,128)} %param.18) | copy-start | bytes 36868
  0.8 13.1 %copy-start.1 = (f32[1,4,1024]{2,1,0:T(4,128)S(1)}, f32[1,4,1024]{2,1,0:T(4,128)}, u32[]{:S(2)}) copy-start(f32[1,4,1024]{2,1,0:T(4,128)} %param.16) | copy-start | bytes 49156
  3.1 14.9 %collective-permute-start = (f32[48,8,256]{2,1,0:T(8,128)S(1)}, f32[48,8,256]{2,1,0:T(8,128)S(1)}, u32[]{:S(2)}, u32[]{:S(2)}) collective-permute-start(f32[48,8,256]{2,1,0:T(8,128)S(1)} %get-tuple-element.61), channel_id=1, source_target_pairs={{0,1},{2,3},{4,5},{6,7},{8,9},{10,11},{12,13},{14,15},{16,17},{18,... | collective-permute-start | bytes 1179656 | tf_op jit(solution)/shard_map/ppermute | solution.py:396
  3.2 14.8 %collective-permute-start.1 = (f32[48,8,256]{2,1,0:T(8,128)S(1)}, f32[48,8,256]{2,1,0:T(8,128)S(1)}, u32[]{:S(2)}, u32[]{:S(2)}) collective-permute-start(f32[48,8,256]{2,1,0:T(8,128)S(1)} %get-tuple-element.62), channel_id=1, source_target_pairs={{1,2},{5,6},{9,10},{13,14},{17,18},{21,22},{25,26},{29,30},{2,1},{... | collective-permute-start | bytes 1179656 | tf_op jit(solution)/shard_map/ppermute | solution.py:396
  8.0 19.5 %collective-permute-start.2 = (f32[8,64,256]{2,1,0:T(8,128)S(1)}, f32[8,64,256]{2,1,0:T(8,128)S(1)}, u32[]{:S(2)}, u32[]{:S(2)}) collective-permute-start(f32[8,64,256]{2,1,0:T(8,128)S(1)} %get-tuple-element.65), channel_id=1, source_target_pairs={{4,8},{5,9},{6,10},{7,11},{12,16},{13,17},{14,18},{15,19},{20,24},... | collective-permute-start | bytes 1572872 | tf_op jit(solution)/shard_map/ppermute | solution.py:396
  13.1 14.4 %collective-permute-start.3 = (f32[8,64,256]{2,1,0:T(8,128)S(1)}, f32[8,64,256]{2,1,0:T(8,128)S(1)}, u32[]{:S(2)}, u32[]{:S(2)}) collective-permute-start(f32[8,64,256]{2,1,0:T(8,128)S(1)} %get-tuple-element.66), channel_id=1, source_target_pairs={{0,4},{1,5},{2,6},{3,7},{8,12},{9,13},{10,14},{11,15},{16,20},{17,... | collective-permute-start | bytes 1572872 | tf_op jit(solution)/shard_map/ppermute | solution.py:396
  13.9 4.1 %copy-start = (s32[1,3]{1,0:T(1,128)S(1)}, s32[1,3]{1,0:T(1,128)}, u32[]{:S(2)}) copy-start(s32[1,3]{1,0:T(1,128)} %refs_8_.15) | copy-start | bytes 40
  30.0 6.8 %collective-permute-start.4 = (f32[24,8,256]{2,1,0:T(8,128)S(1)}, f32[24,8,256]{2,1,0:T(8,128)S(1)}, u32[]{:S(2)}, u32[]{:S(2)}) collective-permute-start(f32[24,8,256]{2,1,0:T(8,128)S(1)} %get-tuple-element.78), channel_id=1, source_target_pairs={{0,1},{2,3},{4,5},{6,7},{8,9},{10,11},{12,13},{14,15},{16,17},{18,... | collective-permute-start | bytes 589832 | tf_op jit(solution)/shard_map/ppermute | solution.py:396
  30.1 6.8 %collective-permute-start.5 = (f32[24,8,256]{2,1,0:T(8,128)S(1)}, f32[24,8,256]{2,1,0:T(8,128)S(1)}, u32[]{:S(2)}, u32[]{:S(2)}) collective-permute-start(f32[24,8,256]{2,1,0:T(8,128)S(1)} %get-tuple-element.79), channel_id=1, source_target_pairs={{1,2},{5,6},{9,10},{13,14},{17,18},{21,22},{25,26},{29,30},{2,1},{... | collective-permute-start | bytes 589832 | tf_op jit(solution)/shard_map/ppermute | solution.py:396
  32.0 11.5 %collective-permute-start.6 = (f32[4,64,256]{2,1,0:T(8,128)S(1)}, f32[4,64,256]{2,1,0:T(8,128)S(1)}, u32[]{:S(2)}, u32[]{:S(2)}) collective-permute-start(f32[4,64,256]{2,1,0:T(8,128)S(1)} %get-tuple-element.80), channel_id=1, source_target_pairs={{4,8},{5,9},{6,10},{7,11},{12,16},{13,17},{14,18},{15,19},{20,24},... | collective-permute-start | bytes 786440 | tf_op jit(solution)/shard_map/ppermute | solution.py:396
  36.7 6.8 %collective-permute-start.7 = (f32[4,64,256]{2,1,0:T(8,128)S(1)}, f32[4,64,256]{2,1,0:T(8,128)S(1)}, u32[]{:S(2)}, u32[]{:S(2)}) collective-permute-start(f32[4,64,256]{2,1,0:T(8,128)S(1)} %get-tuple-element.81), channel_id=1, source_target_pairs={{0,4},{1,5},{2,6},{3,7},{8,12},{9,13},{10,14},{11,15},{16,20},{17,... | collective-permute-start | bytes 786440 | tf_op jit(solution)/shard_map/ppermute | solution.py:396
  45.2 7.4 %collective-permute-start.8 = (f32[24,8,256]{2,1,0:T(8,128)S(1)}, f32[24,8,256]{2,1,0:T(8,128)S(1)}, u32[]{:S(2)}, u32[]{:S(2)}) collective-permute-start(f32[24,8,256]{2,1,0:T(8,128)S(1)} %get-tuple-element.91), channel_id=1, source_target_pairs={{0,1},{2,3},{4,5},{6,7},{8,9},{10,11},{12,13},{14,15},{16,17},{18,... | collective-permute-start | bytes 589832 | tf_op jit(solution)/shard_map/ppermute | solution.py:396
  45.5 7.1 %collective-permute-start.9 = (f32[24,8,256]{2,1,0:T(8,128)S(1)}, f32[24,8,256]{2,1,0:T(8,128)S(1)}, u32[]{:S(2)}, u32[]{:S(2)}) collective-permute-start(f32[24,8,256]{2,1,0:T(8,128)S(1)} %get-tuple-element.92), channel_id=1, source_target_pairs={{1,2},{5,6},{9,10},{13,14},{17,18},{21,22},{25,26},{29,30},{2,1},{... | collective-permute-start | bytes 589832 | tf_op jit(solution)/shard_map/ppermute | solution.py:396
  48.7 10.7 %collective-permute-start.10 = (f32[4,64,256]{2,1,0:T(8,128)S(1)}, f32[4,64,256]{2,1,0:T(8,128)S(1)}, u32[]{:S(2)}, u32[]{:S(2)}) collective-permute-start(f32[4,64,256]{2,1,0:T(8,128)S(1)} %get-tuple-element.93), channel_id=1, source_target_pairs={{4,8},{5,9},{6,10},{7,11},{12,16},{13,17},{14,18},{15,19},{20,24},... | collective-permute-start | bytes 786440 | tf_op jit(solution)/shard_map/ppermute | solution.py:396
  52.5 6.9 %collective-permute-start.11 = (f32[4,64,256]{2,1,0:T(8,128)S(1)}, f32[4,64,256]{2,1,0:T(8,128)S(1)}, u32[]{:S(2)}, u32[]{:S(2)}) collective-permute-start(f32[4,64,256]{2,1,0:T(8,128)S(1)} %get-tuple-element.94), channel_id=1, source_target_pairs={{0,4},{1,5},{2,6},{3,7},{8,12},{9,13},{10,14},{11,15},{16,20},{17,... | collective-permute-start | bytes 786440 | tf_op jit(solution)/shard_map/ppermute | solution.py:396
  61.1 6.7 %collective-permute-start.12 = (f32[24,8,256]{2,1,0:T(8,128)S(1)}, f32[24,8,256]{2,1,0:T(8,128)S(1)}, u32[]{:S(2)}, u32[]{:S(2)}) collective-permute-start(f32[24,8,256]{2,1,0:T(8,128)S(1)} %get-tuple-element.100), channel_id=1, source_target_pairs={{0,1},{2,3},{4,5},{6,7},{8,9},{10,11},{12,13},{14,15},{16,17},{18,... | collective-permute-start | bytes 589832 | tf_op jit(solution)/shard_map/ppermute | solution.py:396
  61.2 6.6 %collective-permute-start.13 = (f32[24,8,256]{2,1,0:T(8,128)S(1)}, f32[24,8,256]{2,1,0:T(8,128)S(1)}, u32[]{:S(2)}, u32[]{:S(2)}) collective-permute-start(f32[24,8,256]{2,1,0:T(8,128)S(1)} %get-tuple-element.101), channel_id=1, source_target_pairs={{1,2},{5,6},{9,10},{13,14},{17,18},{21,22},{25,26},{29,30},{2,1},{... | collective-permute-start | bytes 589832 | tf_op jit(solution)/shard_map/ppermute | solution.py:396
  63.3 10.9 %collective-permute-start.14 = (f32[4,64,256]{2,1,0:T(8,128)S(1)}, f32[4,64,256]{2,1,0:T(8,128)S(1)}, u32[]{:S(2)}, u32[]{:S(2)}) collective-permute-start(f32[4,64,256]{2,1,0:T(8,128)S(1)} %get-tuple-element.102), channel_id=1, source_target_pairs={{4,8},{5,9},{6,10},{7,11},{12,16},{13,17},{14,18},{15,19},{20,24},... | collective-permute-start | bytes 786440 | tf_op jit(solution)/shard_map/ppermute | solution.py:396
  67.7 6.5 %collective-permute-start.15 = (f32[4,64,256]{2,1,0:T(8,128)S(1)}, f32[4,64,256]{2,1,0:T(8,128)S(1)}, u32[]{:S(2)}, u32[]{:S(2)}) collective-permute-start(f32[4,64,256]{2,1,0:T(8,128)S(1)} %get-tuple-element.103), channel_id=1, source_target_pairs={{0,4},{1,5},{2,6},{3,7},{8,12},{9,13},{10,14},{11,15},{16,20},{17,... | collective-permute-start | bytes 786440 | tf_op jit(solution)/shard_map/ppermute | solution.py:396
  76.3 7.5 %collective-permute-start.21 = (f32[10,64,256]{2,1,0:T(8,128)S(1)}, f32[10,64,256]{2,1,0:T(8,128)S(1)}, u32[]{:S(2)}, u32[]{:S(2)}) collective-permute-start(f32[10,64,256]{2,1,0:T(8,128)S(1)} %get-tuple-element.111.rest_0_), channel_id=1, source_target_pairs={{0,32},{32,0},{64,96},{96,64},{1,33},{33,1},{65,97},{97,65},{2,34}... | collective-permute-start | bytes 1966088 | tf_op jit(solution)/shard_map/ppermute | solution.py:408
  83.8 16.0 %collective-permute-start.22 = (f32[10,64,256]{2,1,0:T(8,128)S(1)}, f32[10,64,256]{2,1,0:T(8,128)S(1)}, u32[]{:S(2)}, u32[]{:S(2)}) collective-permute-start(f32[10,64,256]{2,1,0:T(8,128)S(1)} %add_cores.5.a), channel_id=1, source_target_pairs={{0,64},{32,96},{64,0},{96,32},{1,65},{33,97},{65,1},{97,33},{2,66}... | collective-permute-start | bytes 1966088 | tf_op jit(solution)/shard_map/ppermute | solution.py:414
  83.9 1.8 %collective-permute-start.18 = (f32[6,64,256]{2,1,0:T(8,128)S(1)}, f32[6,64,256]{2,1,0:T(8,128)S(1)}, u32[]{:S(2)}, u32[]{:S(2)}) collective-permute-start(f32[6,64,256]{2,1,0:T(8,128)S(1)} %get-tuple-element.110), channel_id=1, source_target_pairs={{0,32},{32,0},{64,96},{96,64},{1,33},{33,1},{65,97},{97,65},{2,34}... | collective-permute-start | bytes 1179656 | tf_op jit(solution)/shard_map/ppermute | solution.py:408
  84.4 17.6 %collective-permute-start.16 = (f32[8,64,256]{2,1,0:T(8,128)S(1)}, f32[8,64,256]{2,1,0:T(8,128)S(1)}, u32[]{:S(2)}, u32[]{:S(2)}) collective-permute-start(f32[8,64,256]{2,1,0:T(8,128)S(1)} %get-tuple-element.108), channel_id=1, source_target_pairs={{0,32},{32,0},{64,96},{96,64},{1,33},{33,1},{65,97},{97,65},{2,34}... | collective-permute-start | bytes 1572872 | tf_op jit(solution)/shard_map/ppermute | solution.py:408
  85.8 22.5 %collective-permute-start.19 = (f32[6,64,256]{2,1,0:T(8,128)S(1)}, f32[6,64,256]{2,1,0:T(8,128)S(1)}, u32[]{:S(2)}, u32[]{:S(2)}) collective-permute-start(f32[6,64,256]{2,1,0:T(8,128)S(1)} %add_cores.4.a), channel_id=1, source_target_pairs={{0,64},{32,96},{64,0},{96,32},{1,65},{33,97},{65,1},{97,33},{2,66}... | collective-permute-start | bytes 1179656 | tf_op jit(solution)/shard_map/ppermute | solution.py:414
  99.9 12.2 %collective-permute-start.23 = (f32[10,64,256]{2,1,0:T(8,128)S(1)}, f32[10,64,256]{2,1,0:T(8,128)S(1)}, u32[]{:S(2)}, u32[]{:S(2)}) collective-permute-start(f32[10,64,256]{2,1,0:T(8,128)S(1)} %add_chips.4.refs_2_), channel_id=1, source_target_pairs={{0,32},{32,0},{64,96},{96,64},{1,33},{33,1},{65,97},{97,65},{2,34}... | collective-permute-start | bytes 1966088 | tf_op jit(solution)/shard_map/ppermute | solution.py:417
  102.1 17.4 %collective-permute-start.17 = (f32[8,64,256]{2,1,0:T(8,128)S(1)}, f32[8,64,256]{2,1,0:T(8,128)S(1)}, u32[]{:S(2)}, u32[]{:S(2)}) collective-permute-start(f32[8,64,256]{2,1,0:T(8,128)S(1)} %add_cores.3.a), channel_id=1, source_target_pairs={{0,64},{32,96},{64,0},{96,32},{1,65},{33,97},{65,1},{97,33},{2,66}... | collective-permute-start | bytes 1572872 | tf_op jit(solution)/shard_map/ppermute | solution.py:414
  108.3 3.8 %collective-permute-start.20 = (f32[6,64,256]{2,1,0:T(8,128)S(1)}, f32[6,64,256]{2,1,0:T(8,128)S(1)}, u32[]{:S(2)}, u32[]{:S(2)}) collective-permute-start(f32[6,64,256]{2,1,0:T(8,128)S(1)} %add_chips.3.refs_0_), channel_id=1, source_target_pairs={{0,32},{32,0},{64,96},{96,64},{1,33},{33,1},{65,97},{97,65},{2,34}... | collective-permute-start | bytes 1179656 | tf_op jit(solution)/shard_map/ppermute | solution.py:417
  119.6 2.8 %collective-permute-start.24 = (f32[8,64,256]{2,1,0:T(8,128)S(1)}, f32[8,64,256]{2,1,0:T(8,128)S(1)}, u32[]{:S(2)}, u32[]{:S(2)}) collective-permute-start(f32[8,64,256]{2,1,0:T(8,128)S(1)} %add_chips.5.refs_0_), channel_id=1, source_target_pairs={{0,32},{32,0},{64,96},{96,64},{1,33},{33,1},{65,97},{97,65},{2,34}... | collective-permute-start | bytes 1572872 | tf_op jit(solution)/shard_map/ppermute | solution.py:417

commit v5 on v4

--- a/solution.py
+++ b/solution.py
@@ -93,7 +93,7 @@
         second_ref[offset + i] = jnp.where(odd_tile, high, low)
         return carry
 
-    lax.fori_loop(0, lowest.shape[0] // 2, body, 0, unroll=4)
+    lax.fori_loop(0, lowest.shape[0] // 2, body, 0, unroll=8)
 
 
 def strips_kernel(q, b, corner, xa, xb, ya, yb, rows, sems):
@@ -124,8 +124,11 @@
     count = (len(refs) - 3) // 2
     sources, targets = refs[:count], refs[count + 1 : 2 * count + 1]
     out, (weights, sems) = refs[count], refs[2 * count + 1 :]
-    sources = [a if a.shape == b.shape else a.at[0] for a, b in zip(sources, targets)]
-    copies = [pltpu.make_async_copy(a, b, sems.at[n]) for n, (a, b) in enumerate(zip(sources, targets))]
+    pairs = list(zip(sources, targets))
+    whole, (previous, stiff, snaps) = pairs[:-3], pairs[-3:]
+    first = slice(0, RADIUS + G)
+    pairs = whole + [(a.at[first], b.at[first]) for a, b in (previous, stiff, (snaps[0].at[0], snaps[1]))]
+    copies = [pltpu.make_async_copy(a, b, sems.at[n]) for n, (a, b) in enumerate(pairs)]
     for copy in copies:
         copy.start()
     size_x, size_y, lanes = out.shape
@@ -190,15 +193,13 @@
                 coef[3][(base + g,) + at] = t * zs[(g,) + at]
 
 
-def advance(base, count, plane, r, step, q, p, out, ya, yb, ymat, zmat, ys, zs, coef, inject, snap, image, scale):
-    size_y = r["size_y"]
+def products(base, count, r, q, ya, yb, ymat, zmat, ys, zs):
     for g in range(count):
         high, low = parts(q[base + g])
         if g % 2 == 0:
             hh, hl = halo_parts(ya, yb, (base + g) // 2)
         ys[g] = dot(ymat[r["variant"] + g % 2], jnp.concatenate([high, low, hh, hl], axis=0))
         zs[g] = dot(jnp.concatenate([high, low], axis=1), zmat[...])
-    elementwise(base, count, plane, r, step, q, p, out, ys, zs, coef, inject, snap, image, scale)
 
 
 def elementwise(base, count, plane, r, step, q, p, out, ys, zs, coef, inject, snap, image, scale):
@@ -268,7 +269,7 @@
         copy.start()
 
     def inflow(start, size, n):
-        pairs = ((r["p_far"], r["p"]), (r["stiff_far"], r["stiff"]))
+        pairs = ((r["p_far"], r["p"]), (r["stiff_far"], r["stiff"]), (r["snaps"].at[0], r["snap"]))
         at = pl.ds(start, size)
         return [pltpu.make_async_copy(a.at[at], b.at[at], r["sems"].at[k, n]) for k, (a, b) in enumerate(pairs)]
 
@@ -276,9 +277,9 @@
     if "sems" in r:
         low, high = ranges[0]
         groups = (high - low) // G
-        for i in range(groups):
+        for i in range(1, groups):
             arriving += inflow(low + i * G, G, i)
-        arriving += inflow(0, RADIUS, groups) + inflow(high, RADIUS, groups + 1)
+        arriving += inflow(high, RADIUS, groups)
         for copy_in in arriving:
             copy_in.start()
 
@@ -293,34 +294,46 @@
 
         return plane
 
-    def group(base, count):
+    def prepare(base, count):
         if step == 0:
             make_coefficients(
                 base, count, reader(r["buoy"], base, RADIUS), r, *common, r["stiff"], r["buoy"], coef, scale
             )
-        advance(
-            base, count, reader(q, base, 0), r, step, q, r["p"], r["out"], *common, coef, r["inject"], r["snap"],
-            r["image"], scale
-        )
+
+    def advance(bases, count):
+        slots = [(r["ys"].at[n * count : (n + 1) * count], r["zs"].at[n * count : (n + 1) * count]) for n in range(len(bases))]
+        for base, slot in zip(bases, slots):
+            products(base, count, r, q, *common[:4], *slot)
+        for base, slot in zip(bases, slots):
+            elementwise(
+                base, count, reader(q, base, 0), r, step, q, r["p"], r["out"], *slot, coef, r["inject"], r["snap"],
+                r["image"], scale
+            )
 
     for low, high in ranges:
         count = G if (high - low) % G == 0 else 4
 
         def body(i, carry):
             if arriving:
-                for copy_in in inflow(low + i * count, count, i):
-                    copy_in.wait()
-            group(low + i * count, count)
+
+                @pl.when(i > 0)
+                def _():
+                    for copy_in in inflow(low + i * count, count, i):
+                        copy_in.wait()
+
+            prepare(low + i * count, count)
+            advance([low + i * count], count)
             return carry
 
         lax.fori_loop(0, (high - low) // count, body, 0)
-    for copy_in in arriving[-4:]:
+    for copy_in in arriving[-3:]:
         copy_in.wait()
     if edges:
         r["halo"][corner[3]] = r["xa"][...]
         r["halo"][1 - corner[3]] = r["xb"][...]
-        group(0, RADIUS)
-        group(size_x - RADIUS, RADIUS)
+        prepare(0, RADIUS)
+        prepare(size_x - RADIUS, RADIUS)
+        advance([0, size_x - RADIUS], RADIUS)
         ranges = ranges + [(0, RADIUS), (size_x - RADIUS, size_x)]
     if step == STEPS - 1:
         mute(r["image"], r["source"], corner, ranges)
@@ -432,28 +445,28 @@
         scratch=[pltpu.VMEM((2, 2, size_x, 8, size_z), F32), pltpu.SemaphoreType.DMA((8,))],
     )
     halos = exchange(strips)
-    fetched = [wave_now[0, 0], buoyancy[0], ymat, zmat, snaps]
+    fetched = [wave_now[0, 0], buoyancy[0], ymat, zmat, wave_prev[0, 0], stiffness[0], snaps]
     shapes = [a.shape for a in fetched[:-1]] + [grid]
     args = [places, traces[0], aperture, corner] + fetched
-    inject, q, buoy, ymat, zmat, snap = call(
+    inject, q, buoy, ymat, zmat, p, stiff, snap = call(
         fetch_kernel, "fetch", args, [VMEM, VMEM, SMEM, SMEM] + [HBM] * len(fetched),
         [(size_x, size_y, 128)] + [pltpu.VMEM(shape, a.dtype) for shape, a in zip(shapes, fetched)],
         scratch=[pltpu.VMEM((traces.shape[2], 128), BF16), pltpu.SemaphoreType.DMA((len(fetched),))],
     )
 
     held = dict(inject=inject, ymat=ymat, zmat=zmat, openness=aperture, source=sources, corner=corner, snaps=snaps)
-    held.update(q=q, buoy=buoy, snap=snap, p_far=wave_prev[0, 0], stiff_far=stiffness[0])
+    held.update(q=q, buoy=buoy, p=p, stiff=stiff, snap=snap, p_far=wave_prev[0, 0], stiff_far=stiffness[0])
     places_of = dict(openness=SMEM, source=SMEM, corner=SMEM, snaps=HBM, p_far=HBM, stiff_far=HBM)
 
     def run(step, ranges, edges, started, extra, splits=(), weight=1):
         ahead = not edges and step < STEPS - 1
         fresh = step == 0 and not edges
-        ins = ["q", "snap", "inject", "ya", "yb", "ymat", "zmat", "openness", "source", "corner"]
+        ins = ["q", "inject", "ya", "yb", "ymat", "zmat", "openness", "source", "corner"]
         ins += (["xa", "xb"] if edges else []) + (["snaps"] if ahead else [])
-        ins += ["p_far", "stiff_far"] if fresh else ["p"]
+        ins += ["p_far", "stiff_far"] if fresh else ["p", "snap"]
         ins += ["buoy"] if step == 0 else ["c0", "c1", "c2", "c3"]
         ins += ["stiff"] if step == 0 and edges else []
-        results = ["out", "image"] + (["c0", "c1", "c2", "c3"] if step == 0 else []) + (["p", "stiff"] if fresh else [])
+        results = ["out", "image"] + (["c0", "c1", "c2", "c3"] if step == 0 else []) + (["p", "stiff", "snap"] if fresh else [])
         given = [n for n in results if n in started]
         extra = dict(extra)
         scratch = dict(
@@ -463,14 +476,14 @@
             extra["snap_next"] = pltpu.VMEM(grid, snaps.dtype)
             scratch["sem"] = pltpu.SemaphoreType.DMA
         if fresh:
-            scratch["sems"] = pltpu.SemaphoreType.DMA((2, size_x // G + 1))
+            scratch["sems"] = pltpu.SemaphoreType.DMA((3, size_x // G))
         if edges:
             scratch["halo"] = pltpu.VMEM((2,) + held["xa"].shape, F32)
         names = ins + [n + "_in" for n in given] + results + list(extra) + list(scratch)
         outs = call(
             functools.partial(step_kernel, step, ranges, edges, splits, names), "step%d" % step,
             [held[n] for n in ins + given], [places_of.get(n, VMEM) for n in ins + given],
-            [grid] * len(results) + list(extra.values()),
+            [pltpu.VMEM(grid, held[n].dtype if n == "snap" else F32) for n in results] + list(extra.values()),
             {len(ins) + i: results.index(n) for i, n in enumerate(given)}, scratch.values(), weight,
         )
         held.update(zip(results, outs))
@@ -481,7 +494,7 @@
     first = ("out", "image", "c0", "c1", "c2", "c3")
     for step in range(STEPS - 1):
         held.update(zip(("xa", "xb", "ya", "yb"), halos))
-        (snap_next,) = run(step, inner, False, ("image",) if step else (), {}, weight=4 << 30)
+        (snap_next,) = run(step, inner, False, ("image",) if step else ("p", "stiff", "snap"), {}, weight=4 << 30)
         extra = dict(sxa=strip_x, sxb=strip_x, sya=strip_y, syb=strip_y)
         halos = exchange(run(step, [], True, first if step == 0 else ("out", "image"), extra))
         held.update(q=held["out"], p=held["q"], snap=snap_next)

time: 125 us -> 124 us (level)
  transfers between devices with their start and end apart: 25 -> 25, of which waited for: 8 -> 9; matrix products, arithmetic and copies ran while one was open for 0% -> 0% of each run, Pallas kernels for 29% -> 28%
where the time goes in v5:
time: 124 us; the launch traced here: 123 us
  Pallas kernels  46.6 us (38%)
  starting transfers between devices  44 us (35%)
  waiting for transfers between devices  30.5 us (25%)
  between operations  1.9 us (2%)
    pallas_call x19, Pallas kernels, call(): pl.pallas_call(kernel, name=name, in_specs=specs, out_specs=[pl.BlockSpec...  46.6 us
    ppermute x16, starting transfers between devices, swap(): return lax.ppermute(strip, 'dom', pairs + [(b, a) for a, b in pairs])  30.4 us
    ppermute x3, waiting for transfers between devices, add_chips(): arrived = lax.ppermute(mine, 'shot', CHIPS)  24 us
    ppermute x3, starting transfers between devices, add_cores(): arrived = lax.ppermute(sent, 'shot', CORES)  6.26 us
    ppermute x3, starting transfers between devices, add_chips(): return (mine, lax.ppermute(mine, 'shot', CORES))  5.44 us
    ppermute x3, waiting for transfers between devices, add_cores(): arrived = lax.ppermute(sent, 'shot', CORES)  2.94 us
  transfers between devices with their start and end apart: 25, of which 9 were waited for; matrix products, arithmetic and copies ran while one was open for 0% of the time, Pallas kernels for 28%

profile of v5, /device:TPU:57, one launch (start us, length us, event | category | flops | bytes accessed | tf_op | source)
XLA Modules:
  0.0 123.1 jit_solution(1382838917527019632)
XLA Ops:
  0.7 0.1 stack.23.corner.refs_8_
  0.8 2.3 %strips.1 = (f32[8,64,256]{2,1,0:T(8,128)S(1)}, f32[8,64,256]{2,1,0:T(8,128)S(1)}, f32[48,8,256]{2,1,0:T(8,128)S(1)}, f32[48,8,256]{2,1,0:T(8,128)S(1)}) custom-call(f32[48,64,256]{2,1,0:T(8,128)} %bitcast.29, f32[48,64,256]{2,1,0:T(8,128)} %bitcast.31, s32[5]{0:T(128)S(1)} %stack.23.corner.refs_8_), custom_call_target="tpu_custom_call" | custom-call | flops 1 | bytes 1 | tf_op jit(solution)/shard_map/strips/pallas_call | solution.py:387
  3.1 0.1 collective-permute-start
  3.2 4.9 %collective-permute-start.1 = (f32[48,8,256]{2,1,0:T(8,128)S(1)}, f32[48,8,256]{2,1,0:T(8,128)S(1)}, u32[]{:S(2)}, u32[]{:S(2)}) collective-permute-start(f32[48,8,256]{2,1,0:T(8,128)S(1)} %get-tuple-element.64), channel_id=1, source_target_pairs={{1,2},{5,6},{9,10},{13,14},{17,18},{21,22},{25,26},{29,30},{2,1},{... | collective-permute-start | bytes 1179656 | tf_op jit(solution)/shard_map/ppermute | solution.py:409
  8.0 5.1 %collective-permute-start.2 = (f32[8,64,256]{2,1,0:T(8,128)S(1)}, f32[8,64,256]{2,1,0:T(8,128)S(1)}, u32[]{:S(2)}, u32[]{:S(2)}) collective-permute-start(f32[8,64,256]{2,1,0:T(8,128)S(1)} %get-tuple-element.67), channel_id=1, source_target_pairs={{4,8},{5,9},{6,10},{7,11},{12,16},{13,17},{14,18},{15,19},{20,24},... | collective-permute-start | bytes 1572872 | tf_op jit(solution)/shard_map/ppermute | solution.py:409
  13.1 0.1 collective-permute-start.3
  13.9 0.0 copy-start
  13.9 4.1 %fetch.1 = (f32[48,64,128]{2,1,0:T(8,128)S(1)}, f32[48,64,256]{2,1,0:T(8,128)S(1)}, f32[48,64,256]{2,1,0:T(8,128)S(1)}, bf16[4,128,160]{2,1,0:T(8,128)(2,1)S(1)}...) custom-call(s32[3,1,1024]{2,1,0:T(1,128)S(1)} %broadcast_in_dim.9.pl, ...), custom_call_target="tpu_custom_call" | custom-call | flops 1 | bytes 1 | tf_op jit(solution)/shard_map/fetch/pallas_call | solution.py:387
  18.0 0.0 collective-permute-done.refs_2_
  18.0 0.0 collective-permute-done.1.refs_3_
  18.1 8.6 %step0.2 = (f32[48,64,256]{2,1,0:T(8,128)S(1)}, f32[48,64,256]{2,1,0:T(8,128)S(1)}, f32[48,64,256]{2,1,0:T(8,128)S(1)}, f32[48,64,256]{2,1,0:T(8,128)S(1)}, f32[...) custom-call(f32[48,64,256]{2,1,0:T(8,128)S(1)} %get-tuple-element.61, ...), custom_call_target="tpu_custom_call", output_to_operand_aliasing={{6}: (13, {}), {7}: (14, {}), {8}: (15, {})} | custom-call | flops 4294967296 | bytes 1 | tf_op jit(solution)/shard_map/step0/pallas_call | solution.py:387
  26.7 0.0 collective-permute-done.2.refs_9_
  26.7 0.0 collective-permute-done.3.refs_10_
  26.7 2.3 %step0.3 = (f32[48,64,256]{2,1,0:T(8,128)S(1)}, f32[48,64,256]{2,1,0:T(8,128)S(1)}, f32[48,64,256]{2,1,0:T(8,128)S(1)}, f32[48,64,256]{2,1,0:T(8,128)S(1)}, f32[...) custom-call(f32[48,64,256]{2,1,0:T(8,128)S(1)} %get-tuple-element.61, ...), custom_call_target="tpu_custom_call", output_to_operand_aliasing={{0}: (15, {}), {1}: (16, {}), {2}: (17, {}), {3}: (18, {}),... | custom-call | flops 1 | bytes 1 | tf_op jit(solution)/shard_map/step0/pallas_call | solution.py:387
  29.0 0.1 collective-permute-start.4
  29.1 1.9 %collective-permute-start.5 = (f32[24,8,256]{2,1,0:T(8,128)S(1)}, f32[24,8,256]{2,1,0:T(8,128)S(1)}, u32[]{:S(2)}, u32[]{:S(2)}) collective-permute-start(f32[24,8,256]{2,1,0:T(8,128)S(1)} %get-tuple-element.84), channel_id=1, source_target_pairs={{1,2},{5,6},{9,10},{13,14},{17,18},{21,22},{25,26},{29,30},{2,1},{... | collective-permute-start | bytes 589832 | tf_op jit(solution)/shard_map/ppermute | solution.py:409
  31.0 4.6 %collective-permute-start.6 = (f32[4,64,256]{2,1,0:T(8,128)S(1)}, f32[4,64,256]{2,1,0:T(8,128)S(1)}, u32[]{:S(2)}, u32[]{:S(2)}) collective-permute-start(f32[4,64,256]{2,1,0:T(8,128)S(1)} %get-tuple-element.85), channel_id=1, source_target_pairs={{4,8},{5,9},{6,10},{7,11},{12,16},{13,17},{14,18},{15,19},{20,24},... | collective-permute-start | bytes 786440 | tf_op jit(solution)/shard_map/ppermute | solution.py:409
  35.7 0.1 collective-permute-start.7
  35.8 0.0 collective-permute-done.4.refs_2_
  35.8 0.1 collective-permute-done.5.refs_3_
  35.9 5.9 %step1.2 = (f32[48,64,256]{2,1,0:T(8,128)S(1)}, f32[48,64,256]{2,1,0:T(8,128)S(1)}, bf16[48,64,256]{2,1,0:T(8,128)(2,1)S(1)}) custom-call(f32[48,64,256]{2,1,0:T(8,128)S(1)} %get-tuple-element.82.refs_0_.refs_10_.refs_11_, f32[48,64,128]{2,1,0:T(8,128)S(1)} %get-tuple-element.62.refs_1_, ...), custom_call_target="tpu_custom_call", output_to_operand_aliasing={{1}: (16, {})} | custom-call | flops 4294967296 | bytes 1 | tf_op jit(solution)/shard_map/step1/pallas_call | solution.py:387
  41.8 0.8 collective-permute-done.6.refs_9_
  42.6 1.7 %step1.3 = (f32[48,64,256]{2,1,0:T(8,128)S(1)}, f32[48,64,256]{2,1,0:T(8,128)S(1)}, f32[4,64,256]{2,1,0:T(8,128)S(1)}, f32[4,64,256]{2,1,0:T(8,128)S(1)}, f32[24...) custom-call(f32[48,64,256]{2,1,0:T(8,128)S(1)} %get-tuple-element.82.refs_0_.refs_1, ...), custom_call_target="tpu_custom_call", output_to_operand_aliasing={{0}: (17, {}), {1}: (18, {})} | custom-call | flops 1 | bytes 1 | tf_op jit(solution)/shard_map/step1/pallas_call | solution.py:387
  44.3 0.2 collective-permute-start.8
  44.5 3.2 %collective-permute-start.9 = (f32[24,8,256]{2,1,0:T(8,128)S(1)}, f32[24,8,256]{2,1,0:T(8,128)S(1)}, u32[]{:S(2)}, u32[]{:S(2)}) collective-permute-start(f32[24,8,256]{2,1,0:T(8,128)S(1)} %get-tuple-element.97), channel_id=1, source_target_pairs={{1,2},{5,6},{9,10},{13,14},{17,18},{21,22},{25,26},{29,30},{2,1},{... | collective-permute-start | bytes 589832 | tf_op jit(solution)/shard_map/ppermute | solution.py:409
  47.7 3.5 %collective-permute-start.10 = (f32[4,64,256]{2,1,0:T(8,128)S(1)}, f32[4,64,256]{2,1,0:T(8,128)S(1)}, u32[]{:S(2)}, u32[]{:S(2)}) collective-permute-start(f32[4,64,256]{2,1,0:T(8,128)S(1)} %get-tuple-element.98), channel_id=1, source_target_pairs={{4,8},{5,9},{6,10},{7,11},{12,16},{13,17},{14,18},{15,19},{20,24},... | collective-permute-start | bytes 786440 | tf_op jit(solution)/shard_map/ppermute | solution.py:409
  51.2 0.1 collective-permute-start.11
  51.3 6.0 %step2.2 = (f32[48,64,256]{2,1,0:T(8,128)S(1)}, f32[48,64,256]{2,1,0:T(8,128)S(1)}, bf16[48,64,256]{2,1,0:T(8,128)(2,1)S(1)}) custom-call(f32[48,64,256]{2,1,0:T(8,128)S(1)} %get-tuple-element.95.refs_0_.refs_9_.refs_11_, f32[48,64,128]{2,1,0:T(8,128)S(1)} %get-tuple-element.62.refs_1_, ...), custom_call_target="tpu_custom_call", output_to_operand_aliasing={{1}: (16, {})} | custom-call | flops 4294967296 | bytes 1 | tf_op jit(solution)/shard_map/step2/pallas_call | solution.py:387
  57.3 1.1 collective-permute-done.10.refs_9_
  58.4 0.0 collective-permute-done.11.refs_10_
  58.4 1.7 %step2.3 = (f32[48,64,256]{2,1,0:T(8,128)S(1)}, f32[48,64,256]{2,1,0:T(8,128)S(1)}, f32[4,64,256]{2,1,0:T(8,128)S(1)}, f32[4,64,256]{2,1,0:T(8,128)S(1)}, f32[24...) custom-call(f32[48,64,256]{2,1,0:T(8,128)S(1)} %get-tuple-element.95.refs_0_.refs_9, ...), custom_call_target="tpu_custom_call", output_to_operand_aliasing={{0}: (17, {}), {1}: (18, {})} | custom-call | flops 1 | bytes 1 | tf_op jit(solution)/shard_map/step2/pallas_call | solution.py:387
  60.2 0.1 collective-permute-start.12
  60.2 2.1 %collective-permute-start.13 = (f32[24,8,256]{2,1,0:T(8,128)S(1)}, f32[24,8,256]{2,1,0:T(8,128)S(1)}, u32[]{:S(2)}, u32[]{:S(2)}) collective-permute-start(f32[24,8,256]{2,1,0:T(8,128)S(1)} %get-tuple-element.106), channel_id=1, source_target_pairs={{1,2},{5,6},{9,10},{13,14},{17,18},{21,22},{25,26},{29,30},{2,1},{... | collective-permute-start | bytes 589832 | tf_op jit(solution)/shard_map/ppermute | solution.py:409
  62.3 4.4 %collective-permute-start.14 = (f32[4,64,256]{2,1,0:T(8,128)S(1)}, f32[4,64,256]{2,1,0:T(8,128)S(1)}, u32[]{:S(2)}, u32[]{:S(2)}) collective-permute-start(f32[4,64,256]{2,1,0:T(8,128)S(1)} %get-tuple-element.107), channel_id=1, source_target_pairs={{4,8},{5,9},{6,10},{7,11},{12,16},{13,17},{14,18},{15,19},{20,24},... | collective-permute-start | bytes 786440 | tf_op jit(solution)/shard_map/ppermute | solution.py:409
  66.7 0.1 collective-permute-start.15
  66.8 0.0 collective-permute-done.12.refs_2_
  66.8 6.5 %step3.2 = (f32[48,64,256]{2,1,0:T(8,128)S(1)}, f32[48,64,256]{2,1,0:T(8,128)S(1)}, f32[6,64,256]{2,1,0:T(8,128)S(1)}, f32[6,64,256]{2,1,0:T(8,128)S(1)}) custom-call(f32[48,64,256]{2,1,0:T(8,128)S(1)} %get-tuple-element.104.refs_0_, f32[48,64,128]{2,1,0:T(8,128)S(1)} %get-tuple-element.62.refs_1_, ...), custom_call_target="tpu_custom_call", output_to_operand_aliasing={{1}: (15, {})} | custom-call | flops 4294967296 | bytes 1 | tf_op jit(solution)/shard_map/step3/pallas_call | solution.py:387
  73.3 0.0 collective-permute-done.14.refs_9_
  73.3 0.0 collective-permute-done.15.refs_10_
  73.3 2.0 %step3.3 = (f32[48,64,256]{2,1,0:T(8,128)S(1)}, f32[48,64,256]{2,1,0:T(8,128)S(1)}, f32[10,64,256]{2,1,0:T(8,128)S(1)}, f32[10,64,256]{2,1,0:T(8,128)S(1)}, f32[...) custom-call(f32[48,64,256]{2,1,0:T(8,128)S(1)} %get-tuple-element.104.refs_0_, ...), custom_call_target="tpu_custom_call", output_to_operand_aliasing={{0}: (17, {}), {1}: (18, {})} | custom-call | flops 4294967296 | bytes 1 | tf_op jit(solution)/shard_map/step3/pallas_call | solution.py:387
  75.4 5.7 %collective-permute-start.21 = (f32[10,64,256]{2,1,0:T(8,128)S(1)}, f32[10,64,256]{2,1,0:T(8,128)S(1)}, u32[]{:S(2)}, u32[]{:S(2)}) collective-permute-start(f32[10,64,256]{2,1,0:T(8,128)S(1)} %get-tuple-element.117.rest_0_), channel_id=1, source_target_pairs={{0,32},{32,0},{64,96},{96,64},{1,33},{33,1},{65,97},{97,65},{2,34}... | collective-permute-start | bytes 1966088 | tf_op jit(solution)/shard_map/ppermute | solution.py:421
  81.0 1.7 %collective-permute-done.21.b = f32[10,64,256]{2,1,0:T(8,128)S(1)} collective-permute-done((f32[10,64,256]{2,1,0:T(8,128)S(1)}, f32[10,64,256]{2,1,0:T(8,128)S(1)}, u32[]{:S(2)}, u32[]{:S(2)}) %collective-permute-start.21) | collective-permute-done | bytes 655392 | tf_op jit(solution)/shard_map/ppermute | solution.py:421
  82.8 0.1 add_cores.5.a
  82.9 0.1 collective-permute-start.22
  83.0 0.5 collective-permute-start.18
  83.4 0.1 collective-permute-start.16
  83.5 1.2 collective-permute-done.18.b
  84.8 1.7 %collective-permute-start.19 = (f32[6,64,256]{2,1,0:T(8,128)S(1)}, f32[6,64,256]{2,1,0:T(8,128)S(1)}, u32[]{:S(2)}, u32[]{:S(2)}) collective-permute-start(f32[6,64,256]{2,1,0:T(8,128)S(1)} %add_cores.4.a), channel_id=1, source_target_pairs={{0,64},{32,96},{64,0},{96,32},{1,65},{33,97},{65,1},{97,33},{2,66}... | collective-permute-start | bytes 1179656 | tf_op jit(solution)/shard_map/ppermute | solution.py:427
  86.5 12.4 %collective-permute-done.22.b = f32[10,64,256]{2,1,0:T(8,128)S(1)} collective-permute-done((f32[10,64,256]{2,1,0:T(8,128)S(1)}, f32[10,64,256]{2,1,0:T(8,128)S(1)}, u32[]{:S(2)}, u32[]{:S(2)}) %collective-permute-start.22) | collective-permute-done | bytes 655392 | tf_op jit(solution)/shard_map/ppermute | solution.py:427
  98.9 0.1 add_chips.4.refs_2_
  99.0 2.1 %collective-permute-start.23 = (f32[10,64,256]{2,1,0:T(8,128)S(1)}, f32[10,64,256]{2,1,0:T(8,128)S(1)}, u32[]{:S(2)}, u32[]{:S(2)}) collective-permute-start(f32[10,64,256]{2,1,0:T(8,128)S(1)} %add_chips.4.refs_2_), channel_id=1, source_target_pairs={{0,32},{32,0},{64,96},{96,64},{1,33},{33,1},{65,97},{97,65},{2,34}... | collective-permute-start | bytes 1966088 | tf_op jit(solution)/shard_map/ppermute | solution.py:430
  101.0 0.1 add_cores.3.a
  101.1 0.1 collective-permute-start.17
  101.2 6.1 %collective-permute-done.19.b = f32[6,64,256]{2,1,0:T(8,128)S(1)} collective-permute-done((f32[6,64,256]{2,1,0:T(8,128)S(1)}, f32[6,64,256]{2,1,0:T(8,128)S(1)}, u32[]{:S(2)}, u32[]{:S(2)}) %collective-permute-start.19) | collective-permute-done | bytes 393248 | tf_op jit(solution)/shard_map/ppermute | solution.py:427
  107.4 2.1 %collective-permute-start.20 = (f32[6,64,256]{2,1,0:T(8,128)S(1)}, f32[6,64,256]{2,1,0:T(8,128)S(1)}, u32[]{:S(2)}, u32[]{:S(2)}) collective-permute-start(f32[6,64,256]{2,1,0:T(8,128)S(1)} %add_chips.3.refs_0_), channel_id=1, source_target_pairs={{0,32},{32,0},{64,96},{96,64},{1,33},{33,1},{65,97},{97,65},{2,34}... | collective-permute-start | bytes 1179656 | tf_op jit(solution)/shard_map/ppermute | solution.py:430
  109.4 1.7 %store.1.rest_1_ = f32[48,64,256]{2,1,0:T(8,128)} custom-call(f32[48,64,256]{2,1,0:T(8,128)S(1)} %get-tuple-element.119.source), custom_call_target="tpu_custom_call" | custom-call | flops 1 | bytes 1 | tf_op jit(solution)/shard_map/store/pallas_call | solution.py:387
  111.1 0.0 collective-permute-done.20.refs_1_
  111.1 0.0 collective-permute-done.23.refs_3_
  111.1 1.9 %gather.2.rest_0_.refs_2_ = f32[48,64,256]{2,1,0:T(8,128)} custom-call(s32[5]{0:T(128)S(1)} %stack.23.corner.refs_8_, f32[6,64,256]{2,1,0:T(8,128)S(1)} %add_chips.3.refs_0_, f32[6,64,256]{2,1,0:T(8,128)S(1)} %collective-permute-done.20.refs_1_, f32[10,64,256]{2,1,0:T(8,128)S(1)} %add_chips.4.refs_2_, f32[10,64,256]{2,1,0:T(8,128)S(1)} %collective-permute-done.23.refs_3_), custom_call_target="tpu_custom_call" | custom-call | flops 1 | bytes 1 | tf_op jit(solution)/shard_map/gather/pallas_call | solution.py:387
  113.0 5.5 %collective-permute-done.17.b = f32[8,64,256]{2,1,0:T(8,128)S(1)} collective-permute-done((f32[8,64,256]{2,1,0:T(8,128)S(1)}, f32[8,64,256]{2,1,0:T(8,128)S(1)}, u32[]{:S(2)}, u32[]{:S(2)}) %collective-permute-start.17) | collective-permute-done | bytes 524320 | tf_op jit(solution)/shard_map/ppermute | solution.py:427
  118.5 0.1 add_chips.5.refs_0_
  118.6 1.3 %collective-permute-start.24 = (f32[8,64,256]{2,1,0:T(8,128)S(1)}, f32[8,64,256]{2,1,0:T(8,128)S(1)}, u32[]{:S(2)}, u32[]{:S(2)}) collective-permute-start(f32[8,64,256]{2,1,0:T(8,128)S(1)} %add_chips.5.refs_0_), channel_id=1, source_target_pairs={{0,32},{32,0},{64,96},{96,64},{1,33},{33,1},{65,97},{97,65},{2,34}... | collective-permute-start | bytes 1572872 | tf_op jit(solution)/shard_map/ppermute | solution.py:430
  119.9 1.5 %collective-permute-done.24.refs_1_ = f32[8,64,256]{2,1,0:T(8,128)S(1)} collective-permute-done((f32[8,64,256]{2,1,0:T(8,128)S(1)}, f32[8,64,256]{2,1,0:T(8,128)S(1)}, u32[]{:S(2)}, u32[]{:S(2)}) %collective-permute-start.24) | collective-permute-done | bytes 524320 | tf_op jit(solution)/shard_map/ppermute | solution.py:430
  121.4 1.5 %gather.3 = f32[48,64,256]{2,1,0:T(8,128)} custom-call(s32[5]{0:T(128)S(1)} %stack.23.corner.refs_8_, f32[8,64,256]{2,1,0:T(8,128)S(1)} %add_chips.5.refs_0_, f32[8,64,256]{2,1,0:T(8,128)S(1)} %collective-permute-done.24.refs_1_, f32[48,64,256]{2,1,0:T(8,128)} %gather.2.rest_0_.refs_2_), custom_call_target="tpu_custom_call", output_to_operand_aliasing={{}: (3, {})} | custom-call | flops 1 | bytes 1 | tf_op jit(solution)/shard_map/gather/pallas_call | solution.py:387
  (14 shorter events, 0.1 us)
Async XLA Ops:
  0.8 13.1 %copy-start.2 = (s32[1,1024,3]{1,0,2:T(1,128)S(1)}, s32[1,1024,3]{1,0,2:T(1,128)}, u32[]{:S(2)}) copy-start(s32[1,1024,3]{1,0,2:T(1,128)} %param.18) | copy-start | bytes 36868
  0.8 13.1 %copy-start.1 = (f32[1,4,1024]{2,1,0:T(4,128)S(1)}, f32[1,4,1024]{2,1,0:T(4,128)}, u32[]{:S(2)}) copy-start(f32[1,4,1024]{2,1,0:T(4,128)} %param.16) | copy-start | bytes 49156
  3.1 15.0 %collective-permute-start = (f32[48,8,256]{2,1,0:T(8,128)S(1)}, f32[48,8,256]{2,1,0:T(8,128)S(1)}, u32[]{:S(2)}, u32[]{:S(2)}) collective-permute-start(f32[48,8,256]{2,1,0:T(8,128)S(1)} %get-tuple-element.63), channel_id=1, source_target_pairs={{0,1},{2,3},{4,5},{6,7},{8,9},{10,11},{12,13},{14,15},{16,17},{18,... | collective-permute-start | bytes 1179656 | tf_op jit(solution)/shard_map/ppermute | solution.py:409
  3.2 14.9 %collective-permute-start.1 = (f32[48,8,256]{2,1,0:T(8,128)S(1)}, f32[48,8,256]{2,1,0:T(8,128)S(1)}, u32[]{:S(2)}, u32[]{:S(2)}) collective-permute-start(f32[48,8,256]{2,1,0:T(8,128)S(1)} %get-tuple-element.64), channel_id=1, source_target_pairs={{1,2},{5,6},{9,10},{13,14},{17,18},{21,22},{25,26},{29,30},{2,1},{... | collective-permute-start | bytes 1179656 | tf_op jit(solution)/shard_map/ppermute | solution.py:409
  8.0 18.6 %collective-permute-start.2 = (f32[8,64,256]{2,1,0:T(8,128)S(1)}, f32[8,64,256]{2,1,0:T(8,128)S(1)}, u32[]{:S(2)}, u32[]{:S(2)}) collective-permute-start(f32[8,64,256]{2,1,0:T(8,128)S(1)} %get-tuple-element.67), channel_id=1, source_target_pairs={{4,8},{5,9},{6,10},{7,11},{12,16},{13,17},{14,18},{15,19},{20,24},... | collective-permute-start | bytes 1572872 | tf_op jit(solution)/shard_map/ppermute | solution.py:409
  13.1 13.6 %collective-permute-start.3 = (f32[8,64,256]{2,1,0:T(8,128)S(1)}, f32[8,64,256]{2,1,0:T(8,128)S(1)}, u32[]{:S(2)}, u32[]{:S(2)}) collective-permute-start(f32[8,64,256]{2,1,0:T(8,128)S(1)} %get-tuple-element.68), channel_id=1, source_target_pairs={{0,4},{1,5},{2,6},{3,7},{8,12},{9,13},{10,14},{11,15},{16,20},{17,... | collective-permute-start | bytes 1572872 | tf_op jit(solution)/shard_map/ppermute | solution.py:409
  13.9 4.2 %copy-start = (s32[1,3]{1,0:T(1,128)S(1)}, s32[1,3]{1,0:T(1,128)}, u32[]{:S(2)}) copy-start(s32[1,3]{1,0:T(1,128)} %refs_7_.15) | copy-start | bytes 40
  29.0 6.8 %collective-permute-start.4 = (f32[24,8,256]{2,1,0:T(8,128)S(1)}, f32[24,8,256]{2,1,0:T(8,128)S(1)}, u32[]{:S(2)}, u32[]{:S(2)}) collective-permute-start(f32[24,8,256]{2,1,0:T(8,128)S(1)} %get-tuple-element.83), channel_id=1, source_target_pairs={{0,1},{2,3},{4,5},{6,7},{8,9},{10,11},{12,13},{14,15},{16,17},{18,... | collective-permute-start | bytes 589832 | tf_op jit(solution)/shard_map/ppermute | solution.py:409
  29.1 6.8 %collective-permute-start.5 = (f32[24,8,256]{2,1,0:T(8,128)S(1)}, f32[24,8,256]{2,1,0:T(8,128)S(1)}, u32[]{:S(2)}, u32[]{:S(2)}) collective-permute-start(f32[24,8,256]{2,1,0:T(8,128)S(1)} %get-tuple-element.84), channel_id=1, source_target_pairs={{1,2},{5,6},{9,10},{13,14},{17,18},{21,22},{25,26},{29,30},{2,1},{... | collective-permute-start | bytes 589832 | tf_op jit(solution)/shard_map/ppermute | solution.py:409
  31.0 11.6 %collective-permute-start.6 = (f32[4,64,256]{2,1,0:T(8,128)S(1)}, f32[4,64,256]{2,1,0:T(8,128)S(1)}, u32[]{:S(2)}, u32[]{:S(2)}) collective-permute-start(f32[4,64,256]{2,1,0:T(8,128)S(1)} %get-tuple-element.85), channel_id=1, source_target_pairs={{4,8},{5,9},{6,10},{7,11},{12,16},{13,17},{14,18},{15,19},{20,24},... | collective-permute-start | bytes 786440 | tf_op jit(solution)/shard_map/ppermute | solution.py:409
  35.7 7.0 %collective-permute-start.7 = (f32[4,64,256]{2,1,0:T(8,128)S(1)}, f32[4,64,256]{2,1,0:T(8,128)S(1)}, u32[]{:S(2)}, u32[]{:S(2)}) collective-permute-start(f32[4,64,256]{2,1,0:T(8,128)S(1)} %get-tuple-element.86), channel_id=1, source_target_pairs={{0,4},{1,5},{2,6},{3,7},{8,12},{9,13},{10,14},{11,15},{16,20},{17,... | collective-permute-start | bytes 786440 | tf_op jit(solution)/shard_map/ppermute | solution.py:409
  44.3 7.0 %collective-permute-start.8 = (f32[24,8,256]{2,1,0:T(8,128)S(1)}, f32[24,8,256]{2,1,0:T(8,128)S(1)}, u32[]{:S(2)}, u32[]{:S(2)}) collective-permute-start(f32[24,8,256]{2,1,0:T(8,128)S(1)} %get-tuple-element.96), channel_id=1, source_target_pairs={{0,1},{2,3},{4,5},{6,7},{8,9},{10,11},{12,13},{14,15},{16,17},{18,... | collective-permute-start | bytes 589832 | tf_op jit(solution)/shard_map/ppermute | solution.py:409
  44.5 6.8 %collective-permute-start.9 = (f32[24,8,256]{2,1,0:T(8,128)S(1)}, f32[24,8,256]{2,1,0:T(8,128)S(1)}, u32[]{:S(2)}, u32[]{:S(2)}) collective-permute-start(f32[24,8,256]{2,1,0:T(8,128)S(1)} %get-tuple-element.97), channel_id=1, source_target_pairs={{1,2},{5,6},{9,10},{13,14},{17,18},{21,22},{25,26},{29,30},{2,1},{... | collective-permute-start | bytes 589832 | tf_op jit(solution)/shard_map/ppermute | solution.py:409
  47.7 10.7 %collective-permute-start.10 = (f32[4,64,256]{2,1,0:T(8,128)S(1)}, f32[4,64,256]{2,1,0:T(8,128)S(1)}, u32[]{:S(2)}, u32[]{:S(2)}) collective-permute-start(f32[4,64,256]{2,1,0:T(8,128)S(1)} %get-tuple-element.98), channel_id=1, source_target_pairs={{4,8},{5,9},{6,10},{7,11},{12,16},{13,17},{14,18},{15,19},{20,24},... | collective-permute-start | bytes 786440 | tf_op jit(solution)/shard_map/ppermute | solution.py:409
  51.2 7.3 %collective-permute-start.11 = (f32[4,64,256]{2,1,0:T(8,128)S(1)}, f32[4,64,256]{2,1,0:T(8,128)S(1)}, u32[]{:S(2)}, u32[]{:S(2)}) collective-permute-start(f32[4,64,256]{2,1,0:T(8,128)S(1)} %get-tuple-element.99), channel_id=1, source_target_pairs={{0,4},{1,5},{2,6},{3,7},{8,12},{9,13},{10,14},{11,15},{16,20},{17,... | collective-permute-start | bytes 786440 | tf_op jit(solution)/shard_map/ppermute | solution.py:409
  60.2 6.7 %collective-permute-start.12 = (f32[24,8,256]{2,1,0:T(8,128)S(1)}, f32[24,8,256]{2,1,0:T(8,128)S(1)}, u32[]{:S(2)}, u32[]{:S(2)}) collective-permute-start(f32[24,8,256]{2,1,0:T(8,128)S(1)} %get-tuple-element.105), channel_id=1, source_target_pairs={{0,1},{2,3},{4,5},{6,7},{8,9},{10,11},{12,13},{14,15},{16,17},{18,... | collective-permute-start | bytes 589832 | tf_op jit(solution)/shard_map/ppermute | solution.py:409
  60.2 6.6 %collective-permute-start.13 = (f32[24,8,256]{2,1,0:T(8,128)S(1)}, f32[24,8,256]{2,1,0:T(8,128)S(1)}, u32[]{:S(2)}, u32[]{:S(2)}) collective-permute-start(f32[24,8,256]{2,1,0:T(8,128)S(1)} %get-tuple-element.106), channel_id=1, source_target_pairs={{1,2},{5,6},{9,10},{13,14},{17,18},{21,22},{25,26},{29,30},{2,1},{... | collective-permute-start | bytes 589832 | tf_op jit(solution)/shard_map/ppermute | solution.py:409
  62.3 11.0 %collective-permute-start.14 = (f32[4,64,256]{2,1,0:T(8,128)S(1)}, f32[4,64,256]{2,1,0:T(8,128)S(1)}, u32[]{:S(2)}, u32[]{:S(2)}) collective-permute-start(f32[4,64,256]{2,1,0:T(8,128)S(1)} %get-tuple-element.107), channel_id=1, source_target_pairs={{4,8},{5,9},{6,10},{7,11},{12,16},{13,17},{14,18},{15,19},{20,24},... | collective-permute-start | bytes 786440 | tf_op jit(solution)/shard_map/ppermute | solution.py:409
  66.7 6.6 %collective-permute-start.15 = (f32[4,64,256]{2,1,0:T(8,128)S(1)}, f32[4,64,256]{2,1,0:T(8,128)S(1)}, u32[]{:S(2)}, u32[]{:S(2)}) collective-permute-start(f32[4,64,256]{2,1,0:T(8,128)S(1)} %get-tuple-element.108), channel_id=1, source_target_pairs={{0,4},{1,5},{2,6},{3,7},{8,12},{9,13},{10,14},{11,15},{16,20},{17,... | collective-permute-start | bytes 786440 | tf_op jit(solution)/shard_map/ppermute | solution.py:409
  75.4 7.4 %collective-permute-start.21 = (f32[10,64,256]{2,1,0:T(8,128)S(1)}, f32[10,64,256]{2,1,0:T(8,128)S(1)}, u32[]{:S(2)}, u32[]{:S(2)}) collective-permute-start(f32[10,64,256]{2,1,0:T(8,128)S(1)} %get-tuple-element.117.rest_0_), channel_id=1, source_target_pairs={{0,32},{32,0},{64,96},{96,64},{1,33},{33,1},{65,97},{97,65},{2,34}... | collective-permute-start | bytes 1966088 | tf_op jit(solution)/shard_map/ppermute | solution.py:421
  82.9 16.0 %collective-permute-start.22 = (f32[10,64,256]{2,1,0:T(8,128)S(1)}, f32[10,64,256]{2,1,0:T(8,128)S(1)}, u32[]{:S(2)}, u32[]{:S(2)}) collective-permute-start(f32[10,64,256]{2,1,0:T(8,128)S(1)} %add_cores.5.a), channel_id=1, source_target_pairs={{0,64},{32,96},{64,0},{96,32},{1,65},{33,97},{65,1},{97,33},{2,66}... | collective-permute-start | bytes 1966088 | tf_op jit(solution)/shard_map/ppermute | solution.py:427
  83.0 1.8 %collective-permute-start.18 = (f32[6,64,256]{2,1,0:T(8,128)S(1)}, f32[6,64,256]{2,1,0:T(8,128)S(1)}, u32[]{:S(2)}, u32[]{:S(2)}) collective-permute-start(f32[6,64,256]{2,1,0:T(8,128)S(1)} %get-tuple-element.116), channel_id=1, source_target_pairs={{0,32},{32,0},{64,96},{96,64},{1,33},{33,1},{65,97},{97,65},{2,34}... | collective-permute-start | bytes 1179656 | tf_op jit(solution)/shard_map/ppermute | solution.py:421
  83.4 17.6 %collective-permute-start.16 = (f32[8,64,256]{2,1,0:T(8,128)S(1)}, f32[8,64,256]{2,1,0:T(8,128)S(1)}, u32[]{:S(2)}, u32[]{:S(2)}) collective-permute-start(f32[8,64,256]{2,1,0:T(8,128)S(1)} %get-tuple-element.114), channel_id=1, source_target_pairs={{0,32},{32,0},{64,96},{96,64},{1,33},{33,1},{65,97},{97,65},{2,34}... | collective-permute-start | bytes 1572872 | tf_op jit(solution)/shard_map/ppermute | solution.py:421
  84.8 22.5 %collective-permute-start.19 = (f32[6,64,256]{2,1,0:T(8,128)S(1)}, f32[6,64,256]{2,1,0:T(8,128)S(1)}, u32[]{:S(2)}, u32[]{:S(2)}) collective-permute-start(f32[6,64,256]{2,1,0:T(8,128)S(1)} %add_cores.4.a), channel_id=1, source_target_pairs={{0,64},{32,96},{64,0},{96,32},{1,65},{33,97},{65,1},{97,33},{2,66}... | collective-permute-start | bytes 1179656 | tf_op jit(solution)/shard_map/ppermute | solution.py:427
  99.0 12.2 %collective-permute-start.23 = (f32[10,64,256]{2,1,0:T(8,128)S(1)}, f32[10,64,256]{2,1,0:T(8,128)S(1)}, u32[]{:S(2)}, u32[]{:S(2)}) collective-permute-start(f32[10,64,256]{2,1,0:T(8,128)S(1)} %add_chips.4.refs_2_), channel_id=1, source_target_pairs={{0,32},{32,0},{64,96},{96,64},{1,33},{33,1},{65,97},{97,65},{2,34}... | collective-permute-start | bytes 1966088 | tf_op jit(solution)/shard_map/ppermute | solution.py:430
  101.1 17.4 %collective-permute-start.17 = (f32[8,64,256]{2,1,0:T(8,128)S(1)}, f32[8,64,256]{2,1,0:T(8,128)S(1)}, u32[]{:S(2)}, u32[]{:S(2)}) collective-permute-start(f32[8,64,256]{2,1,0:T(8,128)S(1)} %add_cores.3.a), channel_id=1, source_target_pairs={{0,64},{32,96},{64,0},{96,32},{1,65},{33,97},{65,1},{97,33},{2,66}... | collective-permute-start | bytes 1572872 | tf_op jit(solution)/shard_map/ppermute | solution.py:427
  107.4 3.8 %collective-permute-start.20 = (f32[6,64,256]{2,1,0:T(8,128)S(1)}, f32[6,64,256]{2,1,0:T(8,128)S(1)}, u32[]{:S(2)}, u32[]{:S(2)}) collective-permute-start(f32[6,64,256]{2,1,0:T(8,128)S(1)} %add_chips.3.refs_0_), channel_id=1, source_target_pairs={{0,32},{32,0},{64,96},{96,64},{1,33},{33,1},{65,97},{97,65},{2,34}... | collective-permute-start | bytes 1179656 | tf_op jit(solution)/shard_map/ppermute | solution.py:430
  118.6 2.8 %collective-permute-start.24 = (f32[8,64,256]{2,1,0:T(8,128)S(1)}, f32[8,64,256]{2,1,0:T(8,128)S(1)}, u32[]{:S(2)}, u32[]{:S(2)}) collective-permute-start(f32[8,64,256]{2,1,0:T(8,128)S(1)} %add_chips.5.refs_0_), channel_id=1, source_target_pairs={{0,32},{32,0},{64,96},{96,64},{1,33},{33,1},{65,97},{97,65},{2,34}... | collective-permute-start | bytes 1572872 | tf_op jit(solution)/shard_map/ppermute | solution.py:430

commit v6 on v5

--- a/solution.py
+++ b/solution.py
@@ -244,12 +244,11 @@
             image[at, :, 0:128] = jnp.where(flat + dx * dx < MUTE * MUTE, 0.0, image[at, :, 0:128])
 
 
-def split_image(image, sent, kept, core, ranges):
+def split_image(image, sent, core, ranges):
     (lower, _), (upper, _) = ranges
 
     def body(i, carry):
         sent[i] = image[jnp.where(core == 0, upper, lower) + i]
-        kept[i] = image[jnp.where(core == 0, lower, upper) + i]
         return carry
 
     lax.fori_loop(0, sent.shape[0], body, 0)
@@ -339,7 +338,7 @@
         mute(r["image"], r["source"], corner, ranges)
     if step == STEPS - 1:
         for n, halves in enumerate(splits):
-            split_image(r["image"], r["sent%d" % n], r["kept%d" % n], corner[2], halves)
+            split_image(r["image"], r["sent%d" % n], corner[2], halves)
     elif edges:
         top = size_x - RADIUS
         r["sxa"][...] = r["out"][pl.ds(top * corner[3], RADIUS)]
@@ -417,10 +416,21 @@
 CHIPS = [(i, i ^ 2) for i in range(4)]
 
 
-def add_cores(sent, kept, after=()):
+def keep_kernel(ranges, image, arrived, corner, out):
+    (lower, _), (upper, _) = ranges
+    first = jnp.where(corner[2] == 0, lower, upper)
+
+    def body(i, carry):
+        out[i] = image[first + i] + arrived[i]
+        return carry
+
+    lax.fori_loop(0, out.shape[0], body, 0)
+
+
+def add_cores(sent, ranges, image, corner):
     arrived = lax.ppermute(sent, "shot", CORES)
-    args = [kept, arrived] + list(after)
-    return call(add_kernel, "add_cores", args, [VMEM] * len(args), [kept.shape])[0]
+    kernel = functools.partial(keep_kernel, ranges)
+    return call(kernel, "add_cores", (image, arrived, corner), [VMEM, VMEM, SMEM], [sent.shape])[0]
 
 
 def add_chips(mine, after):
@@ -507,11 +517,11 @@
 
     def halves(splits):
         shapes = [(lower[1] - lower[0], size_y, size_z) for lower, _ in splits]
-        return {name + str(i): shape for i, shape in enumerate(shapes) for name in ("sent", "kept")}
+        return {name + str(i): shape for i, shape in enumerate(shapes) for name in ("sent",)}
 
     early = run(STEPS - 1, inner, False, ("image",), halves(splits[:1]), splits[:1], weight=4 << 30)
     late = run(STEPS - 1, [], True, ("out", "image"), halves(splits[1:]), splits[1:], weight=4 << 30)
-    sums = [add_cores(*early, after=late[:1]), add_cores(*late[:2]), add_cores(*late[2:])]
+    sums = [add_cores(sent, ranges, held["image"], corner) for sent, ranges in zip(early + late, splits)]
     (last,) = call(store_kernel, "store", [held["out"]], [VMEM], [pltpu.HBM(grid, F32)], {}, [pltpu.SemaphoreType.DMA])
     def gather(splits, chunks, started):
         return call(

time: 124 us -> 124 us (level)
  waiting for transfers between devices: 30.5 us -> 28.4 us
  transfers between devices with their start and end apart: 25 -> 25, of which waited for: 9 -> 8; matrix products, arithmetic and copies ran while one was open for 0% -> 0% of each run, Pallas kernels for 28% -> 29%
where the time goes in v6:
time: 124 us; the launch traced here: 123 us
  Pallas kernels  47.4 us (38%)
  starting transfers between devices  45.1 us (36%)
  waiting for transfers between devices  28.4 us (23%)
  between operations  1.9 us (2%)
    pallas_call x19, Pallas kernels, call(): pl.pallas_call(kernel, name=name, in_specs=specs, out_specs=[pl.BlockSpec...  47.4 us
    ppermute x16, starting transfers between devices, swap(): return lax.ppermute(strip, 'dom', pairs + [(b, a) for a, b in pairs])  31.4 us
    ppermute x3, waiting for transfers between devices, add_chips(): arrived = lax.ppermute(mine, 'shot', CHIPS)  22.8 us
    ppermute x3, starting transfers between devices, add_cores(): arrived = lax.ppermute(sent, 'shot', CORES)  6.49 us
    ppermute x3, starting transfers between devices, add_chips(): return (mine, lax.ppermute(mine, 'shot', CORES))  5.44 us
    ppermute x3, waiting for transfers between devices, add_cores(): arrived = lax.ppermute(sent, 'shot', CORES)  3.07 us
  transfers between devices with their start and end apart: 25, of which 8 were waited for; matrix products, arithmetic and copies ran while one was open for 0% of the time, Pallas kernels for 29%

profile of v6, /device:TPU:57, one launch (start us, length us, event | category | flops | bytes accessed | tf_op | source)
XLA Modules:
  0.0 122.9 jit_solution(14817228043840226925)
XLA Ops:
  0.7 0.1 stack.23.corner.refs_8_
  0.8 2.3 %strips.1 = (f32[8,64,256]{2,1,0:T(8,128)S(1)}, f32[8,64,256]{2,1,0:T(8,128)S(1)}, f32[48,8,256]{2,1,0:T(8,128)S(1)}, f32[48,8,256]{2,1,0:T(8,128)S(1)}) custom-call(f32[48,64,256]{2,1,0:T(8,128)} %bitcast.29, f32[48,64,256]{2,1,0:T(8,128)} %bitcast.31, s32[5]{0:T(128)S(1)} %stack.23.corner.refs_8_), custom_call_target="tpu_custom_call" | custom-call | flops 1 | bytes 1 | tf_op jit(solution)/shard_map/strips/pallas_call | solution.py:386
  3.1 0.1 collective-permute-start
  3.2 4.9 %collective-permute-start.1 = (f32[48,8,256]{2,1,0:T(8,128)S(1)}, f32[48,8,256]{2,1,0:T(8,128)S(1)}, u32[]{:S(2)}, u32[]{:S(2)}) collective-permute-start(f32[48,8,256]{2,1,0:T(8,128)S(1)} %get-tuple-element.62), channel_id=1, source_target_pairs={{1,2},{5,6},{9,10},{13,14},{17,18},{21,22},{25,26},{29,30},{2,1},{... | collective-permute-start | bytes 1179656 | tf_op jit(solution)/shard_map/ppermute | solution.py:408
  8.0 5.1 %collective-permute-start.2 = (f32[8,64,256]{2,1,0:T(8,128)S(1)}, f32[8,64,256]{2,1,0:T(8,128)S(1)}, u32[]{:S(2)}, u32[]{:S(2)}) collective-permute-start(f32[8,64,256]{2,1,0:T(8,128)S(1)} %get-tuple-element.65), channel_id=1, source_target_pairs={{4,8},{5,9},{6,10},{7,11},{12,16},{13,17},{14,18},{15,19},{20,24},... | collective-permute-start | bytes 1572872 | tf_op jit(solution)/shard_map/ppermute | solution.py:408
  13.1 0.1 collective-permute-start.3
  13.9 0.0 copy-start
  13.9 4.1 %fetch.1 = (f32[48,64,128]{2,1,0:T(8,128)S(1)}, f32[48,64,256]{2,1,0:T(8,128)S(1)}, f32[48,64,256]{2,1,0:T(8,128)S(1)}, bf16[4,128,160]{2,1,0:T(8,128)(2,1)S(1)}...) custom-call(s32[3,1,1024]{2,1,0:T(1,128)S(1)} %broadcast_in_dim.9.pl, ...), custom_call_target="tpu_custom_call" | custom-call | flops 1 | bytes 1 | tf_op jit(solution)/shard_map/fetch/pallas_call | solution.py:386
  18.0 0.0 collective-permute-done.refs_2_
  18.0 0.0 collective-permute-done.1.refs_3_
  18.1 8.0 %step0.2 = (f32[48,64,256]{2,1,0:T(8,128)S(1)}, f32[48,64,256]{2,1,0:T(8,128)S(1)}, f32[48,64,256]{2,1,0:T(8,128)S(1)}, f32[48,64,256]{2,1,0:T(8,128)S(1)}, f32[...) custom-call(f32[48,64,256]{2,1,0:T(8,128)S(1)} %get-tuple-element.59, ...), custom_call_target="tpu_custom_call", output_to_operand_aliasing={{6}: (13, {}), {7}: (14, {}), {8}: (15, {})} | custom-call | flops 4294967296 | bytes 1 | tf_op jit(solution)/shard_map/step0/pallas_call | solution.py:386
  26.1 0.0 collective-permute-done.2.refs_9_
  26.1 0.0 collective-permute-done.3.refs_10_
  26.1 2.2 %step0.3 = (f32[48,64,256]{2,1,0:T(8,128)S(1)}, f32[48,64,256]{2,1,0:T(8,128)S(1)}, f32[48,64,256]{2,1,0:T(8,128)S(1)}, f32[48,64,256]{2,1,0:T(8,128)S(1)}, f32[...) custom-call(f32[48,64,256]{2,1,0:T(8,128)S(1)} %get-tuple-element.59, ...), custom_call_target="tpu_custom_call", output_to_operand_aliasing={{0}: (15, {}), {1}: (16, {}), {2}: (17, {}), {3}: (18, {}),... | custom-call | flops 1 | bytes 1 | tf_op jit(solution)/shard_map/step0/pallas_call | solution.py:386
  28.4 0.1 collective-permute-start.4
  28.5 1.9 %collective-permute-start.5 = (f32[24,8,256]{2,1,0:T(8,128)S(1)}, f32[24,8,256]{2,1,0:T(8,128)S(1)}, u32[]{:S(2)}, u32[]{:S(2)}) collective-permute-start(f32[24,8,256]{2,1,0:T(8,128)S(1)} %get-tuple-element.82), channel_id=1, source_target_pairs={{1,2},{5,6},{9,10},{13,14},{17,18},{21,22},{25,26},{29,30},{2,1},{... | collective-permute-start | bytes 589832 | tf_op jit(solution)/shard_map/ppermute | solution.py:408
  30.4 4.9 %collective-permute-start.6 = (f32[4,64,256]{2,1,0:T(8,128)S(1)}, f32[4,64,256]{2,1,0:T(8,128)S(1)}, u32[]{:S(2)}, u32[]{:S(2)}) collective-permute-start(f32[4,64,256]{2,1,0:T(8,128)S(1)} %get-tuple-element.83), channel_id=1, source_target_pairs={{4,8},{5,9},{6,10},{7,11},{12,16},{13,17},{14,18},{15,19},{20,24},... | collective-permute-start | bytes 786440 | tf_op jit(solution)/shard_map/ppermute | solution.py:408
  35.3 0.1 collective-permute-start.7
  35.4 0.0 collective-permute-done.4.refs_2_
  35.4 0.0 collective-permute-done.5.refs_3_
  35.4 5.9 %step1.2 = (f32[48,64,256]{2,1,0:T(8,128)S(1)}, f32[48,64,256]{2,1,0:T(8,128)S(1)}, bf16[48,64,256]{2,1,0:T(8,128)(2,1)S(1)}) custom-call(f32[48,64,256]{2,1,0:T(8,128)S(1)} %get-tuple-element.80.refs_0_.refs_10_.refs_11_, f32[48,64,128]{2,1,0:T(8,128)S(1)} %get-tuple-element.60.refs_1_, ...), custom_call_target="tpu_custom_call", output_to_operand_aliasing={{1}: (16, {})} | custom-call | flops 4294967296 | bytes 1 | tf_op jit(solution)/shard_map/step1/pallas_call | solution.py:386
  41.3 0.4 collective-permute-done.6.refs_9_
  41.7 0.0 collective-permute-done.7.refs_10_
  41.7 1.7 %step1.3 = (f32[48,64,256]{2,1,0:T(8,128)S(1)}, f32[48,64,256]{2,1,0:T(8,128)S(1)}, f32[4,64,256]{2,1,0:T(8,128)S(1)}, f32[4,64,256]{2,1,0:T(8,128)S(1)}, f32[24...) custom-call(f32[48,64,256]{2,1,0:T(8,128)S(1)} %get-tuple-element.80.refs_0_.refs_1, ...), custom_call_target="tpu_custom_call", output_to_operand_aliasing={{0}: (17, {}), {1}: (18, {})} | custom-call | flops 1 | bytes 1 | tf_op jit(solution)/shard_map/step1/pallas_call | solution.py:386
  43.4 0.3 collective-permute-start.8
  43.7 3.2 %collective-permute-start.9 = (f32[24,8,256]{2,1,0:T(8,128)S(1)}, f32[24,8,256]{2,1,0:T(8,128)S(1)}, u32[]{:S(2)}, u32[]{:S(2)}) collective-permute-start(f32[24,8,256]{2,1,0:T(8,128)S(1)} %get-tuple-element.95), channel_id=1, source_target_pairs={{1,2},{5,6},{9,10},{13,14},{17,18},{21,22},{25,26},{29,30},{2,1},{... | collective-permute-start | bytes 589832 | tf_op jit(solution)/shard_map/ppermute | solution.py:408
  46.9 4.0 %collective-permute-start.10 = (f32[4,64,256]{2,1,0:T(8,128)S(1)}, f32[4,64,256]{2,1,0:T(8,128)S(1)}, u32[]{:S(2)}, u32[]{:S(2)}) collective-permute-start(f32[4,64,256]{2,1,0:T(8,128)S(1)} %get-tuple-element.96), channel_id=1, source_target_pairs={{4,8},{5,9},{6,10},{7,11},{12,16},{13,17},{14,18},{15,19},{20,24},... | collective-permute-start | bytes 786440 | tf_op jit(solution)/shard_map/ppermute | solution.py:408
  50.9 0.1 collective-permute-start.11
  51.0 0.0 collective-permute-done.8.refs_2_
  51.0 6.0 %step2.2 = (f32[48,64,256]{2,1,0:T(8,128)S(1)}, f32[48,64,256]{2,1,0:T(8,128)S(1)}, bf16[48,64,256]{2,1,0:T(8,128)(2,1)S(1)}) custom-call(f32[48,64,256]{2,1,0:T(8,128)S(1)} %get-tuple-element.93.refs_0_.refs_9_.refs_11_, f32[48,64,128]{2,1,0:T(8,128)S(1)} %get-tuple-element.60.refs_1_, ...), custom_call_target="tpu_custom_call", output_to_operand_aliasing={{1}: (16, {})} | custom-call | flops 4294967296 | bytes 1 | tf_op jit(solution)/shard_map/step2/pallas_call | solution.py:386
  57.0 0.6 collective-permute-done.10.refs_9_
  57.6 1.7 %step2.3 = (f32[48,64,256]{2,1,0:T(8,128)S(1)}, f32[48,64,256]{2,1,0:T(8,128)S(1)}, f32[4,64,256]{2,1,0:T(8,128)S(1)}, f32[4,64,256]{2,1,0:T(8,128)S(1)}, f32[24...) custom-call(f32[48,64,256]{2,1,0:T(8,128)S(1)} %get-tuple-element.93.refs_0_.refs_9, ...), custom_call_target="tpu_custom_call", output_to_operand_aliasing={{0}: (17, {}), {1}: (18, {})} | custom-call | flops 1 | bytes 1 | tf_op jit(solution)/shard_map/step2/pallas_call | solution.py:386
  59.3 0.1 collective-permute-start.12
  59.4 2.1 %collective-permute-start.13 = (f32[24,8,256]{2,1,0:T(8,128)S(1)}, f32[24,8,256]{2,1,0:T(8,128)S(1)}, u32[]{:S(2)}, u32[]{:S(2)}) collective-permute-start(f32[24,8,256]{2,1,0:T(8,128)S(1)} %get-tuple-element.104), channel_id=1, source_target_pairs={{1,2},{5,6},{9,10},{13,14},{17,18},{21,22},{25,26},{29,30},{2,1},{... | collective-permute-start | bytes 589832 | tf_op jit(solution)/shard_map/ppermute | solution.py:408
  61.6 4.5 %collective-permute-start.14 = (f32[4,64,256]{2,1,0:T(8,128)S(1)}, f32[4,64,256]{2,1,0:T(8,128)S(1)}, u32[]{:S(2)}, u32[]{:S(2)}) collective-permute-start(f32[4,64,256]{2,1,0:T(8,128)S(1)} %get-tuple-element.105), channel_id=1, source_target_pairs={{4,8},{5,9},{6,10},{7,11},{12,16},{13,17},{14,18},{15,19},{20,24},... | collective-permute-start | bytes 786440 | tf_op jit(solution)/shard_map/ppermute | solution.py:408
  66.1 0.1 collective-permute-start.15
  66.2 0.0 collective-permute-done.12.refs_2_
  66.2 6.3 %step3.2 = (f32[48,64,256]{2,1,0:T(8,128)S(1)}, f32[48,64,256]{2,1,0:T(8,128)S(1)}, f32[6,64,256]{2,1,0:T(8,128)S(1)}) custom-call(f32[48,64,256]{2,1,0:T(8,128)S(1)} %get-tuple-element.102.refs_0_, f32[48,64,128]{2,1,0:T(8,128)S(1)} %get-tuple-element.60.refs_1_, ...), custom_call_target="tpu_custom_call", output_to_operand_aliasing={{1}: (15, {})} | custom-call | flops 4294967296 | bytes 1 | tf_op jit(solution)/shard_map/step3/pallas_call | solution.py:386
  72.5 0.0 collective-permute-done.14.refs_9_
  72.5 1.9 %step3.3 = (f32[48,64,256]{2,1,0:T(8,128)S(1)}, f32[48,64,256]{2,1,0:T(8,128)S(1)}, f32[10,64,256]{2,1,0:T(8,128)S(1)}, f32[8,64,256]{2,1,0:T(8,128)S(1)}) custom-call(f32[48,64,256]{2,1,0:T(8,128)S(1)} %get-tuple-element.102.refs_0_, f32[48,64,128]{2,1,0:T(8,128)S(1)} %get-tuple-element.60.refs_1_, ...), custom_call_target="tpu_custom_call", output_to_operand_aliasing={{0}: (17, {}), {1}: (18, {})} | custom-call | flops 4294967296 | bytes 1 | tf_op jit(solution)/shard_map/step3/pallas_call | solution.py:386
  74.5 5.8 %collective-permute-start.21 = (f32[10,64,256]{2,1,0:T(8,128)S(1)}, f32[10,64,256]{2,1,0:T(8,128)S(1)}, u32[]{:S(2)}, u32[]{:S(2)}) collective-permute-start(f32[10,64,256]{2,1,0:T(8,128)S(1)} %get-tuple-element.114), channel_id=1, source_target_pairs={{0,32},{32,0},{64,96},{96,64},{1,33},{33,1},{65,97},{97,65},{2,34}... | collective-permute-start | bytes 1966088 | tf_op jit(solution)/shard_map/ppermute | solution.py:431
  80.3 1.7 %collective-permute-done.21.arrived = f32[10,64,256]{2,1,0:T(8,128)S(1)} collective-permute-done((f32[10,64,256]{2,1,0:T(8,128)S(1)}, f32[10,64,256]{2,1,0:T(8,128)S(1)}, u32[]{:S(2)}, u32[]{:S(2)}) %collective-permute-start.21) | collective-permute-done | bytes 655392 | tf_op jit(solution)/shard_map/ppermute | solution.py:431
  82.0 0.6 add_cores.5.a
  82.7 0.2 collective-permute-start.22
  82.8 0.7 collective-permute-start.18
  83.5 0.0 collective-permute-start.16
  83.5 1.3 %collective-permute-done.18.arrived = f32[6,64,256]{2,1,0:T(8,128)S(1)} collective-permute-done((f32[6,64,256]{2,1,0:T(8,128)S(1)}, f32[6,64,256]{2,1,0:T(8,128)S(1)}, u32[]{:S(2)}, u32[]{:S(2)}) %collective-permute-start.18) | collective-permute-done | bytes 393248 | tf_op jit(solution)/shard_map/ppermute | solution.py:431
  84.9 0.6 add_cores.4.a
  85.5 1.5 %collective-permute-start.19 = (f32[6,64,256]{2,1,0:T(8,128)S(1)}, f32[6,64,256]{2,1,0:T(8,128)S(1)}, u32[]{:S(2)}, u32[]{:S(2)}) collective-permute-start(f32[6,64,256]{2,1,0:T(8,128)S(1)} %add_cores.4.a), channel_id=1, source_target_pairs={{0,64},{32,96},{64,0},{96,32},{1,65},{33,97},{65,1},{97,33},{2,66}... | collective-permute-start | bytes 1179656 | tf_op jit(solution)/shard_map/ppermute | solution.py:437
  86.9 11.8 %collective-permute-done.22.b = f32[10,64,256]{2,1,0:T(8,128)S(1)} collective-permute-done((f32[10,64,256]{2,1,0:T(8,128)S(1)}, f32[10,64,256]{2,1,0:T(8,128)S(1)}, u32[]{:S(2)}, u32[]{:S(2)}) %collective-permute-start.22) | collective-permute-done | bytes 655392 | tf_op jit(solution)/shard_map/ppermute | solution.py:437
  98.7 0.1 add_chips.4.refs_2_
  98.8 2.1 %collective-permute-start.23 = (f32[10,64,256]{2,1,0:T(8,128)S(1)}, f32[10,64,256]{2,1,0:T(8,128)S(1)}, u32[]{:S(2)}, u32[]{:S(2)}) collective-permute-start(f32[10,64,256]{2,1,0:T(8,128)S(1)} %add_chips.4.refs_2_), channel_id=1, source_target_pairs={{0,32},{32,0},{64,96},{96,64},{1,33},{33,1},{65,97},{97,65},{2,34}... | collective-permute-start | bytes 1966088 | tf_op jit(solution)/shard_map/ppermute | solution.py:440
  100.9 0.0 collective-permute-done.16.arrived
  100.9 0.6 add_cores.3.a
  101.5 0.2 collective-permute-start.17
  101.7 5.5 %collective-permute-done.19.b = f32[6,64,256]{2,1,0:T(8,128)S(1)} collective-permute-done((f32[6,64,256]{2,1,0:T(8,128)S(1)}, f32[6,64,256]{2,1,0:T(8,128)S(1)}, u32[]{:S(2)}, u32[]{:S(2)}) %collective-permute-start.19) | collective-permute-done | bytes 393248 | tf_op jit(solution)/shard_map/ppermute | solution.py:437
  107.2 2.1 %collective-permute-start.20 = (f32[6,64,256]{2,1,0:T(8,128)S(1)}, f32[6,64,256]{2,1,0:T(8,128)S(1)}, u32[]{:S(2)}, u32[]{:S(2)}) collective-permute-start(f32[6,64,256]{2,1,0:T(8,128)S(1)} %add_chips.3.refs_0_), channel_id=1, source_target_pairs={{0,32},{32,0},{64,96},{96,64},{1,33},{33,1},{65,97},{97,65},{2,34}... | collective-permute-start | bytes 1179656 | tf_op jit(solution)/shard_map/ppermute | solution.py:440
  109.3 1.7 %store.1.rest_1_ = f32[48,64,256]{2,1,0:T(8,128)} custom-call(f32[48,64,256]{2,1,0:T(8,128)S(1)} %get-tuple-element.115.source), custom_call_target="tpu_custom_call" | custom-call | flops 1 | bytes 1 | tf_op jit(solution)/shard_map/store/pallas_call | solution.py:386
  111.0 1.9 %gather.2.rest_0_.refs_2_ = f32[48,64,256]{2,1,0:T(8,128)} custom-call(s32[5]{0:T(128)S(1)} %stack.23.corner.refs_8_, f32[6,64,256]{2,1,0:T(8,128)S(1)} %add_chips.3.refs_0_, f32[6,64,256]{2,1,0:T(8,128)S(1)} %collective-permute-done.20.refs_1_, f32[10,64,256]{2,1,0:T(8,128)S(1)} %add_chips.4.refs_2_, f32[10,64,256]{2,1,0:T(8,128)S(1)} %collective-permute-done.23.refs_3_), custom_call_target="tpu_custom_call" | custom-call | flops 1 | bytes 1 | tf_op jit(solution)/shard_map/gather/pallas_call | solution.py:386
  112.9 5.5 %collective-permute-done.17.b = f32[8,64,256]{2,1,0:T(8,128)S(1)} collective-permute-done((f32[8,64,256]{2,1,0:T(8,128)S(1)}, f32[8,64,256]{2,1,0:T(8,128)S(1)}, u32[]{:S(2)}, u32[]{:S(2)}) %collective-permute-start.17) | collective-permute-done | bytes 524320 | tf_op jit(solution)/shard_map/ppermute | solution.py:437
  118.4 0.1 add_chips.5.refs_0_
  118.4 1.3 %collective-permute-start.24 = (f32[8,64,256]{2,1,0:T(8,128)S(1)}, f32[8,64,256]{2,1,0:T(8,128)S(1)}, u32[]{:S(2)}, u32[]{:S(2)}) collective-permute-start(f32[8,64,256]{2,1,0:T(8,128)S(1)} %add_chips.5.refs_0_), channel_id=1, source_target_pairs={{0,32},{32,0},{64,96},{96,64},{1,33},{33,1},{65,97},{97,65},{2,34}... | collective-permute-start | bytes 1572872 | tf_op jit(solution)/shard_map/ppermute | solution.py:440
  119.7 1.5 %collective-permute-done.24.refs_1_ = f32[8,64,256]{2,1,0:T(8,128)S(1)} collective-permute-done((f32[8,64,256]{2,1,0:T(8,128)S(1)}, f32[8,64,256]{2,1,0:T(8,128)S(1)}, u32[]{:S(2)}, u32[]{:S(2)}) %collective-permute-start.24) | collective-permute-done | bytes 524320 | tf_op jit(solution)/shard_map/ppermute | solution.py:440
  121.2 1.5 %gather.3 = f32[48,64,256]{2,1,0:T(8,128)} custom-call(s32[5]{0:T(128)S(1)} %stack.23.corner.refs_8_, f32[8,64,256]{2,1,0:T(8,128)S(1)} %add_chips.5.refs_0_, f32[8,64,256]{2,1,0:T(8,128)S(1)} %collective-permute-done.24.refs_1_, f32[48,64,256]{2,1,0:T(8,128)} %gather.2.rest_0_.refs_2_), custom_call_target="tpu_custom_call", output_to_operand_aliasing={{}: (3, {})} | custom-call | flops 1 | bytes 1 | tf_op jit(solution)/shard_map/gather/pallas_call | solution.py:386
  (14 shorter events, 0.1 us)
Async XLA Ops:
  0.8 13.1 %copy-start.2 = (s32[1,1024,3]{1,0,2:T(1,128)S(1)}, s32[1,1024,3]{1,0,2:T(1,128)}, u32[]{:S(2)}) copy-start(s32[1,1024,3]{1,0,2:T(1,128)} %param.18) | copy-start | bytes 36868
  0.8 13.1 %copy-start.1 = (f32[1,4,1024]{2,1,0:T(4,128)S(1)}, f32[1,4,1024]{2,1,0:T(4,128)}, u32[]{:S(2)}) copy-start(f32[1,4,1024]{2,1,0:T(4,128)} %param.16) | copy-start | bytes 49156
  3.1 15.0 %collective-permute-start = (f32[48,8,256]{2,1,0:T(8,128)S(1)}, f32[48,8,256]{2,1,0:T(8,128)S(1)}, u32[]{:S(2)}, u32[]{:S(2)}) collective-permute-start(f32[48,8,256]{2,1,0:T(8,128)S(1)} %get-tuple-element.61), channel_id=1, source_target_pairs={{0,1},{2,3},{4,5},{6,7},{8,9},{10,11},{12,13},{14,15},{16,17},{18,... | collective-permute-start | bytes 1179656 | tf_op jit(solution)/shard_map/ppermute | solution.py:408
  3.2 14.9 %collective-permute-start.1 = (f32[48,8,256]{2,1,0:T(8,128)S(1)}, f32[48,8,256]{2,1,0:T(8,128)S(1)}, u32[]{:S(2)}, u32[]{:S(2)}) collective-permute-start(f32[48,8,256]{2,1,0:T(8,128)S(1)} %get-tuple-element.62), channel_id=1, source_target_pairs={{1,2},{5,6},{9,10},{13,14},{17,18},{21,22},{25,26},{29,30},{2,1},{... | collective-permute-start | bytes 1179656 | tf_op jit(solution)/shard_map/ppermute | solution.py:408
  8.0 18.1 %collective-permute-start.2 = (f32[8,64,256]{2,1,0:T(8,128)S(1)}, f32[8,64,256]{2,1,0:T(8,128)S(1)}, u32[]{:S(2)}, u32[]{:S(2)}) collective-permute-start(f32[8,64,256]{2,1,0:T(8,128)S(1)} %get-tuple-element.65), channel_id=1, source_target_pairs={{4,8},{5,9},{6,10},{7,11},{12,16},{13,17},{14,18},{15,19},{20,24},... | collective-permute-start | bytes 1572872 | tf_op jit(solution)/shard_map/ppermute | solution.py:408
  13.1 13.0 %collective-permute-start.3 = (f32[8,64,256]{2,1,0:T(8,128)S(1)}, f32[8,64,256]{2,1,0:T(8,128)S(1)}, u32[]{:S(2)}, u32[]{:S(2)}) collective-permute-start(f32[8,64,256]{2,1,0:T(8,128)S(1)} %get-tuple-element.66), channel_id=1, source_target_pairs={{0,4},{1,5},{2,6},{3,7},{8,12},{9,13},{10,14},{11,15},{16,20},{17,... | collective-permute-start | bytes 1572872 | tf_op jit(solution)/shard_map/ppermute | solution.py:408
  13.9 4.2 %copy-start = (s32[1,3]{1,0:T(1,128)S(1)}, s32[1,3]{1,0:T(1,128)}, u32[]{:S(2)}) copy-start(s32[1,3]{1,0:T(1,128)} %refs_7_.15) | copy-start | bytes 40
  28.4 7.0 %collective-permute-start.4 = (f32[24,8,256]{2,1,0:T(8,128)S(1)}, f32[24,8,256]{2,1,0:T(8,128)S(1)}, u32[]{:S(2)}, u32[]{:S(2)}) collective-permute-start(f32[24,8,256]{2,1,0:T(8,128)S(1)} %get-tuple-element.81), channel_id=1, source_target_pairs={{0,1},{2,3},{4,5},{6,7},{8,9},{10,11},{12,13},{14,15},{16,17},{18,... | collective-permute-start | bytes 589832 | tf_op jit(solution)/shard_map/ppermute | solution.py:408
  28.5 6.9 %collective-permute-start.5 = (f32[24,8,256]{2,1,0:T(8,128)S(1)}, f32[24,8,256]{2,1,0:T(8,128)S(1)}, u32[]{:S(2)}, u32[]{:S(2)}) collective-permute-start(f32[24,8,256]{2,1,0:T(8,128)S(1)} %get-tuple-element.82), channel_id=1, source_target_pairs={{1,2},{5,6},{9,10},{13,14},{17,18},{21,22},{25,26},{29,30},{2,1},{... | collective-permute-start | bytes 589832 | tf_op jit(solution)/shard_map/ppermute | solution.py:408
  30.4 11.3 %collective-permute-start.6 = (f32[4,64,256]{2,1,0:T(8,128)S(1)}, f32[4,64,256]{2,1,0:T(8,128)S(1)}, u32[]{:S(2)}, u32[]{:S(2)}) collective-permute-start(f32[4,64,256]{2,1,0:T(8,128)S(1)} %get-tuple-element.83), channel_id=1, source_target_pairs={{4,8},{5,9},{6,10},{7,11},{12,16},{13,17},{14,18},{15,19},{20,24},... | collective-permute-start | bytes 786440 | tf_op jit(solution)/shard_map/ppermute | solution.py:408
  35.3 6.4 %collective-permute-start.7 = (f32[4,64,256]{2,1,0:T(8,128)S(1)}, f32[4,64,256]{2,1,0:T(8,128)S(1)}, u32[]{:S(2)}, u32[]{:S(2)}) collective-permute-start(f32[4,64,256]{2,1,0:T(8,128)S(1)} %get-tuple-element.84), channel_id=1, source_target_pairs={{0,4},{1,5},{2,6},{3,7},{8,12},{9,13},{10,14},{11,15},{16,20},{17,... | collective-permute-start | bytes 786440 | tf_op jit(solution)/shard_map/ppermute | solution.py:408
  43.4 7.6 %collective-permute-start.8 = (f32[24,8,256]{2,1,0:T(8,128)S(1)}, f32[24,8,256]{2,1,0:T(8,128)S(1)}, u32[]{:S(2)}, u32[]{:S(2)}) collective-permute-start(f32[24,8,256]{2,1,0:T(8,128)S(1)} %get-tuple-element.94), channel_id=1, source_target_pairs={{0,1},{2,3},{4,5},{6,7},{8,9},{10,11},{12,13},{14,15},{16,17},{18,... | collective-permute-start | bytes 589832 | tf_op jit(solution)/shard_map/ppermute | solution.py:408
  43.7 7.3 %collective-permute-start.9 = (f32[24,8,256]{2,1,0:T(8,128)S(1)}, f32[24,8,256]{2,1,0:T(8,128)S(1)}, u32[]{:S(2)}, u32[]{:S(2)}) collective-permute-start(f32[24,8,256]{2,1,0:T(8,128)S(1)} %get-tuple-element.95), channel_id=1, source_target_pairs={{1,2},{5,6},{9,10},{13,14},{17,18},{21,22},{25,26},{29,30},{2,1},{... | collective-permute-start | bytes 589832 | tf_op jit(solution)/shard_map/ppermute | solution.py:408
  46.9 10.7 %collective-permute-start.10 = (f32[4,64,256]{2,1,0:T(8,128)S(1)}, f32[4,64,256]{2,1,0:T(8,128)S(1)}, u32[]{:S(2)}, u32[]{:S(2)}) collective-permute-start(f32[4,64,256]{2,1,0:T(8,128)S(1)} %get-tuple-element.96), channel_id=1, source_target_pairs={{4,8},{5,9},{6,10},{7,11},{12,16},{13,17},{14,18},{15,19},{20,24},... | collective-permute-start | bytes 786440 | tf_op jit(solution)/shard_map/ppermute | solution.py:408
  50.9 6.7 %collective-permute-start.11 = (f32[4,64,256]{2,1,0:T(8,128)S(1)}, f32[4,64,256]{2,1,0:T(8,128)S(1)}, u32[]{:S(2)}, u32[]{:S(2)}) collective-permute-start(f32[4,64,256]{2,1,0:T(8,128)S(1)} %get-tuple-element.97), channel_id=1, source_target_pairs={{0,4},{1,5},{2,6},{3,7},{8,12},{9,13},{10,14},{11,15},{16,20},{17,... | collective-permute-start | bytes 786440 | tf_op jit(solution)/shard_map/ppermute | solution.py:408
  59.3 6.8 %collective-permute-start.12 = (f32[24,8,256]{2,1,0:T(8,128)S(1)}, f32[24,8,256]{2,1,0:T(8,128)S(1)}, u32[]{:S(2)}, u32[]{:S(2)}) collective-permute-start(f32[24,8,256]{2,1,0:T(8,128)S(1)} %get-tuple-element.103), channel_id=1, source_target_pairs={{0,1},{2,3},{4,5},{6,7},{8,9},{10,11},{12,13},{14,15},{16,17},{18,... | collective-permute-start | bytes 589832 | tf_op jit(solution)/shard_map/ppermute | solution.py:408
  59.4 6.8 %collective-permute-start.13 = (f32[24,8,256]{2,1,0:T(8,128)S(1)}, f32[24,8,256]{2,1,0:T(8,128)S(1)}, u32[]{:S(2)}, u32[]{:S(2)}) collective-permute-start(f32[24,8,256]{2,1,0:T(8,128)S(1)} %get-tuple-element.104), channel_id=1, source_target_pairs={{1,2},{5,6},{9,10},{13,14},{17,18},{21,22},{25,26},{29,30},{2,1},{... | collective-permute-start | bytes 589832 | tf_op jit(solution)/shard_map/ppermute | solution.py:408
  61.6 11.0 %collective-permute-start.14 = (f32[4,64,256]{2,1,0:T(8,128)S(1)}, f32[4,64,256]{2,1,0:T(8,128)S(1)}, u32[]{:S(2)}, u32[]{:S(2)}) collective-permute-start(f32[4,64,256]{2,1,0:T(8,128)S(1)} %get-tuple-element.105), channel_id=1, source_target_pairs={{4,8},{5,9},{6,10},{7,11},{12,16},{13,17},{14,18},{15,19},{20,24},... | collective-permute-start | bytes 786440 | tf_op jit(solution)/shard_map/ppermute | solution.py:408
  66.1 6.4 %collective-permute-start.15 = (f32[4,64,256]{2,1,0:T(8,128)S(1)}, f32[4,64,256]{2,1,0:T(8,128)S(1)}, u32[]{:S(2)}, u32[]{:S(2)}) collective-permute-start(f32[4,64,256]{2,1,0:T(8,128)S(1)} %get-tuple-element.106), channel_id=1, source_target_pairs={{0,4},{1,5},{2,6},{3,7},{8,12},{9,13},{10,14},{11,15},{16,20},{17,... | collective-permute-start | bytes 786440 | tf_op jit(solution)/shard_map/ppermute | solution.py:408
  74.5 7.6 %collective-permute-start.21 = (f32[10,64,256]{2,1,0:T(8,128)S(1)}, f32[10,64,256]{2,1,0:T(8,128)S(1)}, u32[]{:S(2)}, u32[]{:S(2)}) collective-permute-start(f32[10,64,256]{2,1,0:T(8,128)S(1)} %get-tuple-element.114), channel_id=1, source_target_pairs={{0,32},{32,0},{64,96},{96,64},{1,33},{33,1},{65,97},{97,65},{2,34}... | collective-permute-start | bytes 1966088 | tf_op jit(solution)/shard_map/ppermute | solution.py:431
  82.7 16.0 %collective-permute-start.22 = (f32[10,64,256]{2,1,0:T(8,128)S(1)}, f32[10,64,256]{2,1,0:T(8,128)S(1)}, u32[]{:S(2)}, u32[]{:S(2)}) collective-permute-start(f32[10,64,256]{2,1,0:T(8,128)S(1)} %add_cores.5.a), channel_id=1, source_target_pairs={{0,64},{32,96},{64,0},{96,32},{1,65},{33,97},{65,1},{97,33},{2,66}... | collective-permute-start | bytes 1966088 | tf_op jit(solution)/shard_map/ppermute | solution.py:437
  82.8 2.0 %collective-permute-start.18 = (f32[6,64,256]{2,1,0:T(8,128)S(1)}, f32[6,64,256]{2,1,0:T(8,128)S(1)}, u32[]{:S(2)}, u32[]{:S(2)}) collective-permute-start(f32[6,64,256]{2,1,0:T(8,128)S(1)} %get-tuple-element.113), channel_id=1, source_target_pairs={{0,32},{32,0},{64,96},{96,64},{1,33},{33,1},{65,97},{97,65},{2,34}... | collective-permute-start | bytes 1179656 | tf_op jit(solution)/shard_map/ppermute | solution.py:431
  83.5 17.4 %collective-permute-start.16 = (f32[8,64,256]{2,1,0:T(8,128)S(1)}, f32[8,64,256]{2,1,0:T(8,128)S(1)}, u32[]{:S(2)}, u32[]{:S(2)}) collective-permute-start(f32[8,64,256]{2,1,0:T(8,128)S(1)} %get-tuple-element.112), channel_id=1, source_target_pairs={{0,32},{32,0},{64,96},{96,64},{1,33},{33,1},{65,97},{97,65},{2,34}... | collective-permute-start | bytes 1572872 | tf_op jit(solution)/shard_map/ppermute | solution.py:431
  85.5 21.7 %collective-permute-start.19 = (f32[6,64,256]{2,1,0:T(8,128)S(1)}, f32[6,64,256]{2,1,0:T(8,128)S(1)}, u32[]{:S(2)}, u32[]{:S(2)}) collective-permute-start(f32[6,64,256]{2,1,0:T(8,128)S(1)} %add_cores.4.a), channel_id=1, source_target_pairs={{0,64},{32,96},{64,0},{96,32},{1,65},{33,97},{65,1},{97,33},{2,66}... | collective-permute-start | bytes 1179656 | tf_op jit(solution)/shard_map/ppermute | solution.py:437
  98.8 12.2 %collective-permute-start.23 = (f32[10,64,256]{2,1,0:T(8,128)S(1)}, f32[10,64,256]{2,1,0:T(8,128)S(1)}, u32[]{:S(2)}, u32[]{:S(2)}) collective-permute-start(f32[10,64,256]{2,1,0:T(8,128)S(1)} %add_chips.4.refs_2_), channel_id=1, source_target_pairs={{0,32},{32,0},{64,96},{96,64},{1,33},{33,1},{65,97},{97,65},{2,34}... | collective-permute-start | bytes 1966088 | tf_op jit(solution)/shard_map/ppermute | solution.py:440
  101.5 16.9 %collective-permute-start.17 = (f32[8,64,256]{2,1,0:T(8,128)S(1)}, f32[8,64,256]{2,1,0:T(8,128)S(1)}, u32[]{:S(2)}, u32[]{:S(2)}) collective-permute-start(f32[8,64,256]{2,1,0:T(8,128)S(1)} %add_cores.3.a), channel_id=1, source_target_pairs={{0,64},{32,96},{64,0},{96,32},{1,65},{33,97},{65,1},{97,33},{2,66}... | collective-permute-start | bytes 1572872 | tf_op jit(solution)/shard_map/ppermute | solution.py:437
  107.2 3.8 %collective-permute-start.20 = (f32[6,64,256]{2,1,0:T(8,128)S(1)}, f32[6,64,256]{2,1,0:T(8,128)S(1)}, u32[]{:S(2)}, u32[]{:S(2)}) collective-permute-start(f32[6,64,256]{2,1,0:T(8,128)S(1)} %add_chips.3.refs_0_), channel_id=1, source_target_pairs={{0,32},{32,0},{64,96},{96,64},{1,33},{33,1},{65,97},{97,65},{2,34}... | collective-permute-start | bytes 1179656 | tf_op jit(solution)/shard_map/ppermute | solution.py:440
  118.4 2.8 %collective-permute-start.24 = (f32[8,64,256]{2,1,0:T(8,128)S(1)}, f32[8,64,256]{2,1,0:T(8,128)S(1)}, u32[]{:S(2)}, u32[]{:S(2)}) collective-permute-start(f32[8,64,256]{2,1,0:T(8,128)S(1)} %add_chips.5.refs_0_), channel_id=1, source_target_pairs={{0,32},{32,0},{64,96},{96,64},{1,33},{33,1},{65,97},{97,65},{2,34}... | collective-permute-start | bytes 1572872 | tf_op jit(solution)/shard_map/ppermute | solution.py:440
